TPU v7x, 32 devices: a whole 2x2x4 slice. The times are simulated.
32 devices in a mesh: groups: 2 (over x), hour: 16 (over z, y, core).
Axes of the slice: x: 2, y: 2, z: 4, core: 2. Of those that a mesh axis runs over, the one named last changes fastest.
Arguments:
- power: float32 [32, 16, 2048], P('groups', 'hour'), parts along dimension 0, may hold values from -3 to 3
- capacity: float32 [4096], P(('groups', 'hour')), parts along dimension 0, may hold values from 0.01 to 20
- flow_dual: float32 [32, 16, 4096], P('groups', 'hour'), parts along dimension 0, may hold values from -3 to 3
- upper_dual: float32 [32, 16, 2048], P('groups', 'hour'), parts along dimension 0, may hold values from 0 to 0.1
- lower_dual: float32 [32, 16, 2048], P('groups', 'hour'), parts along dimension 0, may hold values from 0 to 0.1
- price: float32 [32, 16], P('groups', 'hour'), parts along dimension 0, may hold values from -5 to 5
- load: bfloat16 [32, 16, 512], P('groups', 'hour'), parts along dimension 0, may hold values from -5 to 5
- shift_factors: bfloat16 [4096, 512], replicated, may hold values from -0.25 to 0.25
- line_limit: float32 [4096], replicated, may hold values from 0.5 to 3
- unit_bus: int32 [2048], replicated, may hold values from 0 to 511
- leakage: float32 [2048], replicated, may hold values from 0.015625 to 0.0625
- initial_state: float32 [4096], P('groups'), parts along dimension 0, may hold values from 0 to 10
- power_limit: float32 [2048], replicated, may hold values from 0.5 to 1.5
- capacity_cost: float32 [2048], replicated, may hold values from 0 to 0.1
Outputs:
- new_power: float32 [32, 16, 2048], P('groups', 'hour'), parts along dimension 0
- new_capacity: float32 [4096], P(('groups', 'hour')), parts along dimension 0
- new_flow_dual: float32 [32, 16, 4096], P('groups', 'hour'), parts along dimension 0
- new_upper_dual: float32 [32, 16, 2048], P('groups', 'hour'), parts along dimension 0
- new_lower_dual: float32 [32, 16, 2048], P('groups', 'hour'), parts along dimension 0
There are 2 independent parts, one for each index of `groups`. A program takes and returns all parts, laid end to end along the dimension named above; an argument that names none is the same for every part. Nothing has to cross between parts.
All inputs are finite; a program needn't handle non-finite values.
Results may differ from a plain program's by a relative error of at most 0.00093.
Values sent between devices are 32-bit elements; how exact they have to be, the bound alone decides.
No kernel may reach another device: no remote copies, remote signals or barrier semaphores. Data moves between devices by JAX's collectives and lax.ppermute only.
A program may use at most 128 MiB of HBM per device.

v0:
```python
import functools

import jax
import jax.numpy as jnp
from jax import lax
from jax.experimental import pallas as pl
from jax.experimental.pallas import tpu as pltpu
from jax.sharding import PartitionSpec as P

ITERS = 4


primal_step = 0.05
dual_step = 0.01
LANES = 128
SUBLANES = 8
CHUNKS = 4


def compose(earlier, later):
    return (earlier[0] * later[0], later[0] * earlier[1] + later[1])


def chain_scan(factor, values, reverse):
    factors = jnp.broadcast_to(factor, values.shape)
    return lax.associative_scan(compose, (factors, values), reverse=reverse, axis=1)[1]


def grid_gradient(flow_dual, shift_factors, incidence):
    scen, hours, lines = flow_dual.shape
    bus_dual = jnp.dot(
        flow_dual.astype(jnp.bfloat16).reshape(-1, lines),
        shift_factors,
        preferred_element_type=jnp.float32,
    ).astype(jnp.bfloat16)
    grid_grad = jnp.dot(bus_dual, incidence.T, preferred_element_type=jnp.float32)
    return grid_grad.reshape(scen, hours, incidence.shape[0])


def flow_update(flow_dual, power_bar, load, shift_factors, incidence, line_limit):
    scen, hours, lines = flow_dual.shape
    injection = jnp.dot(
        power_bar.astype(jnp.bfloat16).reshape(-1, incidence.shape[0]),
        incidence,
        preferred_element_type=jnp.float32,
    )
    injection = (injection - load.astype(jnp.float32).reshape(-1, incidence.shape[1])).astype(
        jnp.bfloat16
    )
    flows = jnp.dot(injection, shift_factors.T, preferred_element_type=jnp.float32).reshape(
        scen, hours, lines
    )
    probe = flow_dual + dual_step * flows
    return probe - dual_step * jnp.clip(probe / dual_step, -line_limit, line_limit)


def by_units(
    power,
    capacity,
    flow_dual,
    upper_dual,
    lower_dual,
    price,
    load,
    shift_factors,
    line_limit,
    unit_bus,
    leakage,
    initial_state,
    power_limit,
    capacity_cost,
):
    retain = 1.0 - leakage
    buses = shift_factors.shape[1]
    incidence = (unit_bus[:, None] == jnp.arange(buses, dtype=jnp.int32)[None, :]).astype(
        jnp.bfloat16
    )
    scen, hdev, units = power.shape
    unit_dev = capacity.shape[0]
    ndev = lax.axis_size("hour")
    position = lax.axis_index("hour")
    hours_total = hdev * ndev

    def own(vector):
        return lax.dynamic_slice_in_dim(vector, position * unit_dev, unit_dev)

    upper_units, lower_units = (
        lax.all_to_all(upper_dual, "hour", split_axis=2, concat_axis=1, tiled=True),
        lax.all_to_all(lower_dual, "hour", split_axis=2, concat_axis=1, tiled=True),
    )
    retain_own = own(retain)
    start_own = own(initial_state)
    cost_own = own(capacity_cost)
    for step in range(ITERS):
        grid_grad = grid_gradient(flow_dual, shift_factors, incidence)
        adjoint_units = -chain_scan(retain_own, upper_units - lower_units, True)
        state_grad = lax.all_to_all(adjoint_units, "hour", split_axis=1, concat_axis=2, tiled=True)
        trial_power = jnp.clip(
            power - primal_step * (grid_grad + state_grad - price[:, :, None]),
            -power_limit,
            power_limit,
        )
        dual_total = jnp.sum(upper_units, axis=(0, 1))
        trial_capacity = jnp.maximum(
            capacity - primal_step * (hours_total * cost_own - dual_total / scen), 0.0
        )
        power_bar = 2.0 * trial_power - power
        capacity_bar = 2.0 * trial_capacity - capacity
        flow_dual = flow_update(flow_dual, power_bar, load, shift_factors, incidence, line_limit)
        bar_units = lax.all_to_all(power_bar, "hour", split_axis=2, concat_axis=1, tiled=True)
        driven = -bar_units
        driven = driven.at[:, 0, :].add(retain_own * start_own)
        state_bar = chain_scan(retain_own, driven, False)
        upper_units = jnp.maximum(upper_units + dual_step * (state_bar - capacity_bar), 0.0)
        lower_units = jnp.maximum(lower_units - dual_step * state_bar, 0.0)
        power = trial_power
        capacity = trial_capacity
    upper_dual, lower_dual = (
        lax.all_to_all(upper_units, "hour", split_axis=1, concat_axis=2, tiled=True),
        lax.all_to_all(lower_units, "hour", split_axis=1, concat_axis=2, tiled=True),
    )
    return (power, capacity, flow_dual, upper_dual, lower_dual)


def by_scenarios(
    power,
    capacity,
    flow_dual,
    upper_dual,
    lower_dual,
    price,
    load,
    shift_factors,
    line_limit,
    unit_bus,
    leakage,
    initial_state,
    power_limit,
    capacity_cost,
):
    ndev = lax.axis_size("hour")
    position = lax.axis_index("hour")
    scen = hours = ndev
    units = power.shape[2]
    lines, buses = shift_factors.shape
    ut, lt, bt = units // LANES, lines // LANES, buses // LANES
    chunk = lines // CHUNKS
    small = -(-(bt + 2) // SUBLANES) * SUBLANES
    at_power, at_upper, at_lower, at_flow = 0, ut, 2 * ut, 3 * ut
    at_total = at_flow + lt
    at_load = at_total + ut
    at_price, at_capacity = at_load + bt, at_load + bt + 1
    rows_in = at_load + small
    back_total, back_flow = 3 * ut, 4 * ut
    rows_back = back_flow + lt
    f32, bf16 = jnp.float32, jnp.bfloat16
    state = (hours * ut, LANES)

    def call(body, outs, scratch, copies, *args, near=0, flops=0):
        moved = sum(a.size * a.dtype.itemsize for a in args)
        far = pl.BlockSpec(memory_space=pltpu.HBM)
        return pl.pallas_call(
            body,
            out_shape=[pltpu.HBM(s, f32) for s in outs],
            in_specs=[pl.BlockSpec(memory_space=pltpu.VMEM)] * near + [far] * (len(args) - near),
            out_specs=[far] * len(outs),
            scratch_shapes=[pltpu.VMEM(*s) for s in scratch] + [pltpu.SemaphoreType.DMA((copies,))],
            compiler_params=pltpu.CompilerParams(vmem_limit_bytes=24 * 1024 * 1024),
            cost_estimate=pl.CostEstimate(flops=flops, bytes_accessed=moved, transcendentals=0),
        )(*args[:near], *(pltpu.with_memory_space_constraint(a, pltpu.HBM) for a in args[near:]))

    class Copies:
        def __init__(self, semaphores):
            self.semaphores, self.count, self.sent = semaphores, 0, []

        def bring(self, source, target):
            copy = pltpu.make_async_copy(source, target, self.semaphores.at[self.count])
            self.count += 1
            copy.start()
            return copy

        def send(self, source, target):
            self.sent.append(self.bring(source, target))

        def close(self):
            for copy in self.sent:
                copy.wait()

    def exchange(blocks):
        return lax.all_to_all(blocks, "hour", split_axis=0, concat_axis=0, tiled=True)

    def rows(ref, first, step):
        return ref[pl.ds(first, ref.shape[0] // step, stride=step), :]

    def wide(ref, first, count, step):
        return jnp.concatenate([rows(ref, first + j, step) for j in range(count)], axis=1)

    def spread(ref, first, step, value):
        for j in range(value.shape[1] // LANES):
            ref[pl.ds(first + j, value.shape[0], stride=step), :] = value[
                :, j * LANES : (j + 1) * LANES
            ]

    def part(ref, index):
        return ref[pl.ds(index * ut, ut), :]

    def bring_chunks(copies, shift, shift_v):
        return [
            copies.bring(shift.at[pl.ds(c * chunk, chunk)], shift_v.at[pl.ds(c * chunk, chunk)])
            for c in range(CHUNKS)
        ]

    def to_units(bus_dual, incidence, grid):
        grid_grad = lax.dot_general(
            bus_dual.astype(bf16), incidence[...], (((1,), (1,)), ((), ())),
            preferred_element_type=f32,
        )
        spread(grid, 0, ut, grid_grad)

    def inject(bar, load, incidence):
        wide_bar = wide(bar, 0, ut, ut).astype(bf16)
        total = jnp.dot(wide_bar, incidence[...], preferred_element_type=f32)
        return (total - load[...]).astype(bf16)

    def advance(flow, injection, shift, limit, c):
        at = pl.ds(c * chunk, chunk)
        flows = lax.dot_general(
            injection, shift[at, :], (((1,), (1,)), ((), ())), preferred_element_type=f32
        )
        probe = flow[:, at] + dual_step * flows
        bound = dual_step * limit[:, at]
        return probe - jnp.clip(probe, -bound, bound)

    def to_buses(flow, shift, c):
        return jnp.dot(
            flow.astype(bf16), shift[pl.ds(c * chunk, chunk), :], preferred_element_type=f32
        )

    def network(bar, load, flow, shift, limit, incidence, grid, arrived):
        injection = inject(bar, load, incidence)
        for c in range(CHUNKS):
            arrived(c)
            flow[:, pl.ds(c * chunk, chunk)] = advance(flow, injection, shift, limit, c)
        to_units(
            jnp.dot(flow[...].astype(bf16), shift[...], preferred_element_type=f32), incidence, grid
        )

    def local(upper, lower, before, grid, price, settings, put_power, bar, put):
        keep, bound = part(settings, 0), part(settings, 2)
        carry = jnp.zeros((ut, LANES), f32)
        for hour in reversed(range(hours)):
            carry = keep * carry + (upper(hour) - lower(hour))
            old = before(hour)
            gradient = part(grid, hour) - carry - price(hour)
            trial = jnp.clip(old - primal_step * gradient, -bound, bound)
            put_power(hour, trial)
            bar[pl.ds(hour * ut, ut), :] = 2.0 * trial - old
        level = part(settings, 1)
        for hour in range(hours):
            level = keep * level - part(bar, hour)
            put(
                hour,
                upper(hour) + dual_step * level,
                jnp.maximum(lower(hour) - dual_step * level, 0.0),
            )

    def capacities(capacity, settings, total):
        cost = part(settings, 3)
        trial = jnp.maximum(capacity - primal_step * (hours * cost - total / scen), 0.0)
        return trial, dual_step * (2.0 * trial - capacity)

    def sum_blocks(ref, first, step):
        return sum(ref[pl.ds(hour * step + first, ut), :] for hour in range(hours))

    def reader(ref):
        return lambda hour: part(ref, hour)

    def writer(ref):
        def put(hour, value):
            ref[pl.ds(hour * ut, ut), :] = value

        return put


    def pack(power, upper, lower, flow, load, price, capacity, out, *scratch):
        load_v, price_v, capacity_v, blocks_v, semaphores = scratch
        copies = Copies(semaphores)
        blocks = blocks_v.reshape(ndev, rows_in, LANES)
        places = [
            blocks.at[:, pl.ds(at, source.shape[1])]
            for source, at in (
                (upper, at_upper), (flow, at_flow), (power, at_power), (lower, at_lower),
            )
        ]
        big = [copies.bring(*pair) for pair in zip((upper, flow, power, lower), places)]
        come = [
            copies.bring(load, load_v),
            copies.bring(price, price_v),
            copies.bring(capacity, capacity_v),
        ]
        for peer in range(ndev):
            blocks_v[pl.ds(peer * rows_in + at_load, small), :] = jnp.zeros((small, LANES), f32)
        for copy in come:
            copy.wait()
        spread(blocks_v, at_load, rows_in, load_v[...].astype(f32))
        across = lax.broadcasted_iota(jnp.int32, (ndev, ndev), 0)
        along = lax.broadcasted_iota(jnp.int32, (ndev, ndev), 1)
        own_price = jnp.sum(
            jnp.where(across == along, jnp.broadcast_to(price_v[...], (ndev, ndev)), 0.0),
            axis=1, keepdims=True,
        )
        spread(blocks_v, at_price, rows_in, jnp.broadcast_to(own_price, (ndev, LANES)))
        spread(blocks_v, at_capacity, rows_in, jnp.broadcast_to(capacity_v[...], (ndev, LANES)))
        big[0].wait()
        total = sum_blocks(blocks_v, at_upper, rows_in)
        for peer in range(ndev):
            blocks_v[pl.ds(peer * rows_in + at_total, ut), :] = total
        for copy in big[1:]:
            copy.wait()
        copies.send(blocks, out)
        copies.close()

    def first(came, incidence, shift, settings, *rest):
        power_o, upper_o, lower_o, bar_o, flow_o, load_o, notes_o, total_o = rest[:8]
        shift_v, settings_v, power, upper, lower, bar, flow, load, notes, out, grid = rest[8:-1]
        copies = Copies(rest[-1])
        chunks = bring_chunks(copies, shift, shift_v)
        come = [copies.bring(settings, settings_v)]
        flow[...] = wide(came, at_flow, lt, rows_in)
        load[...] = wide(came, at_load, bt, rows_in)
        notes[pl.ds(ut, hours), :] = rows(came, at_price, rows_in)
        copies.send(flow, flow_o)
        copies.send(load, load_o)
        come[0].wait()
        capacity, pull = capacities(
            rows(came, at_capacity, rows_in), settings_v, sum_blocks(came, at_total, rows_in)
        )
        notes[pl.ds(0, ut), :] = capacity
        copies.send(notes, notes_o)
        bus_dual = jnp.zeros((hours, buses), f32)
        for c in range(CHUNKS):
            chunks[c].wait()
            bus_dual = bus_dual + to_buses(flow[:, pl.ds(c * chunk, chunk)], shift_v, c)
        to_units(bus_dual, incidence, grid)
        total = [jnp.zeros((ut, LANES), f32)]

        def put(hour, lifted, low):
            new = jnp.maximum(lifted - pull, 0.0)
            upper[pl.ds(hour * ut, ut), :] = new
            lower[pl.ds(hour * ut, ut), :] = low
            total[0] = total[0] + new

        def received(first_row, count=ut):
            return lambda hour: came[pl.ds(hour * rows_in + first_row, count), :]

        local(
            received(at_upper), received(at_lower), received(at_power), grid,
            received(at_price, 1), settings_v, writer(power), bar, put,
        )
        for peer in range(ndev):
            out[pl.ds(peer * ut, ut), :] = total[0]
        copies.send(out, total_o)
        copies.send(power, power_o)
        copies.send(bar, bar_o)
        copies.send(upper, upper_o)
        copies.send(lower, lower_o)
        copies.close()

    def middle(ahead, *refs):
        given, outs, scratch = refs[:11], refs[11:16], refs[16:-1]
        copies = Copies(refs[-1])
        held = dict(zip(names, scratch))
        incidence, shift, *others = given
        come = {}
        for name, source in zip(names, others):
            come[name] = copies.bring(source, held[name])
            if name == "flow":
                chunks = bring_chunks(copies, shift, scratch[-6])
        shift_v, grid, power_v, bar_v, lifted, low = scratch[-6:]
        for name in ("bar", "load", "flow", "line"):
            come.pop(name).wait()
        net = (held["load"], held["flow"], shift_v, held["line"], incidence, grid)
        network(held["bar"], *net, lambda c: chunks[c].wait())
        if not ahead:
            copies.send(held["flow"], outs[0])
        for copy in come.values():
            copy.wait()

        def put(hour, lift, new_low):
            lifted[pl.ds(hour * ut, ut), :] = lift
            low[pl.ds(hour * ut, ut), :] = new_low

        local(
            reader(held["upper"]), reader(held["lower"]), reader(held["power"]), grid,
            lambda hour: held["notes"][pl.ds(ut + hour, 1), :], held["settings"],
            writer(power_v), bar_v, put,
        )
        for value, out in zip((power_v, lifted, low), outs[1:]):
            copies.send(value, out)
        if ahead:
            network(bar_v, *net, lambda c: None)
            copies.send(held["flow"], outs[0])
            copies.send(grid, outs[4])
        else:
            copies.send(bar_v, outs[4])
        copies.close()

    names = (
        "bar", "load", "flow", "line", "upper", "lower", "power", "notes", "settings",
    )

    def update(came, lifted, notes, settings, *rest):
        upper_o, notes_o, total_o, lifted_v, notes_v, settings_v, upper, out, semaphores = rest
        copies = Copies(semaphores)
        come = [
            copies.bring(notes, notes_v),
            copies.bring(settings, settings_v),
            copies.bring(lifted, lifted_v),
        ]
        total = sum_blocks(came, 0, ut)
        come[0].wait()
        come[1].wait()
        capacity, pull = capacities(part(notes_v, 0), settings_v, total)
        notes_v[pl.ds(0, ut), :] = capacity
        copies.send(notes_v, notes_o)
        come[2].wait()
        total = jnp.zeros((ut, LANES), f32)
        for hour in range(hours):
            new = jnp.maximum(part(lifted_v, hour) - pull, 0.0)
            upper[pl.ds(hour * ut, ut), :] = new
            total = total + new
        for peer in range(ndev):
            out[pl.ds(peer * ut, ut), :] = total
        copies.send(out, total_o)
        copies.send(upper, upper_o)
        copies.close()

    def last(came, incidence, *refs):
        outs, scratch, copies = refs[10:12], refs[12:-1], Copies(refs[-1])
        held = dict(zip(final_names, scratch))
        shift_v, out, upper, bar = scratch[-4:]
        come = {
            name: copies.bring(source, held[name]) for name, source in zip(final_names, refs)
        }
        chunks = bring_chunks(copies, refs[9], shift_v)
        total = sum_blocks(came, 0, ut)
        for name in ("notes", "settings", "lifted"):
            come.pop(name).wait()
        notes, settings = held["notes"], held["settings"]
        capacity, pull = capacities(part(notes, 0), settings, total)
        notes[pl.ds(0, ut), :] = capacity
        copies.send(notes, outs[1])
        total = jnp.zeros((ut, LANES), f32)
        for hour in range(hours):
            new = jnp.maximum(part(held["lifted"], hour) - pull, 0.0)
            upper[pl.ds(hour * ut, ut), :] = new
            total = total + new
        for peer in range(ndev):
            out[pl.ds(peer * rows_back + back_total, ut), :] = total
        for name in ("lower", "power", "grid"):
            come.pop(name).wait()

        def put_power(hour, value):
            out[pl.ds(hour * rows_back, ut), :] = value

        def put(hour, lift, low):
            out[pl.ds(hour * rows_back + ut, ut), :] = lift
            out[pl.ds(hour * rows_back + 2 * ut, ut), :] = low

        local(
            reader(upper), reader(held["lower"]), reader(held["power"]), held["grid"],
            lambda hour: notes[pl.ds(ut + hour, 1), :], settings, put_power, bar, put,
        )
        blocks = out.reshape(ndev, rows_back, LANES)
        copies.send(blocks.at[:, pl.ds(0, back_flow)], outs[0].at[:, pl.ds(0, back_flow)])
        for copy in come.values():
            copy.wait()
        injection = inject(bar, held["load"], incidence)
        tiles_of = chunk // LANES
        for c in range(CHUNKS):
            chunks[c].wait()
            new = advance(held["flow"], injection, shift_v, held["line"], c)
            spread(out, back_flow + c * tiles_of, rows_back, new)
        at = pl.ds(back_flow, lt)
        copies.send(blocks.at[:, at], outs[0].at[:, at])
        copies.close()

    final_names = (
        "notes", "settings", "lifted", "lower", "power", "grid", "load", "flow", "line",
    )

    def finish(came, notes, settings, power_o, upper_o, lower_o, flow_o, capacity_o, *rest):
        notes_v, settings_v, upper, own, semaphores = rest
        copies = Copies(semaphores)
        come = [copies.bring(notes, notes_v), copies.bring(settings, settings_v)]
        blocks = came.reshape(ndev, rows_back, LANES)
        copies.send(blocks.at[:, pl.ds(0, ut)], power_o)
        copies.send(blocks.at[:, pl.ds(2 * ut, ut)], lower_o)
        copies.send(blocks.at[:, pl.ds(back_flow, lt)], flow_o)
        total = sum_blocks(came, back_total, rows_back)
        for copy in come:
            copy.wait()
        capacity, pull = capacities(part(notes_v, 0), settings_v, total)
        notes_v[pl.ds(0, ut), :] = capacity
        own[...] = notes_v[pl.ds(lax.axis_index("hour"), 1), :]
        copies.send(own, capacity_o)
        for peer in range(ndev):
            upper[peer] = jnp.maximum(came[pl.ds(peer * rows_back + ut, ut), :] - pull, 0.0)
        copies.send(upper, upper_o)
        copies.close()


    def tiles(vector):
        return vector.reshape(-1, LANES)

    settings = jnp.concatenate(
        [tiles(v) for v in (1.0 - leakage, initial_state, power_limit, capacity_cost)]
    )
    line = line_limit.reshape(1, lines)
    incidence = (unit_bus[:, None] == jnp.arange(buses, dtype=jnp.int32)[None, :]).astype(bf16)
    shift = shift_factors

    state_v, wide_v, load_v = (state, f32), ((hours, lines), f32), ((hours, buses), f32)
    notes, notes_v = (ut + hours, LANES), ((ut + hours, LANES), f32)
    settings_v, line_v = ((4 * ut, LANES), f32), ((1, lines), f32)
    shift_v = ((lines, buses), bf16)
    flops = 4 * hours * buses * (lines + units)

    (sent,) = call(
        pack,
        [(ndev, rows_in, LANES)],
        [
            ((scen, buses), bf16), ((1, scen), f32), ((1, LANES), f32),
            ((ndev * rows_in, LANES), f32),
        ],
        8,
        power.reshape(scen, ut, LANES),
        upper_dual.reshape(scen, ut, LANES),
        lower_dual.reshape(scen, ut, LANES),
        flow_dual.reshape(scen, lt, LANES),
        load.reshape(scen, buses),
        price.reshape(1, scen),
        capacity.reshape(1, LANES),
    )
    came = exchange(sent).reshape(-1, LANES)
    power, upper, lower, bar, flow, load, note, total = call(
        first,
        [state] * 4 + [(hours, lines), (hours, buses), notes, state],
        [shift_v, settings_v] + [state_v] * 4 + [wide_v, load_v, notes_v, state_v, state_v],
        CHUNKS + 9,
        came, incidence, shift, settings,
        near=2, flops=flops,
    )
    for iteration in range(1, ITERS - 1):
        ahead = iteration == ITERS - 2
        came = exchange(total.reshape(ndev, ut, LANES)).reshape(-1, LANES)
        flow, power, lifted, lower, more = call(
            functools.partial(middle, ahead),
            [(hours, lines)] + [state] * 4,
            [state_v, load_v, wide_v, line_v, state_v, state_v, state_v, notes_v]
            + [settings_v, shift_v] + [state_v] * 5,
            CHUNKS + 14,
            incidence, shift, bar, load, flow, line, upper, lower, power, note, settings,
            near=1, flops=flops * (1 + ahead),
        )
        if not ahead:
            bar = more
            upper, note, total = call(
                update,
                [state, notes, state],
                [state_v, notes_v, settings_v, state_v, state_v],
                6,
                came, lifted, note, settings,
                near=1,
            )
    sent, note = call(
        last,
        [(ndev, rows_back, LANES), notes],
        [notes_v, settings_v] + [state_v] * 4 + [load_v, wide_v, line_v, shift_v]
        + [((ndev * rows_back, LANES), f32), state_v, state_v],
        CHUNKS + 12,
        came, incidence, note, settings, lifted, lower, power, more, load, flow, line, shift,
        near=2, flops=flops,
    )
    came = exchange(sent).reshape(-1, LANES)
    hourly = (scen, ut, LANES)
    power, upper, lower, flow, capacity = call(
        finish,
        [hourly, hourly, hourly, (scen, lt, LANES), (1, LANES)],
        [notes_v, settings_v, (hourly, f32), ((1, LANES), f32)],
        7,
        came, note, settings,
        near=1,
    )
    return (
        power.reshape(scen, 1, units),
        capacity.reshape(LANES),
        flow.reshape(scen, 1, lines),
        upper.reshape(scen, 1, units),
        lower.reshape(scen, 1, units),
    )


def on_device(power, capacity, flow_dual, *rest):
    ndev = lax.axis_size("hour")
    buses = rest[4].shape[1]
    fits = (
        power.shape[0] == ndev
        and power.shape[1] == 1
        and capacity.shape[0] == LANES
        and flow_dual.shape[2] % (CHUNKS * LANES) == 0
        and ndev % (2 * SUBLANES) == 0
        and all(size % (SUBLANES * LANES) == 0 for size in (power.shape[2], flow_dual.shape[2]))
        and buses % LANES == 0
    )
    plan = by_scenarios if fits else by_units
    return plan(power, capacity, flow_dual, *rest)


def solution(mesh):
    return jax.shard_map(
        on_device,
        mesh=mesh,
        in_specs=(
            P("groups", "hour", None),
            P(("groups", "hour")),
            P("groups", "hour", None),
            P("groups", "hour", None),
            P("groups", "hour", None),
            P("groups", "hour"),
            P("groups", "hour", None),
            P(),
            P(),
            P(),
            P(),
            P("groups"),
            P(),
            P(),
        ),
        out_specs=(
            P("groups", "hour", None),
            P(("groups", "hour")),
            P("groups", "hour", None),
            P("groups", "hour", None),
            P("groups", "hour", None),
        ),
        check_vma=False,
    )
```

profile of v0, /device:TPU:0, one launch (start us, length us, event | category | flops | bytes accessed | tf_op | source)
XLA Modules:
  0.0 95.1 jit_solution(5703463097438350968)
XLA Ops:
  0.6 2.1 %shard_map.173 = f32[16,104,128]{2,1,0:T(8,128)} custom-call(f32[16,16,128]{2,1,0:T(8,128)} %bitcast.34, f32[16,16,128]{2,1,0:T(8,128)} %bitcast.35, f32[16,16,128]{2,1,0:T(8,128)} %bitcast.36, f32[16,32,128]{2,1,0:T(8,128)} %bitcast.28, bf16[16,512]{1,0:T(8,128)(2,1)} %bitcast.37, f32[1,16]{1,0:T(1,128)} %bitcast.41, f32[1,128]{1,0:T(1,128)} %bitcast.42), custom_call_target="tpu_custom_call" | custom-call | bytes 672320 | tf_op jit(solution)/shard_map/pallas_call | solution.py:162
  2.8 7.4 %all-to-all-start = ((f32[16,104,128]{2,1,0:T(8,128)}), f32[16,104,128]{2,1,0:T(8,128)S(1)}, u32[]{:S(2)}, u32[]{:S(2)}) async-start(f32[16,104,128]{2,1,0:T(8,128)} %shard_map.173), calls=%async_computation | async-start | bytes 1703936 | tf_op jit(solution)/shard_map/all_to_all | solution.py:190
  10.2 0.7 subtract_bitcast_fusion
  10.9 1.3 %pad_maximum_fusion.settings.refs_10_.refs_1_ = f32[64,128]{1,0:T(8,128)} fusion(f32[16,128]{1,0:T(8,128)} %bitcast.38, f32[16,128]{1,0:T(8,128)} %bitcast.39, f32[16,128]{1,0:T(8,128)} %bitcast.40, f32[16,128]{1,0:T(8,128)S(1)} %subtract_bitcast_fusion), kind=kLoop, calls=%fused_computation.2 | loop fusion | flops 24576 | bytes 65536 | tf_op jit(solution)/shard_map/concatenate | solution.py:516
  12.2 1.2 %fusion.incidence.refs_0_ = bf16[2048,512]{1,0:T(8,128)(2,1)S(1)} fusion(s32[2048]{0:T(1024)} %param.23), kind=kLoop, calls=%fused_computation.1 | loop fusion | flops 2097152 | bytes 2105344 | tf_op jit(solution)/shard_map/convert_element_type | solution.py:520
  13.4 16.5 %all-to-all-done = f32[16,104,128]{2,1,0:T(8,128)S(1)} async-done(((f32[16,104,128]{2,1,0:T(8,128)}), f32[16,104,128]{2,1,0:T(8,128)S(1)}, u32[]{:S(2)}, u32[]{:S(2)}) %all-to-all-start) | async-done | bytes 852000 | tf_op jit(solution)/shard_map/all_to_all | solution.py:190
  29.9 4.5 %shard_map.174 = (f32[256,128]{1,0:T(8,128)}, f32[256,128]{1,0:T(8,128)}, f32[256,128]{1,0:T(8,128)}, f32[256,128]{1,0:T(8,128)}, f32[16,4096]{1,0:T(8,128)}, /*...) custom-call(f32[1664,128]{1,0:T(8,128)S(1)} %bitcast.24, bf16[2048,512]{1,0:T(8,128)(2,1)S(1)} %fusion.incidence.refs_0_, ...), custom_call_target="tpu_custom_call" | custom-call | flops 201326592 | bytes 7176192 | tf_op jit(solution)/shard_map/pallas_call | solution.py:162
  34.4 5.8 %all-to-all-start.1 = ((f32[16,16,128]{2,1,0:T(8,128)}), f32[16,16,128]{2,1,0:T(8,128)S(1)}, u32[]{:S(2)}, u32[]{:S(2)}) async-start(f32[16,16,128]{2,1,0:T(8,128)} %bitcast.33), calls=%async_computation.1 | async-start | bytes 262144 | tf_op jit(solution)/shard_map/all_to_all | solution.py:190
  40.3 6.3 %shard_map.175 = (f32[16,4096]{1,0:T(8,128)}, f32[256,128]{1,0:T(8,128)}, f32[256,128]{1,0:T(8,128)}, f32[256,128]{1,0:T(8,128)}, f32[256,128]{1,0:T(8,128)}) custom-call(bf16[2048,512]{1,0:T(8,128)(2,1)S(1)} %fusion.incidence.refs_0_, bf16[4096,512]{1,0:T(8,128)(2,1)} %refs_9_.1, f32[256,128]{1,0:T(8,128)} %get-tuple-element.34.refs_2_, ...), custom_call_target="tpu_custom_call" | custom-call | flops 201326592 | bytes 7176192 | tf_op jit(solution)/shard_map/pallas_call | solution.py:162
  46.5 1.7 %all-to-all-done.1 = f32[16,16,128]{2,1,0:T(8,128)S(1)} async-done(((f32[16,16,128]{2,1,0:T(8,128)}), f32[16,16,128]{2,1,0:T(8,128)S(1)}, u32[]{:S(2)}, u32[]{:S(2)}) %all-to-all-start.1) | async-done | bytes 131104 | tf_op jit(solution)/shard_map/all_to_all | solution.py:190
  48.2 1.7 %shard_map.176 = (f32[256,128]{1,0:T(8,128)}, f32[32,128]{1,0:T(8,128)}, f32[256,128]{1,0:T(8,128)}) custom-call(f32[256,128]{1,0:T(8,128)S(1)} %bitcast.27, f32[256,128]{1,0:T(8,128)} %get-tuple-element.41.lifted, f32[32,128]{1,0:T(8,128)} %get-tuple-element.40.refs_9_.notes, f32[64,128]{1,0:T(8,128)} %pad_maximum_fusion.settings.refs_10_.refs_1_), custom_call_target="tpu_custom_call" | custom-call | bytes 311296 | tf_op jit(solution)/shard_map/pallas_call | solution.py:162
  49.9 4.4 %all-to-all-start.2 = ((f32[16,16,128]{2,1,0:T(8,128)}), f32[16,16,128]{2,1,0:T(8,128)S(1)}, u32[]{:S(2)}, u32[]{:S(2)}) async-start(f32[16,16,128]{2,1,0:T(8,128)} %bitcast.32), calls=%async_computation.2 | async-start | bytes 262144 | tf_op jit(solution)/shard_map/all_to_all | solution.py:190
  54.3 8.7 %shard_map.177 = (f32[16,4096]{1,0:T(8,128)}, f32[256,128]{1,0:T(8,128)}, f32[256,128]{1,0:T(8,128)}, f32[256,128]{1,0:T(8,128)}, f32[256,128]{1,0:T(8,128)}) custom-call(bf16[2048,512]{1,0:T(8,128)(2,1)S(1)} %fusion.incidence.refs_0_, bf16[4096,512]{1,0:T(8,128)(2,1)} %refs_9_.1, f32[256,128]{1,0:T(8,128)} %get-tuple-element.44.refs_2_, ...), custom_call_target="tpu_custom_call" | custom-call | flops 402653184 | bytes 7176192 | tf_op jit(solution)/shard_map/pallas_call | solution.py:162
  63.0 0.0 all-to-all-done.2
  63.0 4.2 %shard_map.178 = (f32[16,96,128]{2,1,0:T(8,128)}, f32[32,128]{1,0:T(8,128)}) custom-call(f32[256,128]{1,0:T(8,128)S(1)} %bitcast.26, bf16[2048,512]{1,0:T(8,128)(2,1)S(1)} %fusion.incidence.refs_0_, f32[32,128]{1,0:T(8,128)} %get-tuple-element.43.refs_9_.refs_0_, f32[64,128]{1,0:T(8,128)} %pad_maximum_fusion.settings.refs_10_.refs_1_, ...), custom_call_target="tpu_custom_call" | custom-call | flops 201326592 | bytes 7307264 | tf_op jit(solution)/shard_map/pallas_call | solution.py:162
  67.2 26.3 %all_to_all.20 = f32[16,96,128]{2,1,0:T(8,128)S(1)} all-to-all(f32[16,96,128]{2,1,0:T(8,128)} %get-tuple-element.54), channel_id=1, replica_groups=mesh['groups'=2,'hour'=16] {'hour'}, dimensions={0} | all-to-all | bytes 1572864 | tf_op jit(solution)/shard_map/all_to_all | solution.py:190
  93.5 1.5 %shard_map.179 = (f32[16,16,128]{2,1,0:T(8,128)}, f32[16,16,128]{2,1,0:T(8,128)}, f32[16,16,128]{2,1,0:T(8,128)}, f32[16,32,128]{2,1,0:T(8,128)}, f32[1,128]{1,0:T(1,128)}) custom-call(f32[1536,128]{1,0:T(8,128)S(1)} %bitcast.25, f32[32,128]{1,0:T(8,128)} %get-tuple-element.55.notes, f32[64,128]{1,0:T(8,128)} %pad_maximum_fusion.settings.refs_10_.refs_1_), custom_call_target="tpu_custom_call" | custom-call | bytes 835584 | tf_op jit(solution)/shard_map/pallas_call | solution.py:162
Async XLA Ops:
  2.8 27.2 %all-to-all-start = ((f32[16,104,128]{2,1,0:T(8,128)}), f32[16,104,128]{2,1,0:T(8,128)S(1)}, u32[]{:S(2)}, u32[]{:S(2)}) async-start(f32[16,104,128]{2,1,0:T(8,128)} %shard_map.173), calls=%async_computation | async-start | bytes 1703936 | tf_op jit(solution)/shard_map/all_to_all | solution.py:190
  34.4 13.8 %all-to-all-start.1 = ((f32[16,16,128]{2,1,0:T(8,128)}), f32[16,16,128]{2,1,0:T(8,128)S(1)}, u32[]{:S(2)}, u32[]{:S(2)}) async-start(f32[16,16,128]{2,1,0:T(8,128)} %bitcast.33), calls=%async_computation.1 | async-start | bytes 262144 | tf_op jit(solution)/shard_map/all_to_all | solution.py:190
  49.9 13.1 %all-to-all-start.2 = ((f32[16,16,128]{2,1,0:T(8,128)}), f32[16,16,128]{2,1,0:T(8,128)S(1)}, u32[]{:S(2)}, u32[]{:S(2)}) async-start(f32[16,16,128]{2,1,0:T(8,128)} %bitcast.32), calls=%async_computation.2 | async-start | bytes 262144 | tf_op jit(solution)/shard_map/all_to_all | solution.py:190
where the time goes:
time: 96.2 us; the launch traced here: 95.1 us
  Pallas kernels  29 us (30%)
  blocking collectives  26.3 us (27%)
  waiting for transfers between devices  18.2 us (19%)
  starting transfers between devices  17.6 us (18%)
  other arithmetic  3.23 us (3%)
    pallas_call x7, Pallas kernels, call(): pl.pallas_call(body, out_shape=[pltpu.HBM(s, f32) for s in outs], in_spec...  29 us
    all_to_all x1, blocking collectives, exchange(): lax.all_to_all(blocks, 'hour', split_axis=0, concat_axis=0, tiled=True)  26.3 us
    all_to_all x3, waiting for transfers between devices, exchange(): lax.all_to_all(blocks, 'hour', split_axis=0, concat_axis=0, tiled=True)  18.2 us
    all_to_all x3, starting transfers between devices, exchange(): lax.all_to_all(blocks, 'hour', split_axis=0, concat_axis=0, tiled=True)  17.6 us
  transfers between devices with their start and end apart: 3, of which 2 were waited for; matrix products, arithmetic and copies ran while one was open for 3% of the time, Pallas kernels for 16%

commit v1 on v0

--- a/solution.py
+++ b/solution.py
@@ -14,7 +14,7 @@
 dual_step = 0.01
 LANES = 128
 SUBLANES = 8
-CHUNKS = 4
+NEAR = 5
 
 
 def compose(earlier, later):
@@ -144,7 +144,8 @@
     units = power.shape[2]
     lines, buses = shift_factors.shape
     ut, lt, bt = units // LANES, lines // LANES, buses // LANES
-    chunk = lines // CHUNKS
+    near_lines = lines * NEAR // 16
+    parts = (pl.ds(0, near_lines), pl.ds(near_lines, lines - near_lines))
     small = -(-(bt + 2) // SUBLANES) * SUBLANES
     at_power, at_upper, at_lower, at_flow = 0, ut, 2 * ut, 3 * ut
     at_total = at_flow + lt
@@ -156,18 +157,18 @@
     f32, bf16 = jnp.float32, jnp.bfloat16
     state = (hours * ut, LANES)
 
-    def call(body, outs, scratch, copies, *args, near=0, flops=0):
-        moved = sum(a.size * a.dtype.itemsize for a in args)
-        far = pl.BlockSpec(memory_space=pltpu.HBM)
+    def call(body, near, far, outs, outs_far, scratch, copies, flops=0):
+        moved = sum(a.size * a.dtype.itemsize for a in near + far)
+        inner, outer = (pl.BlockSpec(memory_space=m) for m in (pltpu.VMEM, pltpu.HBM))
         return pl.pallas_call(
             body,
-            out_shape=[pltpu.HBM(s, f32) for s in outs],
-            in_specs=[pl.BlockSpec(memory_space=pltpu.VMEM)] * near + [far] * (len(args) - near),
-            out_specs=[far] * len(outs),
+            out_shape=[pltpu.VMEM(s, f32) for s in outs] + [pltpu.HBM(s, f32) for s in outs_far],
+            in_specs=[inner] * len(near) + [outer] * len(far),
+            out_specs=[inner] * len(outs) + [outer] * len(outs_far),
             scratch_shapes=[pltpu.VMEM(*s) for s in scratch] + [pltpu.SemaphoreType.DMA((copies,))],
             compiler_params=pltpu.CompilerParams(vmem_limit_bytes=24 * 1024 * 1024),
             cost_estimate=pl.CostEstimate(flops=flops, bytes_accessed=moved, transcendentals=0),
-        )(*args[:near], *(pltpu.with_memory_space_constraint(a, pltpu.HBM) for a in args[near:]))
+        )(*near, *(pltpu.with_memory_space_constraint(a, pltpu.HBM) for a in far))
 
     class Copies:
         def __init__(self, semaphores):
@@ -204,46 +205,47 @@
     def part(ref, index):
         return ref[pl.ds(index * ut, ut), :]
 
-    def bring_chunks(copies, shift, shift_v):
-        return [
-            copies.bring(shift.at[pl.ds(c * chunk, chunk)], shift_v.at[pl.ds(c * chunk, chunk)])
-            for c in range(CHUNKS)
-        ]
+    def one_hot(settings, incidence):
+        buses_of = lax.broadcasted_iota(jnp.int32, (buses, LANES), 0).astype(f32)
+        for j in range(ut):
+            same = buses_of == settings[pl.ds(4 * ut + j, 1), :]
+            incidence[:, pl.ds(j * LANES, LANES)] = jnp.where(same, 1.0, 0.0).astype(bf16)
 
     def to_units(bus_dual, incidence, grid):
-        grid_grad = lax.dot_general(
-            bus_dual.astype(bf16), incidence[...], (((1,), (1,)), ((), ())),
-            preferred_element_type=f32,
-        )
-        spread(grid, 0, ut, grid_grad)
+        spread(
+            grid, 0, ut,
+            jnp.dot(bus_dual.astype(bf16), incidence[...], preferred_element_type=f32),
+        )
+
+    def across(left, right):
+        return lax.dot_general(left, right, (((1,), (1,)), ((), ())), preferred_element_type=f32)
 
     def inject(bar, load, incidence):
         wide_bar = wide(bar, 0, ut, ut).astype(bf16)
-        total = jnp.dot(wide_bar, incidence[...], preferred_element_type=f32)
-        return (total - load[...]).astype(bf16)
-
-    def advance(flow, injection, shift, limit, c):
-        at = pl.ds(c * chunk, chunk)
-        flows = lax.dot_general(
-            injection, shift[at, :], (((1,), (1,)), ((), ())), preferred_element_type=f32
-        )
-        probe = flow[:, at] + dual_step * flows
+        return (across(wide_bar, incidence[...]) - load[...]).astype(bf16)
+
+    def advance(flow, injection, shift, limit, at):
+        probe = flow[:, at] + dual_step * across(injection, shift[...])
         bound = dual_step * limit[:, at]
         return probe - jnp.clip(probe, -bound, bound)
 
-    def to_buses(flow, shift, c):
-        return jnp.dot(
-            flow.astype(bf16), shift[pl.ds(c * chunk, chunk), :], preferred_element_type=f32
-        )
-
-    def network(bar, load, flow, shift, limit, incidence, grid, arrived):
+    def to_buses(flow, shifts, wait):
+        total = jnp.zeros((hours, buses), f32)
+        for at, shift, arrived in zip(parts, shifts, (None, wait)):
+            if arrived:
+                arrived()
+            total = total + jnp.dot(
+                flow[:, at].astype(bf16), shift[...], preferred_element_type=f32
+            )
+        return total
+
+    def network(bar, load, flow, shifts, limit, incidence, new_flow, grid, wait):
         injection = inject(bar, load, incidence)
-        for c in range(CHUNKS):
-            arrived(c)
-            flow[:, pl.ds(c * chunk, chunk)] = advance(flow, injection, shift, limit, c)
-        to_units(
-            jnp.dot(flow[...].astype(bf16), shift[...], preferred_element_type=f32), incidence, grid
-        )
+        for at, shift, arrived in zip(parts, shifts, (None, wait)):
+            if arrived:
+                arrived()
+            new_flow[:, at] = advance(flow, injection, shift, limit, at)
+        to_units(to_buses(new_flow, shifts, None), incidence, grid)
 
     def local(upper, lower, before, grid, price, settings, put_power, bar, put):
         keep, bound = part(settings, 0), part(settings, 2)
@@ -320,28 +322,20 @@
         copies.send(blocks, out)
         copies.close()
 
-    def first(came, incidence, shift, settings, *rest):
-        power_o, upper_o, lower_o, bar_o, flow_o, load_o, notes_o, total_o = rest[:8]
-        shift_v, settings_v, power, upper, lower, bar, flow, load, notes, out, grid = rest[8:-1]
-        copies = Copies(rest[-1])
-        chunks = bring_chunks(copies, shift, shift_v)
-        come = [copies.bring(settings, settings_v)]
+    def first(came, shift, settings, shift_far, *rest):
+        power, upper, lower, bar, flow, load, notes, total_o = rest[:8]
+        shift_v, incidence, out, grid, semaphores = rest[8:]
+        copies = Copies(semaphores)
+        rest_of_shift = copies.bring(shift_far.at[parts[1]], shift_v)
         flow[...] = wide(came, at_flow, lt, rows_in)
         load[...] = wide(came, at_load, bt, rows_in)
         notes[pl.ds(ut, hours), :] = rows(came, at_price, rows_in)
-        copies.send(flow, flow_o)
-        copies.send(load, load_o)
-        come[0].wait()
+        one_hot(settings, incidence)
         capacity, pull = capacities(
-            rows(came, at_capacity, rows_in), settings_v, sum_blocks(came, at_total, rows_in)
+            rows(came, at_capacity, rows_in), settings, sum_blocks(came, at_total, rows_in)
         )
         notes[pl.ds(0, ut), :] = capacity
-        copies.send(notes, notes_o)
-        bus_dual = jnp.zeros((hours, buses), f32)
-        for c in range(CHUNKS):
-            chunks[c].wait()
-            bus_dual = bus_dual + to_buses(flow[:, pl.ds(c * chunk, chunk)], shift_v, c)
-        to_units(bus_dual, incidence, grid)
+        to_units(to_buses(flow, (shift, shift_v), rest_of_shift.wait), incidence, grid)
         total = [jnp.zeros((ut, LANES), f32)]
 
         def put(hour, lifted, low):
@@ -355,110 +349,64 @@
 
         local(
             received(at_upper), received(at_lower), received(at_power), grid,
-            received(at_price, 1), settings_v, writer(power), bar, put,
+            received(at_price, 1), settings, writer(power), bar, put,
         )
         for peer in range(ndev):
             out[pl.ds(peer * ut, ut), :] = total[0]
         copies.send(out, total_o)
-        copies.send(power, power_o)
-        copies.send(bar, bar_o)
-        copies.send(upper, upper_o)
-        copies.send(lower, lower_o)
         copies.close()
 
-    def middle(ahead, *refs):
-        given, outs, scratch = refs[:11], refs[11:16], refs[16:-1]
-        copies = Copies(refs[-1])
-        held = dict(zip(names, scratch))
-        incidence, shift, *others = given
-        come = {}
-        for name, source in zip(names, others):
-            come[name] = copies.bring(source, held[name])
-            if name == "flow":
-                chunks = bring_chunks(copies, shift, scratch[-6])
-        shift_v, grid, power_v, bar_v, lifted, low = scratch[-6:]
-        for name in ("bar", "load", "flow", "line"):
-            come.pop(name).wait()
-        net = (held["load"], held["flow"], shift_v, held["line"], incidence, grid)
-        network(held["bar"], *net, lambda c: chunks[c].wait())
-        if not ahead:
-            copies.send(held["flow"], outs[0])
-        for copy in come.values():
-            copy.wait()
+    def middle(
+        ahead, shift, bar, load, flow, line, upper, lower, power, notes, settings,
+        shift_far, new_flow, new_power, lifted, low, more, shift_v, incidence, spare, semaphores,
+    ):
+        rest_of_shift = Copies(semaphores).bring(shift_far.at[parts[1]], shift_v)
+        one_hot(settings, incidence)
+        shifts = (shift, shift_v)
+        grid, new_bar = (more, spare) if ahead else (spare, more)
+        network(
+            bar, load, flow, shifts, line, incidence, new_flow, grid, rest_of_shift.wait
+        )
 
         def put(hour, lift, new_low):
             lifted[pl.ds(hour * ut, ut), :] = lift
             low[pl.ds(hour * ut, ut), :] = new_low
 
         local(
-            reader(held["upper"]), reader(held["lower"]), reader(held["power"]), grid,
-            lambda hour: held["notes"][pl.ds(ut + hour, 1), :], held["settings"],
-            writer(power_v), bar_v, put,
-        )
-        for value, out in zip((power_v, lifted, low), outs[1:]):
-            copies.send(value, out)
+            reader(upper), reader(lower), reader(power), grid,
+            lambda hour: notes[pl.ds(ut + hour, 1), :], settings, writer(new_power), new_bar, put,
+        )
         if ahead:
-            network(bar_v, *net, lambda c: None)
-            copies.send(held["flow"], outs[0])
-            copies.send(grid, outs[4])
-        else:
-            copies.send(bar_v, outs[4])
-        copies.close()
-
-    names = (
-        "bar", "load", "flow", "line", "upper", "lower", "power", "notes", "settings",
-    )
-
-    def update(came, lifted, notes, settings, *rest):
-        upper_o, notes_o, total_o, lifted_v, notes_v, settings_v, upper, out, semaphores = rest
-        copies = Copies(semaphores)
-        come = [
-            copies.bring(notes, notes_v),
-            copies.bring(settings, settings_v),
-            copies.bring(lifted, lifted_v),
-        ]
-        total = sum_blocks(came, 0, ut)
-        come[0].wait()
-        come[1].wait()
-        capacity, pull = capacities(part(notes_v, 0), settings_v, total)
-        notes_v[pl.ds(0, ut), :] = capacity
-        copies.send(notes_v, notes_o)
-        come[2].wait()
+            network(new_bar, load, new_flow, shifts, line, incidence, new_flow, grid, None)
+
+    def raise_upper(came, lifted, notes, settings, upper, new_notes):
+        capacity, pull = capacities(part(notes, 0), settings, sum_blocks(came, 0, ut))
+        new_notes[pl.ds(0, ut), :] = capacity
+        new_notes[pl.ds(ut, hours), :] = notes[pl.ds(ut, hours), :]
         total = jnp.zeros((ut, LANES), f32)
         for hour in range(hours):
-            new = jnp.maximum(part(lifted_v, hour) - pull, 0.0)
+            new = jnp.maximum(part(lifted, hour) - pull, 0.0)
             upper[pl.ds(hour * ut, ut), :] = new
             total = total + new
+        return total
+
+    def update(came, lifted, notes, settings, upper, new_notes, total_o, out, semaphores):
+        total = raise_upper(came, lifted, notes, settings, upper, new_notes)
         for peer in range(ndev):
             out[pl.ds(peer * ut, ut), :] = total
+        copies = Copies(semaphores)
         copies.send(out, total_o)
-        copies.send(upper, upper_o)
         copies.close()
 
-    def last(came, incidence, *refs):
-        outs, scratch, copies = refs[10:12], refs[12:-1], Copies(refs[-1])
-        held = dict(zip(final_names, scratch))
-        shift_v, out, upper, bar = scratch[-4:]
-        come = {
-            name: copies.bring(source, held[name]) for name, source in zip(final_names, refs)
-        }
-        chunks = bring_chunks(copies, refs[9], shift_v)
-        total = sum_blocks(came, 0, ut)
-        for name in ("notes", "settings", "lifted"):
-            come.pop(name).wait()
-        notes, settings = held["notes"], held["settings"]
-        capacity, pull = capacities(part(notes, 0), settings, total)
-        notes[pl.ds(0, ut), :] = capacity
-        copies.send(notes, outs[1])
-        total = jnp.zeros((ut, LANES), f32)
-        for hour in range(hours):
-            new = jnp.maximum(part(held["lifted"], hour) - pull, 0.0)
-            upper[pl.ds(hour * ut, ut), :] = new
-            total = total + new
+    def last(
+        came, shift, lifted, lower, power, grid, notes, settings, load, flow, line,
+        shift_far, new_notes, out_o, shift_v, incidence, out, upper, bar, semaphores,
+    ):
+        copies = Copies(semaphores)
+        rest_of_shift = copies.bring(shift_far.at[parts[1]], shift_v)
+        total = raise_upper(came, lifted, notes, settings, upper, new_notes)
         for peer in range(ndev):
             out[pl.ds(peer * rows_back + back_total, ut), :] = total
-        for name in ("lower", "power", "grid"):
-            come.pop(name).wait()
 
         def put_power(hour, value):
             out[pl.ds(hour * rows_back, ut), :] = value
@@ -468,45 +416,39 @@
             out[pl.ds(hour * rows_back + 2 * ut, ut), :] = low
 
         local(
-            reader(upper), reader(held["lower"]), reader(held["power"]), held["grid"],
+            reader(upper), reader(lower), reader(power), grid,
             lambda hour: notes[pl.ds(ut + hour, 1), :], settings, put_power, bar, put,
         )
         blocks = out.reshape(ndev, rows_back, LANES)
-        copies.send(blocks.at[:, pl.ds(0, back_flow)], outs[0].at[:, pl.ds(0, back_flow)])
-        for copy in come.values():
-            copy.wait()
-        injection = inject(bar, held["load"], incidence)
-        tiles_of = chunk // LANES
-        for c in range(CHUNKS):
-            chunks[c].wait()
-            new = advance(held["flow"], injection, shift_v, held["line"], c)
-            spread(out, back_flow + c * tiles_of, rows_back, new)
-        at = pl.ds(back_flow, lt)
-        copies.send(blocks.at[:, at], outs[0].at[:, at])
+        copies.send(blocks.at[:, pl.ds(0, back_flow)], out_o.at[:, pl.ds(0, back_flow)])
+        one_hot(settings, incidence)
+        injection = inject(bar, load, incidence)
+        row = back_flow
+        for at, factors, arrived in zip(parts, (shift, shift_v), (None, rest_of_shift.wait)):
+            if arrived:
+                arrived()
+            new = advance(flow, injection, factors, line, at)
+            spread(out, row, rows_back, new)
+            row += new.shape[1] // LANES
+        flow_rows = pl.ds(back_flow, lt)
+        copies.send(blocks.at[:, flow_rows], out_o.at[:, flow_rows])
         copies.close()
 
-    final_names = (
-        "notes", "settings", "lifted", "lower", "power", "grid", "load", "flow", "line",
-    )
-
     def finish(came, notes, settings, power_o, upper_o, lower_o, flow_o, capacity_o, *rest):
-        notes_v, settings_v, upper, own, semaphores = rest
+        notes_v, upper, own, semaphores = rest
         copies = Copies(semaphores)
-        come = [copies.bring(notes, notes_v), copies.bring(settings, settings_v)]
         blocks = came.reshape(ndev, rows_back, LANES)
         copies.send(blocks.at[:, pl.ds(0, ut)], power_o)
         copies.send(blocks.at[:, pl.ds(2 * ut, ut)], lower_o)
         copies.send(blocks.at[:, pl.ds(back_flow, lt)], flow_o)
         total = sum_blocks(came, back_total, rows_back)
-        for copy in come:
-            copy.wait()
-        capacity, pull = capacities(part(notes_v, 0), settings_v, total)
-        notes_v[pl.ds(0, ut), :] = capacity
-        own[...] = notes_v[pl.ds(lax.axis_index("hour"), 1), :]
-        copies.send(own, capacity_o)
+        capacity, pull = capacities(part(notes, 0), settings, total)
         for peer in range(ndev):
             upper[peer] = jnp.maximum(came[pl.ds(peer * rows_back + ut, ut), :] - pull, 0.0)
         copies.send(upper, upper_o)
+        notes_v[...] = capacity
+        own[...] = notes_v[pl.ds(lax.axis_index("hour"), 1), :]
+        copies.send(own, capacity_o)
         copies.close()
 
 
@@ -514,83 +456,88 @@
         return vector.reshape(-1, LANES)
 
     settings = jnp.concatenate(
-        [tiles(v) for v in (1.0 - leakage, initial_state, power_limit, capacity_cost)]
+        [
+            tiles(v)
+            for v in (1.0 - leakage, initial_state, power_limit, capacity_cost, unit_bus.astype(f32))
+        ]
     )
     line = line_limit.reshape(1, lines)
-    incidence = (unit_bus[:, None] == jnp.arange(buses, dtype=jnp.int32)[None, :]).astype(bf16)
-    shift = shift_factors
-
-    state_v, wide_v, load_v = (state, f32), ((hours, lines), f32), ((hours, buses), f32)
-    notes, notes_v = (ut + hours, LANES), ((ut + hours, LANES), f32)
-    settings_v, line_v = ((4 * ut, LANES), f32), ((1, lines), f32)
-    shift_v = ((lines, buses), bf16)
+    shift, shift_far = shift_factors[:near_lines], shift_factors
+
+    state_v, incidence_v = (state, f32), ((buses, units), bf16)
+    shift_v = ((lines - near_lines, buses), bf16)
+    notes = (ut + hours, LANES)
     flops = 4 * hours * buses * (lines + units)
 
     (sent,) = call(
         pack,
+        [],
+        [
+            power.reshape(scen, ut, LANES),
+            upper_dual.reshape(scen, ut, LANES),
+            lower_dual.reshape(scen, ut, LANES),
+            flow_dual.reshape(scen, lt, LANES),
+            load.reshape(scen, buses),
+            price.reshape(1, scen),
+            capacity.reshape(1, LANES),
+        ],
+        [],
         [(ndev, rows_in, LANES)],
         [
             ((scen, buses), bf16), ((1, scen), f32), ((1, LANES), f32),
             ((ndev * rows_in, LANES), f32),
         ],
         8,
-        power.reshape(scen, ut, LANES),
-        upper_dual.reshape(scen, ut, LANES),
-        lower_dual.reshape(scen, ut, LANES),
-        flow_dual.reshape(scen, lt, LANES),
-        load.reshape(scen, buses),
-        price.reshape(1, scen),
-        capacity.reshape(1, LANES),
     )
     came = exchange(sent).reshape(-1, LANES)
     power, upper, lower, bar, flow, load, note, total = call(
         first,
-        [state] * 4 + [(hours, lines), (hours, buses), notes, state],
-        [shift_v, settings_v] + [state_v] * 4 + [wide_v, load_v, notes_v, state_v, state_v],
-        CHUNKS + 9,
-        came, incidence, shift, settings,
-        near=2, flops=flops,
+        [came, shift, settings],
+        [shift_far],
+        [state] * 4 + [(hours, lines), (hours, buses), notes],
+        [state],
+        [shift_v, incidence_v, state_v, state_v],
+        2,
+        flops=flops,
     )
     for iteration in range(1, ITERS - 1):
         ahead = iteration == ITERS - 2
         came = exchange(total.reshape(ndev, ut, LANES)).reshape(-1, LANES)
         flow, power, lifted, lower, more = call(
             functools.partial(middle, ahead),
+            [shift, bar, load, flow, line, upper, lower, power, note, settings],
+            [shift_far],
             [(hours, lines)] + [state] * 4,
-            [state_v, load_v, wide_v, line_v, state_v, state_v, state_v, notes_v]
-            + [settings_v, shift_v] + [state_v] * 5,
-            CHUNKS + 14,
-            incidence, shift, bar, load, flow, line, upper, lower, power, note, settings,
-            near=1, flops=flops * (1 + ahead),
+            [],
+            [shift_v, incidence_v, state_v],
+            1,
+            flops=flops * (1 + ahead),
         )
         if not ahead:
             bar = more
             upper, note, total = call(
-                update,
-                [state, notes, state],
-                [state_v, notes_v, settings_v, state_v, state_v],
-                6,
-                came, lifted, note, settings,
-                near=1,
+                update, [came, lifted, note, settings], [], [state, notes], [state], [state_v], 1
             )
-    sent, note = call(
+    note, sent = call(
         last,
-        [(ndev, rows_back, LANES), notes],
-        [notes_v, settings_v] + [state_v] * 4 + [load_v, wide_v, line_v, shift_v]
-        + [((ndev * rows_back, LANES), f32), state_v, state_v],
-        CHUNKS + 12,
-        came, incidence, note, settings, lifted, lower, power, more, load, flow, line, shift,
-        near=2, flops=flops,
+        [came, shift, lifted, lower, power, more, note, settings, load, flow, line],
+        [shift_far],
+        [notes],
+        [(ndev, rows_back, LANES)],
+        [shift_v, incidence_v, ((ndev * rows_back, LANES), f32), state_v, state_v],
+        3,
+        flops=flops,
     )
     came = exchange(sent).reshape(-1, LANES)
     hourly = (scen, ut, LANES)
     power, upper, lower, flow, capacity = call(
         finish,
+        [came, note, settings],
+        [],
+        [],
         [hourly, hourly, hourly, (scen, lt, LANES), (1, LANES)],
-        [notes_v, settings_v, (hourly, f32), ((1, LANES), f32)],
-        7,
-        came, note, settings,
-        near=1,
+        [((ut, LANES), f32), (hourly, f32), ((1, LANES), f32)],
+        5,
     )
     return (
         power.reshape(scen, 1, units),
@@ -608,7 +555,7 @@
         power.shape[0] == ndev
         and power.shape[1] == 1
         and capacity.shape[0] == LANES
-        and flow_dual.shape[2] % (CHUNKS * LANES) == 0
+        and flow_dual.shape[2] % (16 * LANES) == 0
         and ndev % (2 * SUBLANES) == 0
         and all(size % (SUBLANES * LANES) == 0 for size in (power.shape[2], flow_dual.shape[2]))
         and buses % LANES == 0

time: 96.2 us -> 90.3 us (0.939)
  Pallas kernels: 29 us -> 22.2 us
  waiting for transfers between devices: 18.2 us -> 22.8 us
  other arithmetic: 3.23 us -> 0.01 us
  local copies, waits for them, and re-layouts: 0 us -> 1.44 us
  blocking collectives: 26.3 us -> 25.2 us
    pallas_call x7, Pallas kernels: 29 us -> 22.2 us  [call(): pl.pallas_call(body, out_shape=[pltpu.VMEM(s, f32) for s in outs] + [pltp...]
    all_to_all x3, waiting for transfers between devices: 18.2 us -> 22.8 us  [exchange(): lax.all_to_all(blocks, 'hour', split_axis=0, concat_axis=0, tiled=True)]
    slice x0 -> x1, local copies, waits for them, and re-layouts: none -> 1.41 us  [by_scenarios(): shift, shift_far = (shift_factors[:near_lines], shift_factors)]
    concatenate x1, other arithmetic: 1.33 us -> 0.01 us  [by_scenarios(): jnp.concatenate([tiles(v) for v in (1.0 - leakage, initial_state, power_l...]
    convert_element_type x1 -> x0, other arithmetic: 1.2 us -> none  [by_scenarios(): (unit_bus[:, None] == jnp.arange(buses, dtype=jnp.int32)[None, :]).astype...]
    all_to_all x1, blocking collectives: 26.3 us -> 25.2 us  [exchange(): lax.all_to_all(blocks, 'hour', split_axis=0, concat_axis=0, tiled=True)]
  transfers between devices with their start and end apart: 3 -> 3, of which waited for: 2 -> 3; matrix products, arithmetic and copies ran while one was open for 3% -> 2% of each run, Pallas kernels for 16% -> 13%
where the time goes in v1:
time: 90.3 us; the launch traced here: 89.3 us
  blocking collectives  25.2 us (28%)
  waiting for transfers between devices  22.8 us (25%)
  Pallas kernels  22.2 us (25%)
  starting transfers between devices  16.8 us (19%)
  local copies, waits for them, and re-layouts  1.44 us (2%)
    all_to_all x1, blocking collectives, exchange(): lax.all_to_all(blocks, 'hour', split_axis=0, concat_axis=0, tiled=True)  25.2 us
    all_to_all x3, waiting for transfers between devices, exchange(): lax.all_to_all(blocks, 'hour', split_axis=0, concat_axis=0, tiled=True)  22.8 us
    pallas_call x7, Pallas kernels, call(): pl.pallas_call(body, out_shape=[pltpu.VMEM(s, f32) for s in outs] + [pltp...  22.2 us
    all_to_all x3, starting transfers between devices, exchange(): lax.all_to_all(blocks, 'hour', split_axis=0, concat_axis=0, tiled=True)  16.8 us
  transfers between devices with their start and end apart: 3, of which 3 were waited for; matrix products, arithmetic and copies ran while one was open for 2% of the time, Pallas kernels for 13%

profile of v1, /device:TPU:0, one launch (start us, length us, event | category | flops | bytes accessed | tf_op | source)
XLA Modules:
  0.0 89.3 jit_solution(3519148443319004892)
XLA Ops:
  0.6 0.0 copy-start.1
  0.6 0.0 copy-start.2
  0.7 0.0 copy-start.3
  0.7 0.0 copy-start.4
  0.7 0.0 copy-start.5
  0.7 2.1 %shard_map.173 = f32[16,104,128]{2,1,0:T(8,128)} custom-call(f32[16,16,128]{2,1,0:T(8,128)} %bitcast.39, f32[16,16,128]{2,1,0:T(8,128)} %bitcast.40, f32[16,16,128]{2,1,0:T(8,128)} %bitcast.41, f32[16,32,128]{2,1,0:T(8,128)} %bitcast.36, bf16[16,512]{1,0:T(8,128)(2,1)} %bitcast.42, f32[1,16]{1,0:T(1,128)} %bitcast.43, f32[1,128]{1,0:T(1,128)} %bitcast.44), custom_call_target="tpu_custom_call" | custom-call | bytes 672320 | tf_op jit(solution)/shard_map/pallas_call | solution.py:163
  2.8 7.4 %all-to-all-start = ((f32[16,104,128]{2,1,0:T(8,128)}), f32[16,104,128]{2,1,0:T(8,128)S(1)}, u32[]{:S(2)}, u32[]{:S(2)}) async-start(f32[16,104,128]{2,1,0:T(8,128)} %shard_map.173), calls=%async_computation | async-start | bytes 1703936 | tf_op jit(solution)/shard_map/all_to_all | solution.py:191
  10.2 0.0 copy-start
  10.2 1.4 %slice.3.shift = bf16[1280,512]{1,0:T(8,128)(2,1)S(1)} slice(bf16[4096,512]{1,0:T(8,128)(2,1)} %shift_far.7), slice={[0:1280], [0:512]} | slice | bytes 2621440 | tf_op jit(solution)/shard_map/slice | solution.py:465
  11.6 0.0 copy-done.1
  11.6 0.0 copy-done.2
  11.7 0.0 copy-done.4
  11.7 18.2 %all-to-all-done = f32[16,104,128]{2,1,0:T(8,128)S(1)} async-done(((f32[16,104,128]{2,1,0:T(8,128)}), f32[16,104,128]{2,1,0:T(8,128)S(1)}, u32[]{:S(2)}, u32[]{:S(2)}) %all-to-all-start) | async-done | bytes 852000 | tf_op jit(solution)/shard_map/all_to_all | solution.py:191
  30.0 3.6 %shard_map.174 = (f32[256,128]{1,0:T(8,128)S(1)}, f32[256,128]{1,0:T(8,128)S(1)}, f32[256,128]{1,0:T(8,128)S(1)}, f32[256,128]{1,0:T(8,128)S(1)}, f32[16,4096]{1...) custom-call(f32[1664,128]{1,0:T(8,128)S(1)} %bitcast.29, ...), custom_call_target="tpu_custom_call" | custom-call | flops 201326592 | bytes 6397952 | tf_op jit(solution)/shard_map/pallas_call | solution.py:163
  33.5 5.8 %all-to-all-start.1 = ((f32[16,16,128]{2,1,0:T(8,128)}), f32[16,16,128]{2,1,0:T(8,128)S(1)}, u32[]{:S(2)}, u32[]{:S(2)}) async-start(f32[16,16,128]{2,1,0:T(8,128)} %bitcast.38), calls=%async_computation.1 | async-start | bytes 262144 | tf_op jit(solution)/shard_map/all_to_all | solution.py:191
  39.4 4.3 %shard_map.175 = (f32[16,4096]{1,0:T(8,128)S(1)}, f32[256,128]{1,0:T(8,128)S(1)}, f32[256,128]{1,0:T(8,128)S(1)}, f32[256,128]{1,0:T(8,128)S(1)}, f32[256,128]{1,0:T(8,128)S(1)}) custom-call(bf16[1280,512]{1,0:T(8,128)(2,1)S(1)} %slice.3.shift, f32[256,128]{1,0:T(8,128)S(1)} %get-tuple-element.34.bar, f32[16,512]{1,0:T(8,128)S(1)} %get-tuple-element.35.load, ...), custom_call_target="tpu_custom_call" | custom-call | flops 201326592 | bytes 6397952 | tf_op jit(solution)/shard_map/pallas_call | solution.py:163
  43.8 3.6 %all-to-all-done.1 = f32[16,16,128]{2,1,0:T(8,128)S(1)} async-done(((f32[16,16,128]{2,1,0:T(8,128)}), f32[16,16,128]{2,1,0:T(8,128)S(1)}, u32[]{:S(2)}, u32[]{:S(2)}) %all-to-all-start.1) | async-done | bytes 131104 | tf_op jit(solution)/shard_map/all_to_all | solution.py:191
  47.3 0.7 shard_map.176
  48.1 3.5 %all-to-all-start.2 = ((f32[16,16,128]{2,1,0:T(8,128)}), f32[16,16,128]{2,1,0:T(8,128)S(1)}, u32[]{:S(2)}, u32[]{:S(2)}) async-start(f32[16,16,128]{2,1,0:T(8,128)} %bitcast.37), calls=%async_computation.2 | async-start | bytes 262144 | tf_op jit(solution)/shard_map/all_to_all | solution.py:191
  51.6 6.9 %shard_map.177 = (f32[16,4096]{1,0:T(8,128)S(1)}, f32[256,128]{1,0:T(8,128)S(1)}, f32[256,128]{1,0:T(8,128)S(1)}, f32[256,128]{1,0:T(8,128)S(1)}, f32[256,128]{1,0:T(8,128)S(1)}) custom-call(bf16[1280,512]{1,0:T(8,128)(2,1)S(1)} %slice.3.shift, f32[256,128]{1,0:T(8,128)S(1)} %get-tuple-element.43.bar, f32[16,512]{1,0:T(8,128)S(1)} %get-tuple-element.35.load, ...), custom_call_target="tpu_custom_call" | custom-call | flops 402653184 | bytes 6397952 | tf_op jit(solution)/shard_map/pallas_call | solution.py:163
  58.5 1.0 %all-to-all-done.2 = f32[16,16,128]{2,1,0:T(8,128)S(1)} async-done(((f32[16,16,128]{2,1,0:T(8,128)}), f32[16,16,128]{2,1,0:T(8,128)S(1)}, u32[]{:S(2)}, u32[]{:S(2)}) %all-to-all-start.2) | async-done | bytes 131104 | tf_op jit(solution)/shard_map/all_to_all | solution.py:191
  59.5 3.7 %shard_map.178 = (f32[32,128]{1,0:T(8,128)S(1)}, f32[16,96,128]{2,1,0:T(8,128)}) custom-call(f32[256,128]{1,0:T(8,128)S(1)} %bitcast.31, bf16[1280,512]{1,0:T(8,128)(2,1)S(1)} %slice.3.shift, f32[256,128]{1,0:T(8,128)S(1)} %get-tuple-element.49.lifted, f32[256,128]{1,0:T(8,128)S(1)} %get-tuple-element.50.lower, f32[256,128]{1,0:T(8,128)S(1)} %get-tuple-element.51.power, ...), custom_call_target="tpu_custom_call" | custom-call | flops 201326592 | bytes 6529024 | tf_op jit(solution)/shard_map/pallas_call | solution.py:163
  63.2 25.2 %all_to_all.20 = f32[16,96,128]{2,1,0:T(8,128)S(1)} all-to-all(f32[16,96,128]{2,1,0:T(8,128)} %get-tuple-element.54), channel_id=1, replica_groups=mesh['groups'=2,'hour'=16] {'hour'}, dimensions={0} | all-to-all | bytes 1572864 | tf_op jit(solution)/shard_map/all_to_all | solution.py:191
  88.5 0.9 shard_map.179
  (8 shorter events, 0.0 us)
Async XLA Ops:
  0.6 11.0 %copy-start.1 = (f32[2048]{0:T(1024)S(1)}, f32[2048]{0:T(1024)}, u32[]{:S(2)}) copy-start(f32[2048]{0:T(1024)} %param.24) | copy-start | bytes 24580
  0.6 11.0 %copy-start.2 = (f32[2048]{0:T(1024)S(1)}, f32[2048]{0:T(1024)}, u32[]{:S(2)}) copy-start(f32[2048]{0:T(1024)} %param.25) | copy-start | bytes 24580
  0.7 11.0 %copy-start.3 = (f32[2048]{0:T(1024)S(1)}, f32[2048]{0:T(1024)}, u32[]{:S(2)}) copy-start(f32[2048]{0:T(1024)} %param.26) | copy-start | bytes 24580
  0.7 11.0 %copy-start.4 = (f32[2048]{0:T(1024)S(1)}, f32[2048]{0:T(1024)}, u32[]{:S(2)}) copy-start(f32[2048]{0:T(1024)} %param.27) | copy-start | bytes 24580
  0.7 11.0 %copy-start.5 = (s32[2048]{0:T(1024)S(1)}, s32[2048]{0:T(1024)}, u32[]{:S(2)}) copy-start(s32[2048]{0:T(1024)} %param.23) | copy-start | bytes 24580
  2.8 27.2 %all-to-all-start = ((f32[16,104,128]{2,1,0:T(8,128)}), f32[16,104,128]{2,1,0:T(8,128)S(1)}, u32[]{:S(2)}, u32[]{:S(2)}) async-start(f32[16,104,128]{2,1,0:T(8,128)} %shard_map.173), calls=%async_computation | async-start | bytes 1703936 | tf_op jit(solution)/shard_map/all_to_all | solution.py:191
  10.2 29.2 %copy-start = (f32[4096]{0:T(1024)S(1)}, f32[4096]{0:T(1024)}, u32[]{:S(2)}) copy-start(f32[4096]{0:T(1024)} %param.22) | copy-start | bytes 49156
  33.5 13.8 %all-to-all-start.1 = ((f32[16,16,128]{2,1,0:T(8,128)}), f32[16,16,128]{2,1,0:T(8,128)S(1)}, u32[]{:S(2)}, u32[]{:S(2)}) async-start(f32[16,16,128]{2,1,0:T(8,128)} %bitcast.38), calls=%async_computation.1 | async-start | bytes 262144 | tf_op jit(solution)/shard_map/all_to_all | solution.py:191
  48.1 11.4 %all-to-all-start.2 = ((f32[16,16,128]{2,1,0:T(8,128)}), f32[16,16,128]{2,1,0:T(8,128)S(1)}, u32[]{:S(2)}, u32[]{:S(2)}) async-start(f32[16,16,128]{2,1,0:T(8,128)} %bitcast.37), calls=%async_computation.2 | async-start | bytes 262144 | tf_op jit(solution)/shard_map/all_to_all | solution.py:191

commit v2 on v1

--- a/solution.py
+++ b/solution.py
@@ -1,5 +1,3 @@
-import functools
-
 import jax
 import jax.numpy as jnp
 from jax import lax
@@ -15,6 +13,7 @@
 LANES = 128
 SUBLANES = 8
 NEAR = 5
+LAST_NEAR = 6
 
 
 def compose(earlier, later):
@@ -146,14 +145,17 @@
     ut, lt, bt = units // LANES, lines // LANES, buses // LANES
     near_lines = lines * NEAR // 16
     parts = (pl.ds(0, near_lines), pl.ds(near_lines, lines - near_lines))
+    last_near = lines * LAST_NEAR // 16
+    last_parts = (pl.ds(0, last_near), pl.ds(last_near, lines - last_near))
     small = -(-(bt + 2) // SUBLANES) * SUBLANES
     at_power, at_upper, at_lower, at_flow = 0, ut, 2 * ut, 3 * ut
     at_total = at_flow + lt
     at_load = at_total + ut
     at_price, at_capacity = at_load + bt, at_load + bt + 1
     rows_in = at_load + small
-    back_total, back_flow = 3 * ut, 4 * ut
-    rows_back = back_flow + lt
+    back_total, back_bus = 3 * ut, 4 * ut
+    rows_back = back_bus + 2 * bt
+    rows_update = ut + 2 * bt
     f32, bf16 = jnp.float32, jnp.bfloat16
     state = (hours * ut, LANES)
 
@@ -224,11 +226,6 @@
         wide_bar = wide(bar, 0, ut, ut).astype(bf16)
         return (across(wide_bar, incidence[...]) - load[...]).astype(bf16)
 
-    def advance(flow, injection, shift, limit, at):
-        probe = flow[:, at] + dual_step * across(injection, shift[...])
-        bound = dual_step * limit[:, at]
-        return probe - jnp.clip(probe, -bound, bound)
-
     def to_buses(flow, shifts, wait):
         total = jnp.zeros((hours, buses), f32)
         for at, shift, arrived in zip(parts, shifts, (None, wait)):
@@ -239,12 +236,16 @@
             )
         return total
 
-    def network(bar, load, flow, shifts, limit, incidence, new_flow, grid, wait):
-        injection = inject(bar, load, incidence)
+    def held_back(probe, limit, at):
+        bound = dual_step * limit[:, at]
+        return probe - jnp.clip(probe, -bound, bound)
+
+    def network(injection, flow, shifts, limit, incidence, new_flow, grid, wait):
         for at, shift, arrived in zip(parts, shifts, (None, wait)):
             if arrived:
                 arrived()
-            new_flow[:, at] = advance(flow, injection, shift, limit, at)
+            probe = flow[:, at] + dual_step * across(injection, shift[...])
+            new_flow[:, at] = held_back(probe, limit, at)
         to_units(to_buses(new_flow, shifts, None), incidence, grid)
 
     def local(upper, lower, before, grid, price, settings, put_power, bar, put):
@@ -356,31 +357,51 @@
         copies.send(out, total_o)
         copies.close()
 
-    def middle(
-        ahead, shift, bar, load, flow, line, upper, lower, power, notes, settings,
-        shift_far, new_flow, new_power, lifted, low, more, shift_v, incidence, spare, semaphores,
+    def second(
+        shift, bar, load, flow, line, upper, lower, power, notes, settings, shift_far,
+        new_flow, new_power, lifted, low, sent, shift_v, incidence, grid, new_bar, semaphores,
+    ):
+        rest_of_shift = Copies(semaphores).bring(shift_far.at[parts[1]], shift_v)
+        one_hot(settings, incidence)
+        injection = inject(bar, load, incidence)
+        sent[pl.ds(0, hours), :] = injection.astype(f32)
+        network(
+            injection, flow, (shift, shift_v), line, incidence, new_flow, grid, rest_of_shift.wait
+        )
+        local(
+            reader(upper), reader(lower), reader(power), grid,
+            lambda hour: notes[pl.ds(ut + hour, 1), :], settings, writer(new_power), new_bar,
+            lift(lifted, low),
+        )
+        sent[pl.ds(hours, hours), :] = inject(new_bar, load, incidence).astype(f32)
+
+    def third(
+        shift, sent, load, flow, line, upper, lower, power, notes, settings, shift_far,
+        new_flow, new_power, lifted, low, grid, later, shift_v, incidence, new_bar, semaphores,
     ):
         rest_of_shift = Copies(semaphores).bring(shift_far.at[parts[1]], shift_v)
         one_hot(settings, incidence)
         shifts = (shift, shift_v)
-        grid, new_bar = (more, spare) if ahead else (spare, more)
-        network(
-            bar, load, flow, shifts, line, incidence, new_flow, grid, rest_of_shift.wait
-        )
-
-        def put(hour, lift, new_low):
-            lifted[pl.ds(hour * ut, ut), :] = lift
-            low[pl.ds(hour * ut, ut), :] = new_low
-
+        injection = sent[pl.ds(hours, hours), :].astype(bf16)
+        network(injection, flow, shifts, line, incidence, new_flow, grid, rest_of_shift.wait)
         local(
             reader(upper), reader(lower), reader(power), grid,
-            lambda hour: notes[pl.ds(ut + hour, 1), :], settings, writer(new_power), new_bar, put,
-        )
-        if ahead:
-            network(new_bar, load, new_flow, shifts, line, incidence, new_flow, grid, None)
-
-    def raise_upper(came, lifted, notes, settings, upper, new_notes):
-        capacity, pull = capacities(part(notes, 0), settings, sum_blocks(came, 0, ut))
+            lambda hour: notes[pl.ds(ut + hour, 1), :], settings, writer(new_power), new_bar,
+            lift(lifted, low),
+        )
+        injection = inject(new_bar, load, incidence)
+        later[...] = injection.astype(f32)
+        network(injection, new_flow, shifts, line, incidence, new_flow, grid, None)
+
+    def lift(lifted, low):
+        def put(hour, new_lifted, new_low):
+            lifted[pl.ds(hour * ut, ut), :] = new_lifted
+            low[pl.ds(hour * ut, ut), :] = new_low
+
+        return put
+
+    def raise_upper(came, step, lifted, notes, settings, upper, new_notes):
+        capacity, pull = capacities(part(notes, 0), settings, sum_blocks(came, 0, step))
         new_notes[pl.ds(0, ut), :] = capacity
         new_notes[pl.ds(ut, hours), :] = notes[pl.ds(ut, hours), :]
         total = jnp.zeros((ut, LANES), f32)
@@ -390,57 +411,68 @@
             total = total + new
         return total
 
-    def update(came, lifted, notes, settings, upper, new_notes, total_o, out, semaphores):
-        total = raise_upper(came, lifted, notes, settings, upper, new_notes)
+    def update(came, lifted, notes, settings, sent, upper, new_notes, out_o, out, semaphores):
+        spread(out, ut, rows_update, sent[pl.ds(0, hours), :])
+        spread(out, ut + bt, rows_update, sent[pl.ds(hours, hours), :])
+        total = raise_upper(came, ut, lifted, notes, settings, upper, new_notes)
         for peer in range(ndev):
-            out[pl.ds(peer * ut, ut), :] = total
+            out[pl.ds(peer * rows_update, ut), :] = total
         copies = Copies(semaphores)
-        copies.send(out, total_o)
+        copies.send(out, out_o)
         copies.close()
 
     def last(
-        came, shift, lifted, lower, power, grid, notes, settings, load, flow, line,
-        shift_far, new_notes, out_o, shift_v, incidence, out, upper, bar, semaphores,
+        came, lifted, lower, power, grid, notes, settings, load, later,
+        new_notes, out_o, early_o, incidence, out, early, upper, bar, semaphores,
     ):
         copies = Copies(semaphores)
-        rest_of_shift = copies.bring(shift_far.at[parts[1]], shift_v)
-        total = raise_upper(came, lifted, notes, settings, upper, new_notes)
+        for step in range(2):
+            early[pl.ds(step * scen, scen), :] = wide(came, ut + step * bt, bt, rows_update)
+        copies.send(early, early_o)
+        total = raise_upper(came, rows_update, lifted, notes, settings, upper, new_notes)
         for peer in range(ndev):
             out[pl.ds(peer * rows_back + back_total, ut), :] = total
 
         def put_power(hour, value):
             out[pl.ds(hour * rows_back, ut), :] = value
 
-        def put(hour, lift, low):
-            out[pl.ds(hour * rows_back + ut, ut), :] = lift
+        def put(hour, new_lifted, low):
+            out[pl.ds(hour * rows_back + ut, ut), :] = new_lifted
             out[pl.ds(hour * rows_back + 2 * ut, ut), :] = low
 
         local(
             reader(upper), reader(lower), reader(power), grid,
             lambda hour: notes[pl.ds(ut + hour, 1), :], settings, put_power, bar, put,
         )
-        blocks = out.reshape(ndev, rows_back, LANES)
-        copies.send(blocks.at[:, pl.ds(0, back_flow)], out_o.at[:, pl.ds(0, back_flow)])
         one_hot(settings, incidence)
-        injection = inject(bar, load, incidence)
-        row = back_flow
-        for at, factors, arrived in zip(parts, (shift, shift_v), (None, rest_of_shift.wait)):
-            if arrived:
-                arrived()
-            new = advance(flow, injection, factors, line, at)
-            spread(out, row, rows_back, new)
-            row += new.shape[1] // LANES
-        flow_rows = pl.ds(back_flow, lt)
-        copies.send(blocks.at[:, flow_rows], out_o.at[:, flow_rows])
+        spread(out, back_bus, rows_back, later[...])
+        spread(out, back_bus + bt, rows_back, inject(bar, load, incidence).astype(f32))
+        copies.send(out, out_o)
         copies.close()
 
-    def finish(came, notes, settings, power_o, upper_o, lower_o, flow_o, capacity_o, *rest):
-        notes_v, upper, own, semaphores = rest
+    def hourly_flow(line, early, flow, turned, new_flow, early_v, flow_v, turned_v, semaphores):
         copies = Copies(semaphores)
+        come = [copies.bring(*pair) for pair in ((early, early_v), (flow, flow_v), (turned, turned_v))]
+        for copy in come:
+            copy.wait()
+        flows = jnp.dot(early_v[...].astype(bf16), turned_v[...], preferred_element_type=f32)
+        every = pl.ds(0, lines)
+        value = wide(flow_v, 0, lt, lt)
+        for step in range(2):
+            flow_step = flows[step * scen : (step + 1) * scen]
+            value = held_back(value + dual_step * flow_step, line, every)
+        new_flow[...] = value
+
+    def finish(
+        came, notes, settings, line, flow, turned, turned_far,
+        power_o, upper_o, lower_o, flow_o, capacity_o,
+        turned_v, notes_v, upper, own, out, semaphores,
+    ):
+        copies = Copies(semaphores)
+        rest_of_turned = copies.bring(turned_far.at[:, last_parts[1]], turned_v)
         blocks = came.reshape(ndev, rows_back, LANES)
         copies.send(blocks.at[:, pl.ds(0, ut)], power_o)
         copies.send(blocks.at[:, pl.ds(2 * ut, ut)], lower_o)
-        copies.send(blocks.at[:, pl.ds(back_flow, lt)], flow_o)
         total = sum_blocks(came, back_total, rows_back)
         capacity, pull = capacities(part(notes, 0), settings, total)
         for peer in range(ndev):
@@ -449,6 +481,20 @@
         notes_v[...] = capacity
         own[...] = notes_v[pl.ds(lax.axis_index("hour"), 1), :]
         copies.send(own, capacity_o)
+        injections = jnp.concatenate(
+            [wide(came, back_bus + step * bt, bt, rows_back) for step in range(2)], axis=0
+        ).astype(bf16)
+        row = 0
+        for at, factors, arrived in zip(last_parts, (turned, turned_v), (None, rest_of_turned.wait)):
+            if arrived:
+                arrived()
+            flows = dual_step * jnp.dot(injections, factors[...], preferred_element_type=f32)
+            value = flow[:, at]
+            for step in range(2):
+                value = held_back(value + flows[step * scen : (step + 1) * scen], line, at)
+            spread(out, row, lt, value)
+            row += value.shape[1] // LANES
+        copies.send(out.reshape(scen, lt, LANES), flow_o)
         copies.close()
 
 
@@ -462,7 +508,7 @@
         ]
     )
     line = line_limit.reshape(1, lines)
-    shift, shift_far = shift_factors[:near_lines], shift_factors
+    shift, shift_far, turned = shift_factors[:near_lines], shift_factors, shift_factors.T
 
     state_v, incidence_v = (state, f32), ((buses, units), bf16)
     shift_v = ((lines - near_lines, buses), bf16)
@@ -500,44 +546,74 @@
         2,
         flops=flops,
     )
-    for iteration in range(1, ITERS - 1):
-        ahead = iteration == ITERS - 2
-        came = exchange(total.reshape(ndev, ut, LANES)).reshape(-1, LANES)
-        flow, power, lifted, lower, more = call(
-            functools.partial(middle, ahead),
-            [shift, bar, load, flow, line, upper, lower, power, note, settings],
-            [shift_far],
-            [(hours, lines)] + [state] * 4,
-            [],
-            [shift_v, incidence_v, state_v],
-            1,
-            flops=flops * (1 + ahead),
-        )
-        if not ahead:
-            bar = more
-            upper, note, total = call(
-                update, [came, lifted, note, settings], [], [state, notes], [state], [state_v], 1
-            )
-    note, sent = call(
+    came = exchange(total.reshape(ndev, ut, LANES)).reshape(-1, LANES)
+    flow, power, lifted, lower, injections = call(
+        second,
+        [shift, bar, load, flow, line, upper, lower, power, note, settings],
+        [shift_far],
+        [(hours, lines)] + [state] * 3 + [(2 * hours, buses)],
+        [],
+        [shift_v, incidence_v, state_v, state_v],
+        1,
+        flops=flops,
+    )
+    upper, note, sent = call(
+        update,
+        [came, lifted, note, settings, injections],
+        [],
+        [state, notes],
+        [(ndev * rows_update, LANES)],
+        [((ndev * rows_update, LANES), f32)],
+        1,
+    )
+    came = exchange(sent.reshape(ndev, rows_update, LANES)).reshape(-1, LANES)
+    flow, power, lifted, lower, grid, injection = call(
+        third,
+        [shift, injections, load, flow, line, upper, lower, power, note, settings],
+        [shift_far],
+        [(hours, lines)] + [state] * 4 + [(hours, buses)],
+        [],
+        [shift_v, incidence_v, state_v],
+        1,
+        flops=2 * flops,
+    )
+    note, sent, early = call(
         last,
-        [came, shift, lifted, lower, power, more, note, settings, load, flow, line],
-        [shift_far],
+        [came, lifted, lower, power, grid, note, settings, load, injection],
+        [],
         [notes],
-        [(ndev, rows_back, LANES)],
-        [shift_v, incidence_v, ((ndev * rows_back, LANES), f32), state_v, state_v],
+        [(ndev * rows_back, LANES), (2 * scen, buses)],
+        [
+            incidence_v, ((ndev * rows_back, LANES), f32), ((2 * scen, buses), f32), state_v,
+            state_v,
+        ],
+        2,
+        flops=flops,
+    )
+    came = exchange(sent.reshape(ndev, rows_back, LANES)).reshape(-1, LANES)
+    own_flow = ((scen * lt, LANES), f32)
+    (flow,) = call(
+        hourly_flow,
+        [line],
+        [early, flow_dual.reshape(scen * lt, LANES), turned],
+        [(scen, lines)],
+        [],
+        [((2 * scen, buses), f32), own_flow, ((buses, lines), bf16)],
         3,
         flops=flops,
     )
-    came = exchange(sent).reshape(-1, LANES)
     hourly = (scen, ut, LANES)
     power, upper, lower, flow, capacity = call(
         finish,
-        [came, note, settings],
-        [],
+        [came, note, settings, line, flow, turned[:, :last_near]],
+        [turned],
         [],
         [hourly, hourly, hourly, (scen, lt, LANES), (1, LANES)],
-        [((ut, LANES), f32), (hourly, f32), ((1, LANES), f32)],
-        5,
+        [
+            ((buses, lines - last_near), bf16), ((ut, LANES), f32), (hourly, f32),
+            ((1, LANES), f32), own_flow,
+        ],
+        6,
     )
     return (
         power.reshape(scen, 1, units),
@@ -552,7 +628,8 @@
     ndev = lax.axis_size("hour")
     buses = rest[4].shape[1]
     fits = (
-        power.shape[0] == ndev
+        ITERS == 4
+        and power.shape[0] == ndev
         and power.shape[1] == 1
         and capacity.shape[0] == LANES
         and flow_dual.shape[2] % (16 * LANES) == 0

time: 90.3 us -> 85.5 us (0.947)
  blocking collectives: 25.2 us -> 0 us
  local copies, waits for them, and re-layouts: 1.44 us -> 9.36 us
  waiting for transfers between devices: 22.8 us -> 28.3 us
  Pallas kernels: 22.2 us -> 25.8 us
  starting transfers between devices: 16.8 us -> 20.4 us
    all_to_all x1 -> x0, blocking collectives: 25.2 us -> none  [exchange(): lax.all_to_all(blocks, 'hour', split_axis=0, concat_axis=0, tiled=True)]
    unnamed x15 -> x16, local copies, waits for them, and re-layouts: 0.04 us -> 6.45 us
    all_to_all x3 -> x4, waiting for transfers between devices: 22.8 us -> 28.3 us  [exchange(): lax.all_to_all(blocks, 'hour', split_axis=0, concat_axis=0, tiled=True)]
    all_to_all x3 -> x4, starting transfers between devices: 16.8 us -> 20.4 us  [exchange(): lax.all_to_all(blocks, 'hour', split_axis=0, concat_axis=0, tiled=True)]
    pallas_call x7 -> x8, Pallas kernels: 22.2 us -> 25.8 us  [call(): pl.pallas_call(body, out_shape=[pltpu.VMEM(s, f32) for s in outs] + [pltp...]
    slice x1 -> x2, local copies, waits for them, and re-layouts: 1.41 us -> 2.92 us  [the longest x1 1.51 us: by_scenarios(): turned[:, :last_near]]
  transfers between devices with their start and end apart: 3 -> 4, of which waited for: 3 -> 4; matrix products, arithmetic and copies ran while one was open for 2% -> 11% of each run, Pallas kernels for 13% -> 17%
where the time goes in v2:
time: 85.5 us; the launch traced here: 84.7 us
  waiting for transfers between devices  28.3 us (33%)
  Pallas kernels  25.8 us (30%)
  starting transfers between devices  20.4 us (24%)
  local copies, waits for them, and re-layouts  9.36 us (11%)
  between operations  0.86 us (1%)
    all_to_all x4, waiting for transfers between devices, exchange(): lax.all_to_all(blocks, 'hour', split_axis=0, concat_axis=0, tiled=True)  28.3 us
    pallas_call x8, Pallas kernels, call(): pl.pallas_call(body, out_shape=[pltpu.VMEM(s, f32) for s in outs] + [pltp...  25.8 us
    all_to_all x4, starting transfers between devices, exchange(): lax.all_to_all(blocks, 'hour', split_axis=0, concat_axis=0, tiled=True)  20.4 us
    unnamed x16, local copies, waits for them, and re-layouts  6.45 us
  transfers between devices with their start and end apart: 4, of which 4 were waited for; matrix products, arithmetic and copies ran while one was open for 11% of the time, Pallas kernels for 17%

profile of v2, /device:TPU:0, one launch (start us, length us, event | category | flops | bytes accessed | tf_op | source)
XLA Modules:
  0.0 84.7 jit_solution(5264922392524452426)
XLA Ops:
  0.6 0.0 copy-start.1
  0.6 0.0 copy-start.2
  0.7 0.0 copy-start.3
  0.7 2.1 %shard_map.173 = f32[16,104,128]{2,1,0:T(8,128)} custom-call(f32[16,16,128]{2,1,0:T(8,128)} %bitcast.48, f32[16,16,128]{2,1,0:T(8,128)} %bitcast.49, f32[16,16,128]{2,1,0:T(8,128)} %bitcast.50, f32[16,32,128]{2,1,0:T(8,128)} %bitcast.43, bf16[16,512]{1,0:T(8,128)(2,1)} %bitcast.51, f32[1,16]{1,0:T(1,128)} %bitcast.52, f32[1,128]{1,0:T(1,128)} %bitcast.53), custom_call_target="tpu_custom_call" | custom-call | bytes 672320 | tf_op jit(solution)/shard_map/pallas_call | solution.py:165
  2.8 7.4 %all-to-all-start = ((f32[16,104,128]{2,1,0:T(8,128)}), f32[16,104,128]{2,1,0:T(8,128)S(1)}, u32[]{:S(2)}, u32[]{:S(2)}) async-start(f32[16,104,128]{2,1,0:T(8,128)} %shard_map.173), calls=%async_computation | async-start | bytes 1703936 | tf_op jit(solution)/shard_map/all_to_all | solution.py:193
  10.2 0.0 copy-start
  10.2 1.4 %slice.6.shift = bf16[1280,512]{1,0:T(8,128)(2,1)S(1)} slice(bf16[4096,512]{1,0:T(8,128)(2,1)} %shift_far.5), slice={[0:1280], [0:512]} | slice | bytes 2621440 | tf_op jit(solution)/shard_map/slice | solution.py:511
  11.7 0.0 copy-done.5
  11.7 18.2 %all-to-all-done = f32[16,104,128]{2,1,0:T(8,128)S(1)} async-done(((f32[16,104,128]{2,1,0:T(8,128)}), f32[16,104,128]{2,1,0:T(8,128)S(1)}, u32[]{:S(2)}, u32[]{:S(2)}) %all-to-all-start) | async-done | bytes 852000 | tf_op jit(solution)/shard_map/all_to_all | solution.py:193
  30.0 3.6 %shard_map.174 = (f32[256,128]{1,0:T(8,128)S(1)}, f32[256,128]{1,0:T(8,128)S(1)}, f32[256,128]{1,0:T(8,128)S(1)}, f32[256,128]{1,0:T(8,128)S(1)}, f32[16,4096]{1...) custom-call(f32[1664,128]{1,0:T(8,128)S(1)} %bitcast.32, ...), custom_call_target="tpu_custom_call" | custom-call | flops 201326592 | bytes 6397952 | tf_op jit(solution)/shard_map/pallas_call | solution.py:165
  33.6 5.8 %all-to-all-start.1 = ((f32[16,16,128]{2,1,0:T(8,128)}), f32[16,16,128]{2,1,0:T(8,128)S(1)}, u32[]{:S(2)}, u32[]{:S(2)}) async-start(f32[16,16,128]{2,1,0:T(8,128)} %bitcast.47), calls=%async_computation.1 | async-start | bytes 262144 | tf_op jit(solution)/shard_map/all_to_all | solution.py:193
  39.4 4.8 %shard_map.175 = (f32[16,4096]{1,0:T(8,128)S(1)}, f32[256,128]{1,0:T(8,128)S(1)}, f32[256,128]{1,0:T(8,128)S(1)}, f32[256,128]{1,0:T(8,128)S(1)}, f32[32,512]{1,0:T(8,128)S(1)}) custom-call(bf16[1280,512]{1,0:T(8,128)(2,1)S(1)} %slice.6.shift, f32[256,128]{1,0:T(8,128)S(1)} %get-tuple-element.35.bar, f32[16,512]{1,0:T(8,128)S(1)} %get-tuple-element.36.load, ...), custom_call_target="tpu_custom_call" | custom-call | flops 201326592 | bytes 6397952 | tf_op jit(solution)/shard_map/pallas_call | solution.py:165
  44.3 3.1 %all-to-all-done.1 = f32[16,16,128]{2,1,0:T(8,128)S(1)} async-done(((f32[16,16,128]{2,1,0:T(8,128)}), f32[16,16,128]{2,1,0:T(8,128)S(1)}, u32[]{:S(2)}, u32[]{:S(2)}) %all-to-all-start.1) | async-done | bytes 131104 | tf_op jit(solution)/shard_map/all_to_all | solution.py:193
  47.3 0.7 shard_map.176
  48.1 3.5 %all-to-all-start.2 = ((f32[16,24,128]{2,1,0:T(8,128)}), f32[16,24,128]{2,1,0:T(8,128)S(1)}, u32[]{:S(2)}, u32[]{:S(2)}) async-start(f32[16,24,128]{2,1,0:T(8,128)} %bitcast.46), calls=%async_computation.2 | async-start | bytes 393216 | tf_op jit(solution)/shard_map/all_to_all | solution.py:193
  51.6 6.4 %shard_map.177 = (f32[16,4096]{1,0:T(8,128)}, f32[256,128]{1,0:T(8,128)S(1)}, f32[256,128]{1,0:T(8,128)S(1)}, f32[256,128]{1,0:T(8,128)S(1)}, f32[256,128]{1,0:T(8,128)S(1)}, /*index=5*/f32[16,512]{1,0:T(8,128)S(1)}) custom-call(bf16[1280,512]{1,0:T(8,128)(2,1)S(1)} %slice.6.shift, f32[32,512]{1,0:T(8,128)S(1)} %get-tuple-element.43.sent, ...), custom_call_target="tpu_custom_call" | custom-call | flops 402653184 | bytes 6332416 | tf_op jit(solution)/shard_map/pallas_call | solution.py:165
  58.0 2.6 %all-to-all-done.2 = f32[16,24,128]{2,1,0:T(8,128)S(1)} async-done(((f32[16,24,128]{2,1,0:T(8,128)}), f32[16,24,128]{2,1,0:T(8,128)S(1)}, u32[]{:S(2)}, u32[]{:S(2)}) %all-to-all-start.2) | async-done | bytes 196640 | tf_op jit(solution)/shard_map/all_to_all | solution.py:193
  60.6 1.7 %shard_map.178 = (f32[32,128]{1,0:T(8,128)S(1)}, f32[1152,128]{1,0:T(8,128)}, f32[32,512]{1,0:T(8,128)}) custom-call(f32[384,128]{1,0:T(8,128)S(1)} %bitcast.34, f32[256,128]{1,0:T(8,128)S(1)} %get-tuple-element.50.lifted, f32[256,128]{1,0:T(8,128)S(1)} %get-tuple-element.51.lower, f32[256,128]{1,0:T(8,128)S(1)} %get-tuple-element.52.power, ...), custom_call_target="tpu_custom_call" | custom-call | flops 201326592 | bytes 843776 | tf_op jit(solution)/shard_map/pallas_call | solution.py:165
  62.3 3.6 %all-to-all-start.3 = ((f32[16,72,128]{2,1,0:T(8,128)}), f32[16,72,128]{2,1,0:T(8,128)S(1)}, u32[]{:S(2)}, u32[]{:S(2)}) async-start(f32[16,72,128]{2,1,0:T(8,128)} %bitcast.45), calls=%async_computation.3 | async-start | bytes 1179648 | tf_op jit(solution)/shard_map/all_to_all | solution.py:193
  65.9 6.4 %copy.19 = bf16[4096,512]{0,1:T(8,128)(2,1)} copy(bf16[4096,512]{1,0:T(8,128)(2,1)} %shift_far.5) | data formatting | bytes 8388608 | tf_op args[7]
  72.3 1.5 %slice.8.turned = bf16[512,1536]{1,0:T(8,128)(2,1)S(1)} slice(bf16[512,4096]{1,0:T(8,128)(2,1)} %bitcast.40), slice={[0:512], [0:1536]} | slice | bytes 3145728 | tf_op jit(solution)/shard_map/slice | solution.py:608
  73.8 3.2 %shard_map.179.flow = f32[16,4096]{1,0:T(8,128)S(1)} custom-call(f32[1,4096]{1,0:T(1,128)S(1)} %bitcast.38, f32[32,512]{1,0:T(8,128)} %get-tuple-element.57.early, f32[512,128]{1,0:T(8,128)} %bitcast.44, bf16[512,4096]{1,0:T(8,128)(2,1)} %bitcast.41), custom_call_target="tpu_custom_call" | custom-call | flops 201326592 | bytes 4538368 | tf_op jit(solution)/shard_map/pallas_call | solution.py:165
  77.0 4.4 %all-to-all-done.3 = f32[16,72,128]{2,1,0:T(8,128)S(1)} async-done(((f32[16,72,128]{2,1,0:T(8,128)}), f32[16,72,128]{2,1,0:T(8,128)S(1)}, u32[]{:S(2)}, u32[]{:S(2)}) %all-to-all-start.3) | async-done | bytes 589856 | tf_op jit(solution)/shard_map/all_to_all | solution.py:193
  81.4 3.3 %shard_map.180 = (f32[16,16,128]{2,1,0:T(8,128)}, f32[16,16,128]{2,1,0:T(8,128)}, f32[16,16,128]{2,1,0:T(8,128)}, f32[16,32,128]{2,1,0:T(8,128)}, f32[1,128]{1,0:T(1,128)}) custom-call(f32[1152,128]{1,0:T(8,128)S(1)} %bitcast.33, f32[32,128]{1,0:T(8,128)S(1)} %get-tuple-element.56.notes, f32[80,128]{1,0:T(8,128)S(1)} %constant_dynamic-update-slice_fusion.settings, ...), custom_call_target="tpu_custom_call" | custom-call | bytes 6692864 | tf_op jit(solution)/shard_map/pallas_call | solution.py:165
  (12 shorter events, 0.0 us)
Async XLA Ops:
  0.6 11.0 %copy-start.1 = (f32[2048]{0:T(1024)S(1)}, f32[2048]{0:T(1024)}, u32[]{:S(2)}) copy-start(f32[2048]{0:T(1024)} %param.24) | copy-start | bytes 24580
  0.6 11.0 %copy-start.2 = (f32[2048]{0:T(1024)S(1)}, f32[2048]{0:T(1024)}, u32[]{:S(2)}) copy-start(f32[2048]{0:T(1024)} %param.25) | copy-start | bytes 24580
  0.7 11.0 %copy-start.3 = (f32[2048]{0:T(1024)S(1)}, f32[2048]{0:T(1024)}, u32[]{:S(2)}) copy-start(f32[2048]{0:T(1024)} %param.26) | copy-start | bytes 24580
  0.7 11.0 %copy-start.4 = (f32[2048]{0:T(1024)S(1)}, f32[2048]{0:T(1024)}, u32[]{:S(2)}) copy-start(f32[2048]{0:T(1024)} %param.27) | copy-start | bytes 24580
  0.7 11.0 %copy-start.5 = (s32[2048]{0:T(1024)S(1)}, s32[2048]{0:T(1024)}, u32[]{:S(2)}) copy-start(s32[2048]{0:T(1024)} %param.23) | copy-start | bytes 24580
  2.8 27.2 %all-to-all-start = ((f32[16,104,128]{2,1,0:T(8,128)}), f32[16,104,128]{2,1,0:T(8,128)S(1)}, u32[]{:S(2)}, u32[]{:S(2)}) async-start(f32[16,104,128]{2,1,0:T(8,128)} %shard_map.173), calls=%async_computation | async-start | bytes 1703936 | tf_op jit(solution)/shard_map/all_to_all | solution.py:193
  10.2 29.2 %copy-start = (f32[4096]{0:T(1024)S(1)}, f32[4096]{0:T(1024)}, u32[]{:S(2)}) copy-start(f32[4096]{0:T(1024)} %param.22) | copy-start | bytes 49156
  33.6 13.8 %all-to-all-start.1 = ((f32[16,16,128]{2,1,0:T(8,128)}), f32[16,16,128]{2,1,0:T(8,128)S(1)}, u32[]{:S(2)}, u32[]{:S(2)}) async-start(f32[16,16,128]{2,1,0:T(8,128)} %bitcast.47), calls=%async_computation.1 | async-start | bytes 262144 | tf_op jit(solution)/shard_map/all_to_all | solution.py:193
  48.1 12.5 %all-to-all-start.2 = ((f32[16,24,128]{2,1,0:T(8,128)}), f32[16,24,128]{2,1,0:T(8,128)S(1)}, u32[]{:S(2)}, u32[]{:S(2)}) async-start(f32[16,24,128]{2,1,0:T(8,128)} %bitcast.46), calls=%async_computation.2 | async-start | bytes 393216 | tf_op jit(solution)/shard_map/all_to_all | solution.py:193
  62.3 19.1 %all-to-all-start.3 = ((f32[16,72,128]{2,1,0:T(8,128)}), f32[16,72,128]{2,1,0:T(8,128)S(1)}, u32[]{:S(2)}, u32[]{:S(2)}) async-start(f32[16,72,128]{2,1,0:T(8,128)} %bitcast.45), calls=%async_computation.3 | async-start | bytes 1179648 | tf_op jit(solution)/shard_map/all_to_all | solution.py:193

commit v3 on v2

--- a/solution.py
+++ b/solution.py
@@ -13,7 +13,8 @@
 LANES = 128
 SUBLANES = 8
 NEAR = 5
-LAST_NEAR = 6
+LAST_NEAR = 8
+FAR_PARTS = 2
 
 
 def compose(earlier, later):
@@ -144,9 +145,7 @@
     lines, buses = shift_factors.shape
     ut, lt, bt = units // LANES, lines // LANES, buses // LANES
     near_lines = lines * NEAR // 16
-    parts = (pl.ds(0, near_lines), pl.ds(near_lines, lines - near_lines))
     last_near = lines * LAST_NEAR // 16
-    last_parts = (pl.ds(0, last_near), pl.ds(last_near, lines - last_near))
     small = -(-(bt + 2) // SUBLANES) * SUBLANES
     at_power, at_upper, at_lower, at_flow = 0, ut, 2 * ut, 3 * ut
     at_total = at_flow + lt
@@ -207,6 +206,24 @@
     def part(ref, index):
         return ref[pl.ds(index * ut, ut), :]
 
+    def bring_lines(copies, near, far, far_v, axis):
+        here = near.shape[axis]
+        size = (lines - here) // FAR_PARTS
+        result = [(pl.ds(0, here), near, lambda: None)]
+        for c in range(FAR_PARTS):
+            source, target = pl.ds(here + c * size, size), pl.ds(c * size, size)
+            if axis == 1:
+                copy = copies.bring(far.at[:, source], far_v.at[:, target])
+                part_v = far_v.at[:, target]
+            else:
+                copy = copies.bring(far.at[source], far_v.at[target])
+                part_v = far_v.at[target]
+            result.append((source, part_v, copy.wait))
+        return result
+
+    def arrived(factors):
+        return [(at, part_v, lambda: None) for at, part_v, _ in factors]
+
     def one_hot(settings, incidence):
         buses_of = lax.broadcasted_iota(jnp.int32, (buses, LANES), 0).astype(f32)
         for j in range(ut):
@@ -226,13 +243,12 @@
         wide_bar = wide(bar, 0, ut, ut).astype(bf16)
         return (across(wide_bar, incidence[...]) - load[...]).astype(bf16)
 
-    def to_buses(flow, shifts, wait):
+    def to_buses(flow, shift):
         total = jnp.zeros((hours, buses), f32)
-        for at, shift, arrived in zip(parts, shifts, (None, wait)):
-            if arrived:
-                arrived()
+        for at, factors, wait in shift:
+            wait()
             total = total + jnp.dot(
-                flow[:, at].astype(bf16), shift[...], preferred_element_type=f32
+                flow[:, at].astype(bf16), factors[...], preferred_element_type=f32
             )
         return total
 
@@ -240,13 +256,17 @@
         bound = dual_step * limit[:, at]
         return probe - jnp.clip(probe, -bound, bound)
 
-    def network(injection, flow, shifts, limit, incidence, new_flow, grid, wait):
-        for at, shift, arrived in zip(parts, shifts, (None, wait)):
-            if arrived:
-                arrived()
-            probe = flow[:, at] + dual_step * across(injection, shift[...])
-            new_flow[:, at] = held_back(probe, limit, at)
-        to_units(to_buses(new_flow, shifts, None), incidence, grid)
+    def network(injection, flow, shift, limit, incidence, new_flow, grid, turned=None):
+        if turned is None:
+            for at, factors, wait in shift:
+                wait()
+                probe = flow[:, at] + dual_step * across(injection, factors[...])
+                new_flow[:, at] = held_back(probe, limit, at)
+        else:
+            flows = jnp.dot(injection, turned[...], preferred_element_type=f32)
+            every = pl.ds(0, lines)
+            new_flow[...] = held_back(flow[...] + dual_step * flows, limit, every)
+        to_units(to_buses(new_flow, arrived(shift)), incidence, grid)
 
     def local(upper, lower, before, grid, price, settings, put_power, bar, put):
         keep, bound = part(settings, 0), part(settings, 2)
@@ -314,20 +334,23 @@
         )
         spread(blocks_v, at_price, rows_in, jnp.broadcast_to(own_price, (ndev, LANES)))
         spread(blocks_v, at_capacity, rows_in, jnp.broadcast_to(capacity_v[...], (ndev, LANES)))
-        big[0].wait()
+        for copy in big:
+            copy.wait()
+        at = pl.ds(0, at_total)
+        copies.send(blocks.at[:, at], out.at[:, at])
         total = sum_blocks(blocks_v, at_upper, rows_in)
         for peer in range(ndev):
             blocks_v[pl.ds(peer * rows_in + at_total, ut), :] = total
-        for copy in big[1:]:
-            copy.wait()
-        copies.send(blocks, out)
+        at = pl.ds(at_total, rows_in - at_total)
+        copies.send(blocks.at[:, at], out.at[:, at])
         copies.close()
 
-    def first(came, shift, settings, shift_far, *rest):
+    def first(came, shift, settings, shift_far, turned, *rest):
+        del turned
         power, upper, lower, bar, flow, load, notes, total_o = rest[:8]
         shift_v, incidence, out, grid, semaphores = rest[8:]
         copies = Copies(semaphores)
-        rest_of_shift = copies.bring(shift_far.at[parts[1]], shift_v)
+        factors = bring_lines(copies, shift, shift_far, shift_v, 0)
         flow[...] = wide(came, at_flow, lt, rows_in)
         load[...] = wide(came, at_load, bt, rows_in)
         notes[pl.ds(ut, hours), :] = rows(came, at_price, rows_in)
@@ -336,7 +359,7 @@
             rows(came, at_capacity, rows_in), settings, sum_blocks(came, at_total, rows_in)
         )
         notes[pl.ds(0, ut), :] = capacity
-        to_units(to_buses(flow, (shift, shift_v), rest_of_shift.wait), incidence, grid)
+        to_units(to_buses(flow, factors), incidence, grid)
         total = [jnp.zeros((ut, LANES), f32)]
 
         def put(hour, lifted, low):
@@ -361,13 +384,11 @@
         shift, bar, load, flow, line, upper, lower, power, notes, settings, shift_far,
         new_flow, new_power, lifted, low, sent, shift_v, incidence, grid, new_bar, semaphores,
     ):
-        rest_of_shift = Copies(semaphores).bring(shift_far.at[parts[1]], shift_v)
+        factors = bring_lines(Copies(semaphores), shift, shift_far, shift_v, 0)
         one_hot(settings, incidence)
         injection = inject(bar, load, incidence)
         sent[pl.ds(0, hours), :] = injection.astype(f32)
-        network(
-            injection, flow, (shift, shift_v), line, incidence, new_flow, grid, rest_of_shift.wait
-        )
+        network(injection, flow, factors, line, incidence, new_flow, grid)
         local(
             reader(upper), reader(lower), reader(power), grid,
             lambda hour: notes[pl.ds(ut + hour, 1), :], settings, writer(new_power), new_bar,
@@ -376,14 +397,16 @@
         sent[pl.ds(hours, hours), :] = inject(new_bar, load, incidence).astype(f32)
 
     def third(
-        shift, sent, load, flow, line, upper, lower, power, notes, settings, shift_far,
-        new_flow, new_power, lifted, low, grid, later, shift_v, incidence, new_bar, semaphores,
+        shift, sent, load, flow, line, upper, lower, power, notes, settings, shift_far, turned,
+        new_flow, new_power, lifted, low, grid, later,
+        shift_v, turned_v, incidence, new_bar, semaphores,
     ):
-        rest_of_shift = Copies(semaphores).bring(shift_far.at[parts[1]], shift_v)
+        copies = Copies(semaphores)
+        factors = bring_lines(copies, shift, shift_far, shift_v, 0)
+        turned_factors = copies.bring(turned, turned_v)
         one_hot(settings, incidence)
-        shifts = (shift, shift_v)
         injection = sent[pl.ds(hours, hours), :].astype(bf16)
-        network(injection, flow, shifts, line, incidence, new_flow, grid, rest_of_shift.wait)
+        network(injection, flow, factors, line, incidence, new_flow, grid)
         local(
             reader(upper), reader(lower), reader(power), grid,
             lambda hour: notes[pl.ds(ut + hour, 1), :], settings, writer(new_power), new_bar,
@@ -391,7 +414,10 @@
         )
         injection = inject(new_bar, load, incidence)
         later[...] = injection.astype(f32)
-        network(injection, new_flow, shifts, line, incidence, new_flow, grid, None)
+        turned_factors.wait()
+        network(
+            injection, new_flow, arrived(factors), line, incidence, new_flow, grid, turned_v
+        )
 
     def lift(lifted, low):
         def put(hour, new_lifted, new_low):
@@ -444,13 +470,17 @@
             reader(upper), reader(lower), reader(power), grid,
             lambda hour: notes[pl.ds(ut + hour, 1), :], settings, put_power, bar, put,
         )
+        blocks = out.reshape(ndev, rows_back, LANES)
+        at = pl.ds(0, back_bus)
+        copies.send(blocks.at[:, at], out_o.at[:, at])
         one_hot(settings, incidence)
         spread(out, back_bus, rows_back, later[...])
         spread(out, back_bus + bt, rows_back, inject(bar, load, incidence).astype(f32))
-        copies.send(out, out_o)
+        at = pl.ds(back_bus, rows_back - back_bus)
+        copies.send(blocks.at[:, at], out_o.at[:, at])
         copies.close()
 
-    def hourly_flow(line, early, flow, turned, new_flow, early_v, flow_v, turned_v, semaphores):
+    def hourly_flow(line, early, flow, turned, new_o, early_v, flow_v, turned_v, new, semaphores):
         copies = Copies(semaphores)
         come = [copies.bring(*pair) for pair in ((early, early_v), (flow, flow_v), (turned, turned_v))]
         for copy in come:
@@ -461,18 +491,35 @@
         for step in range(2):
             flow_step = flows[step * scen : (step + 1) * scen]
             value = held_back(value + dual_step * flow_step, line, every)
-        new_flow[...] = value
+        new[...] = value
+        copies.send(new, new_o)
+        copies.close()
 
     def finish(
-        came, notes, settings, line, flow, turned, turned_far,
+        came, notes, settings, line, turned, flow, turned_far,
         power_o, upper_o, lower_o, flow_o, capacity_o,
-        turned_v, notes_v, upper, own, out, semaphores,
+        turned_v, flow_v, notes_v, upper, own, out, semaphores,
     ):
         copies = Copies(semaphores)
-        rest_of_turned = copies.bring(turned_far.at[:, last_parts[1]], turned_v)
+        flow_came = copies.bring(flow, flow_v)
+        factors = bring_lines(copies, turned, turned_far, turned_v, 1)
         blocks = came.reshape(ndev, rows_back, LANES)
         copies.send(blocks.at[:, pl.ds(0, ut)], power_o)
         copies.send(blocks.at[:, pl.ds(2 * ut, ut)], lower_o)
+        injections = jnp.concatenate(
+            [wide(came, back_bus + step * bt, bt, rows_back) for step in range(2)], axis=0
+        ).astype(bf16)
+        flow_came.wait()
+        row = 0
+        for at, part_v, wait in factors:
+            wait()
+            flows = dual_step * jnp.dot(injections, part_v[...], preferred_element_type=f32)
+            value = flow_v[:, at]
+            for step in range(2):
+                value = held_back(value + flows[step * scen : (step + 1) * scen], line, at)
+            spread(out, row, lt, value)
+            row += value.shape[1] // LANES
+        copies.send(out.reshape(scen, lt, LANES), flow_o)
         total = sum_blocks(came, back_total, rows_back)
         capacity, pull = capacities(part(notes, 0), settings, total)
         for peer in range(ndev):
@@ -481,20 +528,6 @@
         notes_v[...] = capacity
         own[...] = notes_v[pl.ds(lax.axis_index("hour"), 1), :]
         copies.send(own, capacity_o)
-        injections = jnp.concatenate(
-            [wide(came, back_bus + step * bt, bt, rows_back) for step in range(2)], axis=0
-        ).astype(bf16)
-        row = 0
-        for at, factors, arrived in zip(last_parts, (turned, turned_v), (None, rest_of_turned.wait)):
-            if arrived:
-                arrived()
-            flows = dual_step * jnp.dot(injections, factors[...], preferred_element_type=f32)
-            value = flow[:, at]
-            for step in range(2):
-                value = held_back(value + flows[step * scen : (step + 1) * scen], line, at)
-            spread(out, row, lt, value)
-            row += value.shape[1] // LANES
-        copies.send(out.reshape(scen, lt, LANES), flow_o)
         copies.close()
 
 
@@ -533,17 +566,17 @@
             ((scen, buses), bf16), ((1, scen), f32), ((1, LANES), f32),
             ((ndev * rows_in, LANES), f32),
         ],
-        8,
+        9,
     )
     came = exchange(sent).reshape(-1, LANES)
     power, upper, lower, bar, flow, load, note, total = call(
         first,
         [came, shift, settings],
-        [shift_far],
+        [shift_far, turned],
         [state] * 4 + [(hours, lines), (hours, buses), notes],
         [state],
         [shift_v, incidence_v, state_v, state_v],
-        2,
+        1 + FAR_PARTS,
         flops=flops,
     )
     came = exchange(total.reshape(ndev, ut, LANES)).reshape(-1, LANES)
@@ -554,7 +587,7 @@
         [(hours, lines)] + [state] * 3 + [(2 * hours, buses)],
         [],
         [shift_v, incidence_v, state_v, state_v],
-        1,
+        FAR_PARTS,
         flops=flops,
     )
     upper, note, sent = call(
@@ -570,11 +603,11 @@
     flow, power, lifted, lower, grid, injection = call(
         third,
         [shift, injections, load, flow, line, upper, lower, power, note, settings],
-        [shift_far],
+        [shift_far, turned],
         [(hours, lines)] + [state] * 4 + [(hours, buses)],
         [],
-        [shift_v, incidence_v, state_v],
-        1,
+        [shift_v, ((buses, lines), bf16), incidence_v, state_v],
+        FAR_PARTS + 1,
         flops=2 * flops,
     )
     note, sent, early = call(
@@ -582,38 +615,38 @@
         [came, lifted, lower, power, grid, note, settings, load, injection],
         [],
         [notes],
-        [(ndev * rows_back, LANES), (2 * scen, buses)],
+        [(ndev, rows_back, LANES), (2 * scen, buses)],
         [
             incidence_v, ((ndev * rows_back, LANES), f32), ((2 * scen, buses), f32), state_v,
             state_v,
         ],
-        2,
+        3,
         flops=flops,
     )
-    came = exchange(sent.reshape(ndev, rows_back, LANES)).reshape(-1, LANES)
+    came = exchange(sent).reshape(-1, LANES)
     own_flow = ((scen * lt, LANES), f32)
     (flow,) = call(
         hourly_flow,
         [line],
         [early, flow_dual.reshape(scen * lt, LANES), turned],
+        [],
         [(scen, lines)],
-        [],
-        [((2 * scen, buses), f32), own_flow, ((buses, lines), bf16)],
-        3,
+        [((2 * scen, buses), f32), own_flow, ((buses, lines), bf16), ((scen, lines), f32)],
+        4,
         flops=flops,
     )
     hourly = (scen, ut, LANES)
     power, upper, lower, flow, capacity = call(
         finish,
-        [came, note, settings, line, flow, turned[:, :last_near]],
-        [turned],
+        [came, note, settings, line, turned[:, :last_near]],
+        [flow, turned],
         [],
         [hourly, hourly, hourly, (scen, lt, LANES), (1, LANES)],
         [
-            ((buses, lines - last_near), bf16), ((ut, LANES), f32), (hourly, f32),
-            ((1, LANES), f32), own_flow,
+            ((buses, lines - last_near), bf16), ((scen, lines), f32), ((ut, LANES), f32),
+            (hourly, f32), ((1, LANES), f32), own_flow,
         ],
-        6,
+        6 + FAR_PARTS,
     )
     return (
         power.reshape(scen, 1, units),
@@ -632,7 +665,7 @@
         and power.shape[0] == ndev
         and power.shape[1] == 1
         and capacity.shape[0] == LANES
-        and flow_dual.shape[2] % (16 * LANES) == 0
+        and flow_dual.shape[2] % (16 * FAR_PARTS * LANES) == 0
         and ndev % (2 * SUBLANES) == 0
         and all(size % (SUBLANES * LANES) == 0 for size in (power.shape[2], flow_dual.shape[2]))
         and buses % LANES == 0

time: 85.5 us -> 84.7 us (level)
  Pallas kernels: 25.8 us -> 24 us
    pallas_call x8, Pallas kernels: 25.8 us -> 24 us  [call(): pl.pallas_call(body, out_shape=[pltpu.VMEM(s, f32) for s in outs] + [pltp...]
  transfers between devices with their start and end apart: 4 -> 4, of which waited for: 4 -> 4; matrix products, arithmetic and copies ran while one was open for 11% -> 11% of each run, Pallas kernels for 17% -> 16%
where the time goes in v3:
time: 84.7 us; the launch traced here: 83.9 us
  waiting for transfers between devices  29.1 us (34%)
  Pallas kernels  24 us (28%)
  starting transfers between devices  20.4 us (24%)
  local copies, waits for them, and re-layouts  9.59 us (11%)
    all_to_all x4, waiting for transfers between devices, exchange(): lax.all_to_all(blocks, 'hour', split_axis=0, concat_axis=0, tiled=True)  29.1 us
    pallas_call x8, Pallas kernels, call(): pl.pallas_call(body, out_shape=[pltpu.VMEM(s, f32) for s in outs] + [pltp...  24 us
    all_to_all x4, starting transfers between devices, exchange(): lax.all_to_all(blocks, 'hour', split_axis=0, concat_axis=0, tiled=True)  20.4 us
    unnamed x16, local copies, waits for them, and re-layouts  6.46 us
    slice x1, local copies, waits for them, and re-layouts, by_scenarios(): turned[:, :last_near]  1.73 us
  transfers between devices with their start and end apart: 4, of which 4 were waited for; matrix products, arithmetic and copies ran while one was open for 11% of the time, Pallas kernels for 16%

profile of v3, /device:TPU:0, one launch (start us, length us, event | category | flops | bytes accessed | tf_op | source)
XLA Modules:
  0.0 83.9 jit_solution(14732170585045504791)
XLA Ops:
  0.6 2.1 %shard_map.173 = f32[16,104,128]{2,1,0:T(8,128)} custom-call(f32[16,16,128]{2,1,0:T(8,128)} %bitcast.48, f32[16,16,128]{2,1,0:T(8,128)} %bitcast.49, f32[16,16,128]{2,1,0:T(8,128)} %bitcast.50, f32[16,32,128]{2,1,0:T(8,128)} %bitcast.44, bf16[16,512]{1,0:T(8,128)(2,1)} %bitcast.51, f32[1,16]{1,0:T(1,128)} %bitcast.52, f32[1,128]{1,0:T(1,128)} %bitcast.53), custom_call_target="tpu_custom_call" | custom-call | bytes 672320 | tf_op jit(solution)/shard_map/pallas_call | solution.py:164
  2.8 7.4 %all-to-all-start = ((f32[16,104,128]{2,1,0:T(8,128)}), f32[16,104,128]{2,1,0:T(8,128)S(1)}, u32[]{:S(2)}, u32[]{:S(2)}) async-start(f32[16,104,128]{2,1,0:T(8,128)} %shard_map.173), calls=%async_computation | async-start | bytes 1703936 | tf_op jit(solution)/shard_map/all_to_all | solution.py:192
  10.2 1.4 %slice.6.shift = bf16[1280,512]{1,0:T(8,128)(2,1)S(1)} slice(bf16[4096,512]{1,0:T(8,128)(2,1)} %shift_far.5), slice={[0:1280], [0:512]} | slice | bytes 2621440 | tf_op jit(solution)/shard_map/slice | solution.py:544
  11.6 0.0 copy-start.1
  11.6 0.0 copy-start.2
  11.6 0.0 copy-start.3
  11.6 0.0 copy-start.4
  11.6 0.0 copy-start.5
  11.6 6.4 %copy.19 = bf16[4096,512]{0,1:T(8,128)(2,1)} copy(bf16[4096,512]{1,0:T(8,128)(2,1)} %shift_far.5) | data formatting | bytes 8388608 | tf_op args[7]
  18.1 11.8 %all-to-all-done = f32[16,104,128]{2,1,0:T(8,128)S(1)} async-done(((f32[16,104,128]{2,1,0:T(8,128)}), f32[16,104,128]{2,1,0:T(8,128)S(1)}, u32[]{:S(2)}, u32[]{:S(2)}) %all-to-all-start) | async-done | bytes 852000 | tf_op jit(solution)/shard_map/all_to_all | solution.py:192
  29.9 3.2 %shard_map.174 = (f32[256,128]{1,0:T(8,128)S(1)}, f32[256,128]{1,0:T(8,128)S(1)}, f32[256,128]{1,0:T(8,128)S(1)}, f32[256,128]{1,0:T(8,128)S(1)}, f32[16,4096]{1...) custom-call(f32[1664,128]{1,0:T(8,128)S(1)} %bitcast.31, ...), custom_call_target="tpu_custom_call" | custom-call | flops 201326592 | bytes 10592256 | tf_op jit(solution)/shard_map/pallas_call | solution.py:164
  33.2 5.8 %all-to-all-start.1 = ((f32[16,16,128]{2,1,0:T(8,128)}), f32[16,16,128]{2,1,0:T(8,128)S(1)}, u32[]{:S(2)}, u32[]{:S(2)}) async-start(f32[16,16,128]{2,1,0:T(8,128)} %bitcast.47), calls=%async_computation.1 | async-start | bytes 262144 | tf_op jit(solution)/shard_map/all_to_all | solution.py:192
  39.0 3.9 %shard_map.175 = (f32[16,4096]{1,0:T(8,128)S(1)}, f32[256,128]{1,0:T(8,128)S(1)}, f32[256,128]{1,0:T(8,128)S(1)}, f32[256,128]{1,0:T(8,128)S(1)}, f32[32,512]{1,0:T(8,128)S(1)}) custom-call(bf16[1280,512]{1,0:T(8,128)(2,1)S(1)} %slice.6.shift, f32[256,128]{1,0:T(8,128)S(1)} %get-tuple-element.35.bar, f32[16,512]{1,0:T(8,128)S(1)} %get-tuple-element.36.load, ...), custom_call_target="tpu_custom_call" | custom-call | flops 201326592 | bytes 6397952 | tf_op jit(solution)/shard_map/pallas_call | solution.py:164
  42.9 4.0 %all-to-all-done.1 = f32[16,16,128]{2,1,0:T(8,128)S(1)} async-done(((f32[16,16,128]{2,1,0:T(8,128)}), f32[16,16,128]{2,1,0:T(8,128)S(1)}, u32[]{:S(2)}, u32[]{:S(2)}) %all-to-all-start.1) | async-done | bytes 131104 | tf_op jit(solution)/shard_map/all_to_all | solution.py:192
  46.9 0.7 shard_map.176
  47.7 3.5 %all-to-all-start.2 = ((f32[16,24,128]{2,1,0:T(8,128)}), f32[16,24,128]{2,1,0:T(8,128)S(1)}, u32[]{:S(2)}, u32[]{:S(2)}) async-start(f32[16,24,128]{2,1,0:T(8,128)} %bitcast.46), calls=%async_computation.2 | async-start | bytes 393216 | tf_op jit(solution)/shard_map/all_to_all | solution.py:192
  51.2 5.6 %shard_map.177 = (f32[16,4096]{1,0:T(8,128)}, f32[256,128]{1,0:T(8,128)S(1)}, f32[256,128]{1,0:T(8,128)S(1)}, f32[256,128]{1,0:T(8,128)S(1)}, f32[256,128]{1,0:T(8,128)S(1)}, /*index=5*/f32[16,512]{1,0:T(8,128)S(1)}) custom-call(bf16[1280,512]{1,0:T(8,128)(2,1)S(1)} %slice.6.shift, f32[32,512]{1,0:T(8,128)S(1)} %get-tuple-element.43.sent, ...), custom_call_target="tpu_custom_call" | custom-call | flops 402653184 | bytes 10526720 | tf_op jit(solution)/shard_map/pallas_call | solution.py:164
  56.8 3.4 %all-to-all-done.2 = f32[16,24,128]{2,1,0:T(8,128)S(1)} async-done(((f32[16,24,128]{2,1,0:T(8,128)}), f32[16,24,128]{2,1,0:T(8,128)S(1)}, u32[]{:S(2)}, u32[]{:S(2)}) %all-to-all-start.2) | async-done | bytes 196640 | tf_op jit(solution)/shard_map/all_to_all | solution.py:192
  60.2 1.6 %shard_map.178 = (f32[32,128]{1,0:T(8,128)S(1)}, f32[16,72,128]{2,1,0:T(8,128)}, f32[32,512]{1,0:T(8,128)}) custom-call(f32[384,128]{1,0:T(8,128)S(1)} %bitcast.33, f32[256,128]{1,0:T(8,128)S(1)} %get-tuple-element.50.lifted, f32[256,128]{1,0:T(8,128)S(1)} %get-tuple-element.51.lower, f32[256,128]{1,0:T(8,128)S(1)} %get-tuple-element.52.power, ...), custom_call_target="tpu_custom_call" | custom-call | flops 201326592 | bytes 843776 | tf_op jit(solution)/shard_map/pallas_call | solution.py:164
  61.8 3.6 %all-to-all-start.3 = ((f32[16,72,128]{2,1,0:T(8,128)}), f32[16,72,128]{2,1,0:T(8,128)S(1)}, u32[]{:S(2)}, u32[]{:S(2)}) async-start(f32[16,72,128]{2,1,0:T(8,128)} %get-tuple-element.55), calls=%async_computation.3 | async-start | bytes 1179648 | tf_op jit(solution)/shard_map/all_to_all | solution.py:192
  65.4 1.7 %slice.8.turned = bf16[512,2048]{1,0:T(8,128)(2,1)S(1)} slice(bf16[512,4096]{1,0:T(8,128)(2,1)} %bitcast.41), slice={[0:512], [0:2048]} | slice | bytes 4194304 | tf_op jit(solution)/shard_map/slice | solution.py:641
  67.1 3.9 %shard_map.179.flow = f32[16,4096]{1,0:T(8,128)} custom-call(f32[1,4096]{1,0:T(1,128)S(1)} %bitcast.37, f32[32,512]{1,0:T(8,128)} %get-tuple-element.57.early, f32[512,128]{1,0:T(8,128)} %bitcast.45, bf16[512,4096]{1,0:T(8,128)(2,1)} %bitcast.42), custom_call_target="tpu_custom_call" | custom-call | flops 201326592 | bytes 4538368 | tf_op jit(solution)/shard_map/pallas_call | solution.py:164
  71.0 9.9 %all-to-all-done.3 = f32[16,72,128]{2,1,0:T(8,128)S(1)} async-done(((f32[16,72,128]{2,1,0:T(8,128)}), f32[16,72,128]{2,1,0:T(8,128)S(1)}, u32[]{:S(2)}, u32[]{:S(2)}) %all-to-all-start.3) | async-done | bytes 589856 | tf_op jit(solution)/shard_map/all_to_all | solution.py:192
  80.9 3.0 %shard_map.180 = (f32[16,16,128]{2,1,0:T(8,128)}, f32[16,16,128]{2,1,0:T(8,128)}, f32[16,16,128]{2,1,0:T(8,128)}, f32[16,32,128]{2,1,0:T(8,128)}, f32[1,128]{1,0:T(1,128)}) custom-call(f32[1152,128]{1,0:T(8,128)S(1)} %bitcast.32, f32[32,128]{1,0:T(8,128)S(1)} %get-tuple-element.56.notes, f32[80,128]{1,0:T(8,128)S(1)} %constant_dynamic-update-slice_fusion.settings, ...), custom_call_target="tpu_custom_call" | custom-call | bytes 7217152 | tf_op jit(solution)/shard_map/pallas_call | solution.py:164
  (12 shorter events, 0.0 us)
Async XLA Ops:
  2.8 27.2 %all-to-all-start = ((f32[16,104,128]{2,1,0:T(8,128)}), f32[16,104,128]{2,1,0:T(8,128)S(1)}, u32[]{:S(2)}, u32[]{:S(2)}) async-start(f32[16,104,128]{2,1,0:T(8,128)} %shard_map.173), calls=%async_computation | async-start | bytes 1703936 | tf_op jit(solution)/shard_map/all_to_all | solution.py:192
  11.6 6.5 %copy-start.1 = (f32[2048]{0:T(1024)S(1)}, f32[2048]{0:T(1024)}, u32[]{:S(2)}) copy-start(f32[2048]{0:T(1024)} %param.24) | copy-start | bytes 24580
  11.6 6.5 %copy-start.2 = (f32[2048]{0:T(1024)S(1)}, f32[2048]{0:T(1024)}, u32[]{:S(2)}) copy-start(f32[2048]{0:T(1024)} %param.25) | copy-start | bytes 24580
  11.6 6.5 %copy-start.3 = (f32[2048]{0:T(1024)S(1)}, f32[2048]{0:T(1024)}, u32[]{:S(2)}) copy-start(f32[2048]{0:T(1024)} %param.26) | copy-start | bytes 24580
  11.6 6.5 %copy-start.4 = (f32[2048]{0:T(1024)S(1)}, f32[2048]{0:T(1024)}, u32[]{:S(2)}) copy-start(f32[2048]{0:T(1024)} %param.27) | copy-start | bytes 24580
  11.6 6.5 %copy-start.5 = (s32[2048]{0:T(1024)S(1)}, s32[2048]{0:T(1024)}, u32[]{:S(2)}) copy-start(s32[2048]{0:T(1024)} %param.23) | copy-start | bytes 24580
  29.9 9.1 %copy-start = (f32[4096]{0:T(1024)S(1)}, f32[4096]{0:T(1024)}, u32[]{:S(2)}) copy-start(f32[4096]{0:T(1024)} %param.22) | copy-start | bytes 49156
  33.2 13.8 %all-to-all-start.1 = ((f32[16,16,128]{2,1,0:T(8,128)}), f32[16,16,128]{2,1,0:T(8,128)S(1)}, u32[]{:S(2)}, u32[]{:S(2)}) async-start(f32[16,16,128]{2,1,0:T(8,128)} %bitcast.47), calls=%async_computation.1 | async-start | bytes 262144 | tf_op jit(solution)/shard_map/all_to_all | solution.py:192
  47.7 12.5 %all-to-all-start.2 = ((f32[16,24,128]{2,1,0:T(8,128)}), f32[16,24,128]{2,1,0:T(8,128)S(1)}, u32[]{:S(2)}, u32[]{:S(2)}) async-start(f32[16,24,128]{2,1,0:T(8,128)} %bitcast.46), calls=%async_computation.2 | async-start | bytes 393216 | tf_op jit(solution)/shard_map/all_to_all | solution.py:192
  61.8 19.1 %all-to-all-start.3 = ((f32[16,72,128]{2,1,0:T(8,128)}), f32[16,72,128]{2,1,0:T(8,128)S(1)}, u32[]{:S(2)}, u32[]{:S(2)}) async-start(f32[16,72,128]{2,1,0:T(8,128)} %get-tuple-element.55), calls=%async_computation.3 | async-start | bytes 1179648 | tf_op jit(solution)/shard_map/all_to_all | solution.py:192

commit v4 on v3

--- a/solution.py
+++ b/solution.py
@@ -13,7 +13,6 @@
 LANES = 128
 SUBLANES = 8
 NEAR = 5
-LAST_NEAR = 8
 FAR_PARTS = 2
 
 
@@ -145,14 +144,13 @@
     lines, buses = shift_factors.shape
     ut, lt, bt = units // LANES, lines // LANES, buses // LANES
     near_lines = lines * NEAR // 16
-    last_near = lines * LAST_NEAR // 16
     small = -(-(bt + 2) // SUBLANES) * SUBLANES
     at_power, at_upper, at_lower, at_flow = 0, ut, 2 * ut, 3 * ut
     at_total = at_flow + lt
-    at_load = at_total + ut
+    at_load = at_total
     at_price, at_capacity = at_load + bt, at_load + bt + 1
     rows_in = at_load + small
-    back_total, back_bus = 3 * ut, 4 * ut
+    back_bus = 3 * ut
     rows_back = back_bus + 2 * bt
     rows_update = ut + 2 * bt
     f32, bf16 = jnp.float32, jnp.bfloat16
@@ -163,7 +161,8 @@
         inner, outer = (pl.BlockSpec(memory_space=m) for m in (pltpu.VMEM, pltpu.HBM))
         return pl.pallas_call(
             body,
-            out_shape=[pltpu.VMEM(s, f32) for s in outs] + [pltpu.HBM(s, f32) for s in outs_far],
+            out_shape=[pltpu.VMEM(*s) if isinstance(s[0], tuple) else pltpu.VMEM(s, f32) for s in outs]
+            + [pltpu.HBM(s, f32) for s in outs_far],
             in_specs=[inner] * len(near) + [outer] * len(far),
             out_specs=[inner] * len(outs) + [outer] * len(outs_far),
             scratch_shapes=[pltpu.VMEM(*s) for s in scratch] + [pltpu.SemaphoreType.DMA((copies,))],
@@ -188,6 +187,21 @@
             for copy in self.sent:
                 copy.wait()
 
+    def add_up(value, stages):
+        for stage in stages:
+            value = sum(
+                [value]
+                + [
+                    lax.ppermute(value, "hour", [(j, j ^ other) for j in range(ndev)])
+                    for other in stage
+                ]
+            )
+        return value
+
+    bits = [1 << b for b in range(ndev.bit_length() - 1)]
+    half = 1 << (len(bits) // 2)
+    two_stages = [range(1, half), range(half, ndev, half)]
+
     def exchange(blocks):
         return lax.all_to_all(blocks, "hour", split_axis=0, concat_axis=0, tiled=True)
 
@@ -206,19 +220,13 @@
     def part(ref, index):
         return ref[pl.ds(index * ut, ut), :]
 
-    def bring_lines(copies, near, far, far_v, axis):
-        here = near.shape[axis]
-        size = (lines - here) // FAR_PARTS
-        result = [(pl.ds(0, here), near, lambda: None)]
+    def bring_lines(copies, near, far, far_v):
+        size = (lines - near_lines) // FAR_PARTS
+        result = [(pl.ds(0, near_lines), near, lambda: None)]
         for c in range(FAR_PARTS):
-            source, target = pl.ds(here + c * size, size), pl.ds(c * size, size)
-            if axis == 1:
-                copy = copies.bring(far.at[:, source], far_v.at[:, target])
-                part_v = far_v.at[:, target]
-            else:
-                copy = copies.bring(far.at[source], far_v.at[target])
-                part_v = far_v.at[target]
-            result.append((source, part_v, copy.wait))
+            source, target = pl.ds(near_lines + c * size, size), pl.ds(c * size, size)
+            copy = copies.bring(far.at[source], far_v.at[target])
+            result.append((source, far_v.at[target], copy.wait))
         return result
 
     def arrived(factors):
@@ -256,16 +264,11 @@
         bound = dual_step * limit[:, at]
         return probe - jnp.clip(probe, -bound, bound)
 
-    def network(injection, flow, shift, limit, incidence, new_flow, grid, turned=None):
-        if turned is None:
-            for at, factors, wait in shift:
-                wait()
-                probe = flow[:, at] + dual_step * across(injection, factors[...])
-                new_flow[:, at] = held_back(probe, limit, at)
-        else:
-            flows = jnp.dot(injection, turned[...], preferred_element_type=f32)
-            every = pl.ds(0, lines)
-            new_flow[...] = held_back(flow[...] + dual_step * flows, limit, every)
+    def network(injection, flow, shift, limit, incidence, new_flow, grid):
+        for at, factors, wait in shift:
+            wait()
+            probe = flow[:, at] + dual_step * across(injection, factors[...])
+            new_flow[:, at] = held_back(probe, limit, at)
         to_units(to_buses(new_flow, arrived(shift)), incidence, grid)
 
     def local(upper, lower, before, grid, price, settings, put_power, bar, put):
@@ -305,8 +308,9 @@
         return put
 
 
-    def pack(power, upper, lower, flow, load, price, capacity, out, *scratch):
-        load_v, price_v, capacity_v, blocks_v, semaphores = scratch
+    def pack(power, upper, lower, flow, load, price, capacity, *rest):
+        vectors, shift_far, unit_bus, total_o, settings, shift, out = rest[:4], *rest[4:10]
+        load_v, price_v, capacity_v, units_v, blocks_v, semaphores = rest[10:]
         copies = Copies(semaphores)
         blocks = blocks_v.reshape(ndev, rows_in, LANES)
         places = [
@@ -320,7 +324,12 @@
             copies.bring(load, load_v),
             copies.bring(price, price_v),
             copies.bring(capacity, capacity_v),
+            copies.bring(unit_bus, units_v),
+        ] + [
+            copies.bring(vector, settings.at[pl.ds(place * ut, ut)])
+            for place, vector in enumerate(vectors)
         ]
+        copies.send(shift_far.at[pl.ds(0, near_lines)], shift)
         for peer in range(ndev):
             blocks_v[pl.ds(peer * rows_in + at_load, small), :] = jnp.zeros((small, LANES), f32)
         for copy in come:
@@ -336,27 +345,23 @@
         spread(blocks_v, at_capacity, rows_in, jnp.broadcast_to(capacity_v[...], (ndev, LANES)))
         for copy in big:
             copy.wait()
-        at = pl.ds(0, at_total)
-        copies.send(blocks.at[:, at], out.at[:, at])
-        total = sum_blocks(blocks_v, at_upper, rows_in)
-        for peer in range(ndev):
-            blocks_v[pl.ds(peer * rows_in + at_total, ut), :] = total
-        at = pl.ds(at_total, rows_in - at_total)
-        copies.send(blocks.at[:, at], out.at[:, at])
+        copies.send(blocks, out)
+        total_o[...] = sum_blocks(blocks_v, at_upper, rows_in)
+        settings[pl.ds(0, ut), :] = 1.0 - settings[pl.ds(0, ut), :]
+        settings[pl.ds(4 * ut, ut), :] = units_v[...].astype(f32)
         copies.close()
 
-    def first(came, shift, settings, shift_far, turned, *rest):
-        del turned
+    def first(came, total_in, shift, settings, shift_far, *rest):
         power, upper, lower, bar, flow, load, notes, total_o = rest[:8]
         shift_v, incidence, out, grid, semaphores = rest[8:]
         copies = Copies(semaphores)
-        factors = bring_lines(copies, shift, shift_far, shift_v, 0)
+        factors = bring_lines(copies, shift, shift_far, shift_v)
         flow[...] = wide(came, at_flow, lt, rows_in)
         load[...] = wide(came, at_load, bt, rows_in)
         notes[pl.ds(ut, hours), :] = rows(came, at_price, rows_in)
         one_hot(settings, incidence)
         capacity, pull = capacities(
-            rows(came, at_capacity, rows_in), settings, sum_blocks(came, at_total, rows_in)
+            rows(came, at_capacity, rows_in), settings, total_in[...]
         )
         notes[pl.ds(0, ut), :] = capacity
         to_units(to_buses(flow, factors), incidence, grid)
@@ -384,7 +389,7 @@
         shift, bar, load, flow, line, upper, lower, power, notes, settings, shift_far,
         new_flow, new_power, lifted, low, sent, shift_v, incidence, grid, new_bar, semaphores,
     ):
-        factors = bring_lines(Copies(semaphores), shift, shift_far, shift_v, 0)
+        factors = bring_lines(Copies(semaphores), shift, shift_far, shift_v)
         one_hot(settings, incidence)
         injection = inject(bar, load, incidence)
         sent[pl.ds(0, hours), :] = injection.astype(f32)
@@ -397,13 +402,11 @@
         sent[pl.ds(hours, hours), :] = inject(new_bar, load, incidence).astype(f32)
 
     def third(
-        shift, sent, load, flow, line, upper, lower, power, notes, settings, shift_far, turned,
+        shift, sent, load, flow, line, upper, lower, power, notes, settings, shift_far,
         new_flow, new_power, lifted, low, grid, later,
-        shift_v, turned_v, incidence, new_bar, semaphores,
+        shift_v, incidence, new_bar, semaphores,
     ):
-        copies = Copies(semaphores)
-        factors = bring_lines(copies, shift, shift_far, shift_v, 0)
-        turned_factors = copies.bring(turned, turned_v)
+        factors = bring_lines(Copies(semaphores), shift, shift_far, shift_v)
         one_hot(settings, incidence)
         injection = sent[pl.ds(hours, hours), :].astype(bf16)
         network(injection, flow, factors, line, incidence, new_flow, grid)
@@ -414,10 +417,7 @@
         )
         injection = inject(new_bar, load, incidence)
         later[...] = injection.astype(f32)
-        turned_factors.wait()
-        network(
-            injection, new_flow, arrived(factors), line, incidence, new_flow, grid, turned_v
-        )
+        network(injection, new_flow, arrived(factors), line, incidence, new_flow, grid)
 
     def lift(lifted, low):
         def put(hour, new_lifted, new_low):
@@ -449,15 +449,14 @@
 
     def last(
         came, lifted, lower, power, grid, notes, settings, load, later,
-        new_notes, out_o, early_o, incidence, out, early, upper, bar, semaphores,
+        new_notes, total_o, out_o, early_o, incidence, out, early, upper, bar, semaphores,
     ):
         copies = Copies(semaphores)
         for step in range(2):
             early[pl.ds(step * scen, scen), :] = wide(came, ut + step * bt, bt, rows_update)
         copies.send(early, early_o)
         total = raise_upper(came, rows_update, lifted, notes, settings, upper, new_notes)
-        for peer in range(ndev):
-            out[pl.ds(peer * rows_back + back_total, ut), :] = total
+        total_o[...] = total
 
         def put_power(hour, value):
             out[pl.ds(hour * rows_back, ut), :] = value
@@ -480,29 +479,36 @@
         copies.send(blocks.at[:, at], out_o.at[:, at])
         copies.close()
 
-    def hourly_flow(line, early, flow, turned, new_o, early_v, flow_v, turned_v, new, semaphores):
+    def two_steps(value, injections, factors, line, at):
+        flows = dual_step * across(injections, factors[...])
+        for step in range(2):
+            value = held_back(value + flows[step * scen : (step + 1) * scen], line, at)
+        return value
+
+    def hourly_flow(
+        shift, line, early, flow, shift_far, new_o, early_v, flow_v, shift_v, new, semaphores
+    ):
         copies = Copies(semaphores)
-        come = [copies.bring(*pair) for pair in ((early, early_v), (flow, flow_v), (turned, turned_v))]
+        come = [copies.bring(early, early_v), copies.bring(flow, flow_v)]
+        factors = bring_lines(copies, shift, shift_far, shift_v)
         for copy in come:
             copy.wait()
-        flows = jnp.dot(early_v[...].astype(bf16), turned_v[...], preferred_element_type=f32)
-        every = pl.ds(0, lines)
-        value = wide(flow_v, 0, lt, lt)
-        for step in range(2):
-            flow_step = flows[step * scen : (step + 1) * scen]
-            value = held_back(value + dual_step * flow_step, line, every)
-        new[...] = value
+        injections = early_v[...].astype(bf16)
+        new[...] = wide(flow_v, 0, lt, lt)
+        for at, part_v, wait in factors:
+            wait()
+            new[:, at] = two_steps(new[:, at], injections, part_v, line, at)
         copies.send(new, new_o)
         copies.close()
 
     def finish(
-        came, notes, settings, line, turned, flow, turned_far,
+        came, total, notes, settings, line, shift, flow, shift_far,
         power_o, upper_o, lower_o, flow_o, capacity_o,
-        turned_v, flow_v, notes_v, upper, own, out, semaphores,
+        shift_v, flow_v, notes_v, upper, own, out, semaphores,
     ):
         copies = Copies(semaphores)
         flow_came = copies.bring(flow, flow_v)
-        factors = bring_lines(copies, turned, turned_far, turned_v, 1)
+        factors = bring_lines(copies, shift, shift_far, shift_v)
         blocks = came.reshape(ndev, rows_back, LANES)
         copies.send(blocks.at[:, pl.ds(0, ut)], power_o)
         copies.send(blocks.at[:, pl.ds(2 * ut, ut)], lower_o)
@@ -513,15 +519,11 @@
         row = 0
         for at, part_v, wait in factors:
             wait()
-            flows = dual_step * jnp.dot(injections, part_v[...], preferred_element_type=f32)
-            value = flow_v[:, at]
-            for step in range(2):
-                value = held_back(value + flows[step * scen : (step + 1) * scen], line, at)
+            value = two_steps(flow_v[:, at], injections, part_v, line, at)
             spread(out, row, lt, value)
             row += value.shape[1] // LANES
         copies.send(out.reshape(scen, lt, LANES), flow_o)
-        total = sum_blocks(came, back_total, rows_back)
-        capacity, pull = capacities(part(notes, 0), settings, total)
+        capacity, pull = capacities(part(notes, 0), settings, total[...])
         for peer in range(ndev):
             upper[peer] = jnp.maximum(came[pl.ds(peer * rows_back + ut, ut), :] - pull, 0.0)
         copies.send(upper, upper_o)
@@ -534,21 +536,15 @@
     def tiles(vector):
         return vector.reshape(-1, LANES)
 
-    settings = jnp.concatenate(
-        [
-            tiles(v)
-            for v in (1.0 - leakage, initial_state, power_limit, capacity_cost, unit_bus.astype(f32))
-        ]
-    )
     line = line_limit.reshape(1, lines)
-    shift, shift_far, turned = shift_factors[:near_lines], shift_factors, shift_factors.T
+    shift_far = shift_factors
 
     state_v, incidence_v = (state, f32), ((buses, units), bf16)
     shift_v = ((lines - near_lines, buses), bf16)
     notes = (ut + hours, LANES)
     flops = 4 * hours * buses * (lines + units)
 
-    (sent,) = call(
+    total, settings, shift, sent = call(
         pack,
         [],
         [
@@ -559,20 +555,27 @@
             load.reshape(scen, buses),
             price.reshape(1, scen),
             capacity.reshape(1, LANES),
+            tiles(leakage),
+            tiles(initial_state),
+            tiles(power_limit),
+            tiles(capacity_cost),
+            shift_far,
+            tiles(unit_bus),
         ],
-        [],
+        [(ut, LANES), (5 * ut, LANES), ((near_lines, buses), bf16)],
         [(ndev, rows_in, LANES)],
         [
-            ((scen, buses), bf16), ((1, scen), f32), ((1, LANES), f32),
+            ((scen, buses), bf16), ((1, scen), f32), ((1, LANES), f32), ((ut, LANES), jnp.int32),
             ((ndev * rows_in, LANES), f32),
         ],
-        9,
+        14,
     )
     came = exchange(sent).reshape(-1, LANES)
+    total = add_up(total, two_stages)
     power, upper, lower, bar, flow, load, note, total = call(
         first,
-        [came, shift, settings],
-        [shift_far, turned],
+        [came, total, shift, settings],
+        [shift_far],
         [state] * 4 + [(hours, lines), (hours, buses), notes],
         [state],
         [shift_v, incidence_v, state_v, state_v],
@@ -603,18 +606,18 @@
     flow, power, lifted, lower, grid, injection = call(
         third,
         [shift, injections, load, flow, line, upper, lower, power, note, settings],
-        [shift_far, turned],
+        [shift_far],
         [(hours, lines)] + [state] * 4 + [(hours, buses)],
         [],
-        [shift_v, ((buses, lines), bf16), incidence_v, state_v],
-        FAR_PARTS + 1,
+        [shift_v, incidence_v, state_v],
+        FAR_PARTS,
         flops=2 * flops,
     )
-    note, sent, early = call(
+    note, total, sent, early = call(
         last,
         [came, lifted, lower, power, grid, note, settings, load, injection],
         [],
-        [notes],
+        [notes, (ut, LANES)],
         [(ndev, rows_back, LANES), (2 * scen, buses)],
         [
             incidence_v, ((ndev * rows_back, LANES), f32), ((2 * scen, buses), f32), state_v,
@@ -624,26 +627,27 @@
         flops=flops,
     )
     came = exchange(sent).reshape(-1, LANES)
+    total = add_up(total, two_stages)
     own_flow = ((scen * lt, LANES), f32)
     (flow,) = call(
         hourly_flow,
-        [line],
-        [early, flow_dual.reshape(scen * lt, LANES), turned],
+        [shift, line],
+        [early, flow_dual.reshape(scen * lt, LANES), shift_far],
         [],
         [(scen, lines)],
-        [((2 * scen, buses), f32), own_flow, ((buses, lines), bf16), ((scen, lines), f32)],
-        4,
+        [((2 * scen, buses), f32), own_flow, shift_v, ((scen, lines), f32)],
+        FAR_PARTS + 3,
         flops=flops,
     )
     hourly = (scen, ut, LANES)
     power, upper, lower, flow, capacity = call(
         finish,
-        [came, note, settings, line, turned[:, :last_near]],
-        [flow, turned],
+        [came, total, note, settings, line, shift],
+        [flow, shift_far],
         [],
         [hourly, hourly, hourly, (scen, lt, LANES), (1, LANES)],
         [
-            ((buses, lines - last_near), bf16), ((scen, lines), f32), ((ut, LANES), f32),
+            shift_v, ((scen, lines), f32), ((ut, LANES), f32),
             (hourly, f32), ((1, LANES), f32), own_flow,
         ],
         6 + FAR_PARTS,
@@ -667,6 +671,7 @@
         and capacity.shape[0] == LANES
         and flow_dual.shape[2] % (16 * FAR_PARTS * LANES) == 0
         and ndev % (2 * SUBLANES) == 0
+        and ndev & (ndev - 1) == 0
         and all(size % (SUBLANES * LANES) == 0 for size in (power.shape[2], flow_dual.shape[2]))
         and buses % LANES == 0
     )

time: 84.7 us -> 82.5 us (0.974)
  starting transfers between devices: 20.4 us -> 31.5 us
  local copies, waits for them, and re-layouts: 9.59 us -> 0.01 us
  waiting for transfers between devices: 29.1 us -> 24.9 us
    all_to_all x4, waiting for transfers between devices: 29.1 us -> 6.93 us  [exchange(): lax.all_to_all(blocks, 'hour', split_axis=0, concat_axis=0, tiled=True)]
    ppermute x0 -> x12, waiting for transfers between devices: none -> 17.9 us  [add_up(): lax.ppermute(value, 'hour', [(j, j ^ other) for j in range(ndev)])]
    ppermute x0 -> x12, starting transfers between devices: none -> 13.2 us  [add_up(): lax.ppermute(value, 'hour', [(j, j ^ other) for j in range(ndev)])]
    unnamed x16 -> x2, local copies, waits for them, and re-layouts: 6.46 us -> 0.01 us
    slice x2 -> x0, local copies, waits for them, and re-layouts: 3.13 us -> none  [the longest x1 1.73 us: by_scenarios(): turned[:, :last_near]]
    all_to_all x4, starting transfers between devices: 20.4 us -> 18.3 us  [exchange(): lax.all_to_all(blocks, 'hour', split_axis=0, concat_axis=0, tiled=True)]
  transfers between devices with their start and end apart: 4 -> 16, of which waited for: 4 -> 9; matrix products, arithmetic and copies ran while one was open for 11% -> 0% of each run, Pallas kernels for 16% -> 16%
where the time goes in v4:
time: 82.5 us; the launch traced here: 81.9 us
  starting transfers between devices  31.5 us (38%)
  waiting for transfers between devices  24.9 us (30%)
  Pallas kernels  24.7 us (30%)
    pallas_call x8, Pallas kernels, call(): pl.pallas_call(body, out_shape=[pltpu.VMEM(*s) if isinstance(s[0], tuple)...  24.7 us
    all_to_all x4, starting transfers between devices, exchange(): lax.all_to_all(blocks, 'hour', split_axis=0, concat_axis=0, tiled=True)  18.3 us
    ppermute x12, waiting for transfers between devices, add_up(): lax.ppermute(value, 'hour', [(j, j ^ other) for j in range(ndev)])  17.9 us
    ppermute x12, starting transfers between devices, add_up(): lax.ppermute(value, 'hour', [(j, j ^ other) for j in range(ndev)])  13.2 us
    all_to_all x4, waiting for transfers between devices, exchange(): lax.all_to_all(blocks, 'hour', split_axis=0, concat_axis=0, tiled=True)  6.93 us
  transfers between devices with their start and end apart: 16, of which 9 were waited for; matrix products, arithmetic and copies ran while one was open for 0% of the time, Pallas kernels for 16%

profile of v4, /device:TPU:0, one launch (start us, length us, event | category | flops | bytes accessed | tf_op | source)
XLA Modules:
  0.0 81.9 jit_solution(14856228381973894045)
XLA Ops:
  0.6 2.1 %shard_map.173 = (f32[16,128]{1,0:T(8,128)S(1)}, f32[80,128]{1,0:T(8,128)S(1)}, bf16[1280,512]{1,0:T(8,128)(2,1)S(1)}, f32[16,88,128]{2,1,0:T(8,128)}) custom-call(f32[16,16,128]{2,1,0:T(8,128)} %bitcast.36, f32[16,16,128]{2,1,0:T(8,128)} %bitcast.37, f32[16,16,128]{2,1,0:T(8,128)} %bitcast.38, f32[16,32,128]{2,1,0:T(8,128)} %bitcast.33, ...), custom_call_target="tpu_custom_call" | custom-call | bytes 4907584 | tf_op jit(solution)/shard_map/pallas_call | solution.py:162
  2.8 7.4 %all-to-all-start = ((f32[16,88,128]{2,1,0:T(8,128)}), f32[16,88,128]{2,1,0:T(8,128)S(1)}, u32[]{:S(2)}, u32[]{:S(2)}) async-start(f32[16,88,128]{2,1,0:T(8,128)} %get-tuple-element.39), calls=%async_computation | async-start | bytes 1441792 | tf_op jit(solution)/shard_map/all_to_all | solution.py:206
  10.2 1.7 %collective-permute-start.2 = (f32[16,128]{1,0:T(8,128)S(1)}, f32[16,128]{1,0:T(8,128)S(1)}, u32[]{:S(2)}, u32[]{:S(2)}) collective-permute-start(f32[16,128]{1,0:T(8,128)S(1)} %get-tuple-element.40), channel_id=1, source_target_pairs={{0,3},{1,2},{2,1},{3,0},{4,7},{5,6},{6,5},{7,4},{8,11},{9,10},{10,... | collective-permute-start | bytes 24584 | tf_op jit(solution)/shard_map/ppermute | solution.py:195
  12.2 4.2 %collective-permute-done.2 = f32[16,128]{1,0:T(8,128)S(1)} collective-permute-done((f32[16,128]{1,0:T(8,128)S(1)}, f32[16,128]{1,0:T(8,128)S(1)}, u32[]{:S(2)}, u32[]{:S(2)}) %collective-permute-start.2) | collective-permute-done | bytes 8224 | tf_op jit(solution)/shard_map/ppermute | solution.py:195
  16.4 0.8 collective-permute-done.1
  17.2 4.1 %collective-permute-start.5 = (f32[16,128]{1,0:T(8,128)S(1)}, f32[16,128]{1,0:T(8,128)S(1)}, u32[]{:S(2)}, u32[]{:S(2)}) collective-permute-start(f32[16,128]{1,0:T(8,128)S(1)} %add_add_fusion.3), channel_id=1, source_target_pairs={{0,12},{1,13},{2,14},{3,15},{4,8},{5,9},{6,10},{7,11},{8,4},{9,5},... | collective-permute-start | bytes 24584 | tf_op jit(solution)/shard_map/ppermute | solution.py:195
  22.0 5.3 %collective-permute-done.5 = f32[16,128]{1,0:T(8,128)S(1)} collective-permute-done((f32[16,128]{1,0:T(8,128)S(1)}, f32[16,128]{1,0:T(8,128)S(1)}, u32[]{:S(2)}, u32[]{:S(2)}) %collective-permute-start.5) | collective-permute-done | bytes 8224 | tf_op jit(solution)/shard_map/ppermute | solution.py:195
  27.3 3.1 %collective-permute-done.4 = f32[16,128]{1,0:T(8,128)S(1)} collective-permute-done((f32[16,128]{1,0:T(8,128)S(1)}, f32[16,128]{1,0:T(8,128)S(1)}, u32[]{:S(2)}, u32[]{:S(2)}) %collective-permute-start.4) | collective-permute-done | bytes 8224 | tf_op jit(solution)/shard_map/ppermute | solution.py:195
  30.4 3.2 %shard_map.174 = (f32[256,128]{1,0:T(8,128)S(1)}, f32[256,128]{1,0:T(8,128)S(1)}, f32[256,128]{1,0:T(8,128)S(1)}, f32[256,128]{1,0:T(8,128)S(1)}, f32[16,4096]{1...) custom-call(f32[1408,128]{1,0:T(8,128)S(1)} %bitcast.25, ...), custom_call_target="tpu_custom_call" | custom-call | flops 201326592 | bytes 6275072 | tf_op jit(solution)/shard_map/pallas_call | solution.py:162
  33.7 3.7 %all-to-all-start.1 = ((f32[16,16,128]{2,1,0:T(8,128)}), f32[16,16,128]{2,1,0:T(8,128)S(1)}, u32[]{:S(2)}, u32[]{:S(2)}) async-start(f32[16,16,128]{2,1,0:T(8,128)} %bitcast.39), calls=%async_computation.1 | async-start | bytes 262144 | tf_op jit(solution)/shard_map/all_to_all | solution.py:206
  37.4 3.9 %shard_map.175 = (f32[16,4096]{1,0:T(8,128)S(1)}, f32[256,128]{1,0:T(8,128)S(1)}, f32[256,128]{1,0:T(8,128)S(1)}, f32[256,128]{1,0:T(8,128)S(1)}, f32[32,512]{1,0:T(8,128)S(1)}) custom-call(bf16[1280,512]{1,0:T(8,128)(2,1)S(1)} %get-tuple-element.41.shift, f32[256,128]{1,0:T(8,128)S(1)} %get-tuple-element.44.bar, f32[16,512]{1,0:T(8,128)S(1)} %get-tuple-element.45.load, ...), custom_call_target="tpu_custom_call" | custom-call | flops 201326592 | bytes 6397952 | tf_op jit(solution)/shard_map/pallas_call | solution.py:162
  41.3 4.0 %all-to-all-done.1 = f32[16,16,128]{2,1,0:T(8,128)S(1)} async-done(((f32[16,16,128]{2,1,0:T(8,128)}), f32[16,16,128]{2,1,0:T(8,128)S(1)}, u32[]{:S(2)}, u32[]{:S(2)}) %all-to-all-start.1) | async-done | bytes 131104 | tf_op jit(solution)/shard_map/all_to_all | solution.py:206
  45.4 0.7 shard_map.176
  46.1 3.5 %all-to-all-start.2 = ((f32[16,24,128]{2,1,0:T(8,128)}), f32[16,24,128]{2,1,0:T(8,128)S(1)}, u32[]{:S(2)}, u32[]{:S(2)}) async-start(f32[16,24,128]{2,1,0:T(8,128)} %bitcast.35), calls=%async_computation.2 | async-start | bytes 393216 | tf_op jit(solution)/shard_map/all_to_all | solution.py:206
  49.6 6.1 %shard_map.177 = (f32[16,4096]{1,0:T(8,128)}, f32[256,128]{1,0:T(8,128)S(1)}, f32[256,128]{1,0:T(8,128)S(1)}, f32[256,128]{1,0:T(8,128)S(1)}, f32[256,128]{1,0:T(8,128)S(1)}, /*index=5*/f32[16,512]{1,0:T(8,128)S(1)}) custom-call(bf16[1280,512]{1,0:T(8,128)(2,1)S(1)} %get-tuple-element.41.shift, f32[32,512]{1,0:T(8,128)S(1)} %get-tuple-element.52.sent, ...), custom_call_target="tpu_custom_call" | custom-call | flops 402653184 | bytes 6332416 | tf_op jit(solution)/shard_map/pallas_call | solution.py:162
  55.7 2.9 %all-to-all-done.2 = f32[16,24,128]{2,1,0:T(8,128)S(1)} async-done(((f32[16,24,128]{2,1,0:T(8,128)}), f32[16,24,128]{2,1,0:T(8,128)S(1)}, u32[]{:S(2)}, u32[]{:S(2)}) %all-to-all-start.2) | async-done | bytes 196640 | tf_op jit(solution)/shard_map/all_to_all | solution.py:206
  58.6 1.6 %shard_map.178 = (f32[32,128]{1,0:T(8,128)S(1)}, f32[16,128]{1,0:T(8,128)S(1)}, f32[16,56,128]{2,1,0:T(8,128)}, f32[32,512]{1,0:T(8,128)}) custom-call(f32[384,128]{1,0:T(8,128)S(1)} %bitcast.27, f32[256,128]{1,0:T(8,128)S(1)} %get-tuple-element.59.lifted, f32[256,128]{1,0:T(8,128)S(1)} %get-tuple-element.60.lower, f32[256,128]{1,0:T(8,128)S(1)} %get-tuple-element.61.power, ...), custom_call_target="tpu_custom_call" | custom-call | flops 201326592 | bytes 843776 | tf_op jit(solution)/shard_map/pallas_call | solution.py:162
  60.2 3.6 %all-to-all-start.3 = ((f32[16,56,128]{2,1,0:T(8,128)}), f32[16,56,128]{2,1,0:T(8,128)S(1)}, u32[]{:S(2)}, u32[]{:S(2)}) async-start(f32[16,56,128]{2,1,0:T(8,128)} %get-tuple-element.64), calls=%async_computation.3 | async-start | bytes 917504 | tf_op jit(solution)/shard_map/all_to_all | solution.py:206
  63.8 1.6 %collective-permute-start.8 = (f32[16,128]{1,0:T(8,128)S(1)}, f32[16,128]{1,0:T(8,128)S(1)}, u32[]{:S(2)}, u32[]{:S(2)}) collective-permute-start(f32[16,128]{1,0:T(8,128)S(1)} %get-tuple-element.65), channel_id=1, source_target_pairs={{0,3},{1,2},{2,1},{3,0},{4,7},{5,6},{6,5},{7,4},{8,11},{9,10},{10,... | collective-permute-start | bytes 24584 | tf_op jit(solution)/shard_map/ppermute | solution.py:195
  65.7 2.0 %collective-permute-done.8 = f32[16,128]{1,0:T(8,128)S(1)} collective-permute-done((f32[16,128]{1,0:T(8,128)S(1)}, f32[16,128]{1,0:T(8,128)S(1)}, u32[]{:S(2)}, u32[]{:S(2)}) %collective-permute-start.8) | collective-permute-done | bytes 8224 | tf_op jit(solution)/shard_map/ppermute | solution.py:195
  67.7 2.0 %collective-permute-done.7 = f32[16,128]{1,0:T(8,128)S(1)} collective-permute-done((f32[16,128]{1,0:T(8,128)S(1)}, f32[16,128]{1,0:T(8,128)S(1)}, u32[]{:S(2)}, u32[]{:S(2)}) %collective-permute-start.7) | collective-permute-done | bytes 8224 | tf_op jit(solution)/shard_map/ppermute | solution.py:195
  69.7 3.8 %collective-permute-start.11 = (f32[16,128]{1,0:T(8,128)S(1)}, f32[16,128]{1,0:T(8,128)S(1)}, u32[]{:S(2)}, u32[]{:S(2)}) collective-permute-start(f32[16,128]{1,0:T(8,128)S(1)} %add_add_fusion.1), channel_id=1, source_target_pairs={{0,12},{1,13},{2,14},{3,15},{4,8},{5,9},{6,10},{7,11},{8,4},{9,5},... | collective-permute-start | bytes 24584 | tf_op jit(solution)/shard_map/ppermute | solution.py:195
  74.2 3.5 %shard_map.179.flow = f32[16,4096]{1,0:T(8,128)} custom-call(bf16[1280,512]{1,0:T(8,128)(2,1)S(1)} %get-tuple-element.41.shift, f32[1,4096]{1,0:T(1,128)S(1)} %bitcast.31, f32[32,512]{1,0:T(8,128)} %get-tuple-element.67.early, f32[512,128]{1,0:T(8,128)} %bitcast.34, bf16[4096,512]{1,0:T(8,128)(2,1)} %shift_far.9), custom_call_target="tpu_custom_call" | custom-call | flops 201326592 | bytes 5849088 | tf_op jit(solution)/shard_map/pallas_call | solution.py:162
  78.3 3.6 %shard_map.180 = (f32[16,16,128]{2,1,0:T(8,128)}, f32[16,16,128]{2,1,0:T(8,128)}, f32[16,16,128]{2,1,0:T(8,128)}, f32[16,32,128]{2,1,0:T(8,128)}, f32[1,128]{1,0:T(1,128)}) custom-call(f32[896,128]{1,0:T(8,128)S(1)} %bitcast.26, f32[16,128]{1,0:T(8,128)S(1)} %add_add_fusion.total, f32[32,128]{1,0:T(8,128)S(1)} %get-tuple-element.66.notes, ...), custom_call_target="tpu_custom_call" | custom-call | bytes 6307840 | tf_op jit(solution)/shard_map/pallas_call | solution.py:162
  (22 shorter events, 2.6 us)
Async XLA Ops:
  2.8 34.7 %copy-start = (f32[4096]{0:T(1024)S(1)}, f32[4096]{0:T(1024)}, u32[]{:S(2)}) copy-start(f32[4096]{0:T(1024)} %param.22) | copy-start | bytes 49156
  2.8 27.6 %all-to-all-start = ((f32[16,88,128]{2,1,0:T(8,128)}), f32[16,88,128]{2,1,0:T(8,128)S(1)}, u32[]{:S(2)}, u32[]{:S(2)}) async-start(f32[16,88,128]{2,1,0:T(8,128)} %get-tuple-element.39), calls=%async_computation | async-start | bytes 1441792 | tf_op jit(solution)/shard_map/all_to_all | solution.py:206
  10.2 6.2 %collective-permute-start.2 = (f32[16,128]{1,0:T(8,128)S(1)}, f32[16,128]{1,0:T(8,128)S(1)}, u32[]{:S(2)}, u32[]{:S(2)}) collective-permute-start(f32[16,128]{1,0:T(8,128)S(1)} %get-tuple-element.40), channel_id=1, source_target_pairs={{0,3},{1,2},{2,1},{3,0},{4,7},{5,6},{6,5},{7,4},{8,11},{9,10},{10,... | collective-permute-start | bytes 24584 | tf_op jit(solution)/shard_map/ppermute | solution.py:195
  11.9 5.3 %collective-permute-start.1 = (f32[16,128]{1,0:T(8,128)S(1)}, f32[16,128]{1,0:T(8,128)S(1)}, u32[]{:S(2)}, u32[]{:S(2)}) collective-permute-start(f32[16,128]{1,0:T(8,128)S(1)} %get-tuple-element.40), channel_id=1, source_target_pairs={{0,2},{1,3},{2,0},{3,1},{4,6},{5,7},{6,4},{7,5},{8,10},{9,11},{10,... | collective-permute-start | bytes 24584 | tf_op jit(solution)/shard_map/ppermute | solution.py:195
  12.2 5.0 %collective-permute-start = (f32[16,128]{1,0:T(8,128)S(1)}, f32[16,128]{1,0:T(8,128)S(1)}, u32[]{:S(2)}, u32[]{:S(2)}) collective-permute-start(f32[16,128]{1,0:T(8,128)S(1)} %get-tuple-element.40), channel_id=1, source_target_pairs={{0,1},{1,0},{2,3},{3,2},{4,5},{5,4},{6,7},{7,6},{8,9},{9,8},{10,11... | collective-permute-start | bytes 24584 | tf_op jit(solution)/shard_map/ppermute | solution.py:195
  17.2 10.1 %collective-permute-start.5 = (f32[16,128]{1,0:T(8,128)S(1)}, f32[16,128]{1,0:T(8,128)S(1)}, u32[]{:S(2)}, u32[]{:S(2)}) collective-permute-start(f32[16,128]{1,0:T(8,128)S(1)} %add_add_fusion.3), channel_id=1, source_target_pairs={{0,12},{1,13},{2,14},{3,15},{4,8},{5,9},{6,10},{7,11},{8,4},{9,5},... | collective-permute-start | bytes 24584 | tf_op jit(solution)/shard_map/ppermute | solution.py:195
  21.3 9.1 %collective-permute-start.4 = (f32[16,128]{1,0:T(8,128)S(1)}, f32[16,128]{1,0:T(8,128)S(1)}, u32[]{:S(2)}, u32[]{:S(2)}) collective-permute-start(f32[16,128]{1,0:T(8,128)S(1)} %add_add_fusion.3), channel_id=1, source_target_pairs={{0,8},{1,9},{2,10},{3,11},{4,12},{5,13},{6,14},{7,15},{8,0},{9,1},... | collective-permute-start | bytes 24584 | tf_op jit(solution)/shard_map/ppermute | solution.py:195
  21.3 9.1 %collective-permute-start.3 = (f32[16,128]{1,0:T(8,128)S(1)}, f32[16,128]{1,0:T(8,128)S(1)}, u32[]{:S(2)}, u32[]{:S(2)}) collective-permute-start(f32[16,128]{1,0:T(8,128)S(1)} %add_add_fusion.3), channel_id=1, source_target_pairs={{0,4},{1,5},{2,6},{3,7},{4,0},{5,1},{6,2},{7,3},{8,12},{9,13},{10,... | collective-permute-start | bytes 24584 | tf_op jit(solution)/shard_map/ppermute | solution.py:195
  33.7 11.7 %all-to-all-start.1 = ((f32[16,16,128]{2,1,0:T(8,128)}), f32[16,16,128]{2,1,0:T(8,128)S(1)}, u32[]{:S(2)}, u32[]{:S(2)}) async-start(f32[16,16,128]{2,1,0:T(8,128)} %bitcast.39), calls=%async_computation.1 | async-start | bytes 262144 | tf_op jit(solution)/shard_map/all_to_all | solution.py:206
  46.1 12.5 %all-to-all-start.2 = ((f32[16,24,128]{2,1,0:T(8,128)}), f32[16,24,128]{2,1,0:T(8,128)S(1)}, u32[]{:S(2)}, u32[]{:S(2)}) async-start(f32[16,24,128]{2,1,0:T(8,128)} %bitcast.35), calls=%async_computation.2 | async-start | bytes 393216 | tf_op jit(solution)/shard_map/all_to_all | solution.py:206
  60.2 18.1 %all-to-all-start.3 = ((f32[16,56,128]{2,1,0:T(8,128)}), f32[16,56,128]{2,1,0:T(8,128)S(1)}, u32[]{:S(2)}, u32[]{:S(2)}) async-start(f32[16,56,128]{2,1,0:T(8,128)} %get-tuple-element.64), calls=%async_computation.3 | async-start | bytes 917504 | tf_op jit(solution)/shard_map/all_to_all | solution.py:206
  63.8 3.9 %collective-permute-start.8 = (f32[16,128]{1,0:T(8,128)S(1)}, f32[16,128]{1,0:T(8,128)S(1)}, u32[]{:S(2)}, u32[]{:S(2)}) collective-permute-start(f32[16,128]{1,0:T(8,128)S(1)} %get-tuple-element.65), channel_id=1, source_target_pairs={{0,3},{1,2},{2,1},{3,0},{4,7},{5,6},{6,5},{7,4},{8,11},{9,10},{10,... | collective-permute-start | bytes 24584 | tf_op jit(solution)/shard_map/ppermute | solution.py:195
  65.3 4.4 %collective-permute-start.7 = (f32[16,128]{1,0:T(8,128)S(1)}, f32[16,128]{1,0:T(8,128)S(1)}, u32[]{:S(2)}, u32[]{:S(2)}) collective-permute-start(f32[16,128]{1,0:T(8,128)S(1)} %get-tuple-element.65), channel_id=1, source_target_pairs={{0,2},{1,3},{2,0},{3,1},{4,6},{5,7},{6,4},{7,5},{8,10},{9,11},{10,... | collective-permute-start | bytes 24584 | tf_op jit(solution)/shard_map/ppermute | solution.py:195
  65.7 4.0 %collective-permute-start.6 = (f32[16,128]{1,0:T(8,128)S(1)}, f32[16,128]{1,0:T(8,128)S(1)}, u32[]{:S(2)}, u32[]{:S(2)}) collective-permute-start(f32[16,128]{1,0:T(8,128)S(1)} %get-tuple-element.65), channel_id=1, source_target_pairs={{0,1},{1,0},{2,3},{3,2},{4,5},{5,4},{6,7},{7,6},{8,9},{9,8},{10,11... | collective-permute-start | bytes 24584 | tf_op jit(solution)/shard_map/ppermute | solution.py:195
  69.7 8.0 %collective-permute-start.11 = (f32[16,128]{1,0:T(8,128)S(1)}, f32[16,128]{1,0:T(8,128)S(1)}, u32[]{:S(2)}, u32[]{:S(2)}) collective-permute-start(f32[16,128]{1,0:T(8,128)S(1)} %add_add_fusion.1), channel_id=1, source_target_pairs={{0,12},{1,13},{2,14},{3,15},{4,8},{5,9},{6,10},{7,11},{8,4},{9,5},... | collective-permute-start | bytes 24584 | tf_op jit(solution)/shard_map/ppermute | solution.py:195
  73.5 4.7 %collective-permute-start.10 = (f32[16,128]{1,0:T(8,128)S(1)}, f32[16,128]{1,0:T(8,128)S(1)}, u32[]{:S(2)}, u32[]{:S(2)}) collective-permute-start(f32[16,128]{1,0:T(8,128)S(1)} %add_add_fusion.1), channel_id=1, source_target_pairs={{0,8},{1,9},{2,10},{3,11},{4,12},{5,13},{6,14},{7,15},{8,0},{9,1},... | collective-permute-start | bytes 24584 | tf_op jit(solution)/shard_map/ppermute | solution.py:195
  73.5 4.7 %collective-permute-start.9 = (f32[16,128]{1,0:T(8,128)S(1)}, f32[16,128]{1,0:T(8,128)S(1)}, u32[]{:S(2)}, u32[]{:S(2)}) collective-permute-start(f32[16,128]{1,0:T(8,128)S(1)} %add_add_fusion.1), channel_id=1, source_target_pairs={{0,4},{1,5},{2,6},{3,7},{4,0},{5,1},{6,2},{7,3},{8,12},{9,13},{10,... | collective-permute-start | bytes 24584 | tf_op jit(solution)/shard_map/ppermute | solution.py:195

commit v5 on v4

--- a/solution.py
+++ b/solution.py
@@ -187,16 +187,15 @@
             for copy in self.sent:
                 copy.wait()
 
-    def add_up(value, stages):
+    def gather_up(value, stages):
+        terms = [value]
         for stage in stages:
-            value = sum(
-                [value]
-                + [
-                    lax.ppermute(value, "hour", [(j, j ^ other) for j in range(ndev)])
-                    for other in stage
-                ]
-            )
-        return value
+            value = sum(terms)
+            terms = [value] + [
+                lax.ppermute(value, "hour", [(j, j ^ other) for j in range(ndev)])
+                for other in stage
+            ]
+        return terms
 
     bits = [1 << b for b in range(ndev.bit_length() - 1)]
     half = 1 << (len(bits) // 2)
@@ -220,13 +219,18 @@
     def part(ref, index):
         return ref[pl.ds(index * ut, ut), :]
 
-    def bring_lines(copies, near, far, far_v):
+    def bring_lines(copies, near, far, far_v, axis=0):
         size = (lines - near_lines) // FAR_PARTS
         result = [(pl.ds(0, near_lines), near, lambda: None)]
         for c in range(FAR_PARTS):
             source, target = pl.ds(near_lines + c * size, size), pl.ds(c * size, size)
-            copy = copies.bring(far.at[source], far_v.at[target])
-            result.append((source, far_v.at[target], copy.wait))
+            if axis == 0:
+                part_v = far_v.at[target]
+                copy = copies.bring(far.at[source], part_v)
+            else:
+                part_v = far_v.at[:, target]
+                copy = copies.bring(far.at[:, source], part_v)
+            result.append((source, part_v, copy.wait))
         return result
 
     def arrived(factors):
@@ -351,37 +355,31 @@
         settings[pl.ds(4 * ut, ut), :] = units_v[...].astype(f32)
         copies.close()
 
-    def first(came, total_in, shift, settings, shift_far, *rest):
-        power, upper, lower, bar, flow, load, notes, total_o = rest[:8]
-        shift_v, incidence, out, grid, semaphores = rest[8:]
+    def first(came, shift, settings, shift_far, turned, *rest):
+        del turned
+        power, lifted, lower, bar, flow, load, notes, shift_v, incidence, grid, semaphores = rest
         copies = Copies(semaphores)
         factors = bring_lines(copies, shift, shift_far, shift_v)
         flow[...] = wide(came, at_flow, lt, rows_in)
         load[...] = wide(came, at_load, bt, rows_in)
         notes[pl.ds(ut, hours), :] = rows(came, at_price, rows_in)
         one_hot(settings, incidence)
-        capacity, pull = capacities(
-            rows(came, at_capacity, rows_in), settings, total_in[...]
-        )
-        notes[pl.ds(0, ut), :] = capacity
+        notes[pl.ds(0, ut), :] = rows(came, at_capacity, rows_in)
         to_units(to_buses(flow, factors), incidence, grid)
-        total = [jnp.zeros((ut, LANES), f32)]
-
-        def put(hour, lifted, low):
-            new = jnp.maximum(lifted - pull, 0.0)
-            upper[pl.ds(hour * ut, ut), :] = new
-            lower[pl.ds(hour * ut, ut), :] = low
-            total[0] = total[0] + new
-
         def received(first_row, count=ut):
             return lambda hour: came[pl.ds(hour * rows_in + first_row, count), :]
 
         local(
             received(at_upper), received(at_lower), received(at_power), grid,
-            received(at_price, 1), settings, writer(power), bar, put,
-        )
+            received(at_price, 1), settings, writer(power), bar, lift(lifted, lower),
+        )
+
+    def begin(lifted, notes, settings, *rest):
+        *terms, upper, new_notes, total_o, out, semaphores = rest
+        total = raise_upper(sum(term[...] for term in terms), lifted, notes, settings, upper, new_notes)
         for peer in range(ndev):
-            out[pl.ds(peer * ut, ut), :] = total[0]
+            out[pl.ds(peer * ut, ut), :] = total
+        copies = Copies(semaphores)
         copies.send(out, total_o)
         copies.close()
 
@@ -426,8 +424,8 @@
 
         return put
 
-    def raise_upper(came, step, lifted, notes, settings, upper, new_notes):
-        capacity, pull = capacities(part(notes, 0), settings, sum_blocks(came, 0, step))
+    def raise_upper(total, lifted, notes, settings, upper, new_notes):
+        capacity, pull = capacities(part(notes, 0), settings, total)
         new_notes[pl.ds(0, ut), :] = capacity
         new_notes[pl.ds(ut, hours), :] = notes[pl.ds(ut, hours), :]
         total = jnp.zeros((ut, LANES), f32)
@@ -440,7 +438,7 @@
     def update(came, lifted, notes, settings, sent, upper, new_notes, out_o, out, semaphores):
         spread(out, ut, rows_update, sent[pl.ds(0, hours), :])
         spread(out, ut + bt, rows_update, sent[pl.ds(hours, hours), :])
-        total = raise_upper(came, ut, lifted, notes, settings, upper, new_notes)
+        total = raise_upper(sum_blocks(came, 0, ut), lifted, notes, settings, upper, new_notes)
         for peer in range(ndev):
             out[pl.ds(peer * rows_update, ut), :] = total
         copies = Copies(semaphores)
@@ -455,7 +453,9 @@
         for step in range(2):
             early[pl.ds(step * scen, scen), :] = wide(came, ut + step * bt, bt, rows_update)
         copies.send(early, early_o)
-        total = raise_upper(came, rows_update, lifted, notes, settings, upper, new_notes)
+        total = raise_upper(
+            sum_blocks(came, 0, rows_update), lifted, notes, settings, upper, new_notes
+        )
         total_o[...] = total
 
         def put_power(hour, value):
@@ -480,17 +480,17 @@
         copies.close()
 
     def two_steps(value, injections, factors, line, at):
-        flows = dual_step * across(injections, factors[...])
+        flows = dual_step * jnp.dot(injections, factors[...], preferred_element_type=f32)
         for step in range(2):
             value = held_back(value + flows[step * scen : (step + 1) * scen], line, at)
         return value
 
     def hourly_flow(
-        shift, line, early, flow, shift_far, new_o, early_v, flow_v, shift_v, new, semaphores
+        turned, line, early, flow, turned_far, new_o, early_v, flow_v, turned_v, new, semaphores
     ):
         copies = Copies(semaphores)
         come = [copies.bring(early, early_v), copies.bring(flow, flow_v)]
-        factors = bring_lines(copies, shift, shift_far, shift_v)
+        factors = bring_lines(copies, turned, turned_far, turned_v, 1)
         for copy in come:
             copy.wait()
         injections = early_v[...].astype(bf16)
@@ -502,13 +502,12 @@
         copies.close()
 
     def finish(
-        came, total, notes, settings, line, shift, flow, shift_far,
-        power_o, upper_o, lower_o, flow_o, capacity_o,
-        shift_v, flow_v, notes_v, upper, own, out, semaphores,
+        came, line, turned, flow, turned_far, power_o, lower_o, flow_o,
+        turned_v, flow_v, out, semaphores,
     ):
         copies = Copies(semaphores)
         flow_came = copies.bring(flow, flow_v)
-        factors = bring_lines(copies, shift, shift_far, shift_v)
+        factors = bring_lines(copies, turned, turned_far, turned_v, 1)
         blocks = came.reshape(ndev, rows_back, LANES)
         copies.send(blocks.at[:, pl.ds(0, ut)], power_o)
         copies.send(blocks.at[:, pl.ds(2 * ut, ut)], lower_o)
@@ -523,7 +522,14 @@
             spread(out, row, lt, value)
             row += value.shape[1] // LANES
         copies.send(out.reshape(scen, lt, LANES), flow_o)
-        capacity, pull = capacities(part(notes, 0), settings, total[...])
+        copies.close()
+
+    def finish_upper(came, notes, settings, *rest):
+        *terms, upper_o, capacity_o, notes_v, upper, own, semaphores = rest
+        copies = Copies(semaphores)
+        capacity, pull = capacities(
+            part(notes, 0), settings, sum(term[...] for term in terms)
+        )
         for peer in range(ndev):
             upper[peer] = jnp.maximum(came[pl.ds(peer * rows_back + ut, ut), :] - pull, 0.0)
         copies.send(upper, upper_o)
@@ -537,10 +543,11 @@
         return vector.reshape(-1, LANES)
 
     line = line_limit.reshape(1, lines)
-    shift_far = shift_factors
+    shift_far, turned = shift_factors, shift_factors.T
+    turned_near = turned[:, :near_lines]
 
     state_v, incidence_v = (state, f32), ((buses, units), bf16)
-    shift_v = ((lines - near_lines, buses), bf16)
+    shift_v, turned_v = ((lines - near_lines, buses), bf16), ((buses, lines - near_lines), bf16)
     notes = (ut + hours, LANES)
     flops = 4 * hours * buses * (lines + units)
 
@@ -571,16 +578,19 @@
         14,
     )
     came = exchange(sent).reshape(-1, LANES)
-    total = add_up(total, two_stages)
-    power, upper, lower, bar, flow, load, note, total = call(
+    totals = gather_up(total, two_stages)
+    power, lifted, lower, bar, flow, load, note = call(
         first,
-        [came, total, shift, settings],
-        [shift_far],
+        [came, shift, settings],
+        [shift_far, turned],
         [state] * 4 + [(hours, lines), (hours, buses), notes],
-        [state],
-        [shift_v, incidence_v, state_v, state_v],
-        1 + FAR_PARTS,
+        [],
+        [shift_v, incidence_v, state_v],
+        FAR_PARTS,
         flops=flops,
+    )
+    upper, note, total = call(
+        begin, [lifted, note, settings, *totals], [], [state, notes], [state], [state_v], 1
     )
     came = exchange(total.reshape(ndev, ut, LANES)).reshape(-1, LANES)
     flow, power, lifted, lower, injections = call(
@@ -627,30 +637,37 @@
         flops=flops,
     )
     came = exchange(sent).reshape(-1, LANES)
-    total = add_up(total, two_stages)
+    totals = gather_up(total, two_stages)
     own_flow = ((scen * lt, LANES), f32)
     (flow,) = call(
         hourly_flow,
-        [shift, line],
-        [early, flow_dual.reshape(scen * lt, LANES), shift_far],
+        [turned_near, line],
+        [early, flow_dual.reshape(scen * lt, LANES), turned],
         [],
         [(scen, lines)],
-        [((2 * scen, buses), f32), own_flow, shift_v, ((scen, lines), f32)],
+        [((2 * scen, buses), f32), own_flow, turned_v, ((scen, lines), f32)],
         FAR_PARTS + 3,
         flops=flops,
     )
     hourly = (scen, ut, LANES)
-    power, upper, lower, flow, capacity = call(
+    power, lower, flow = call(
         finish,
-        [came, total, note, settings, line, shift],
-        [flow, shift_far],
-        [],
-        [hourly, hourly, hourly, (scen, lt, LANES), (1, LANES)],
-        [
-            shift_v, ((scen, lines), f32), ((ut, LANES), f32),
-            (hourly, f32), ((1, LANES), f32), own_flow,
-        ],
-        6 + FAR_PARTS,
+        [came, line, turned_near],
+        [flow, turned],
+        [],
+        [hourly, hourly, (scen, lt, LANES)],
+        [turned_v, ((scen, lines), f32), own_flow],
+        FAR_PARTS + 4,
+        flops=flops,
+    )
+    upper, capacity = call(
+        finish_upper,
+        [came, note, settings, *totals],
+        [],
+        [],
+        [hourly, (1, LANES)],
+        [((ut, LANES), f32), (hourly, f32), ((1, LANES), f32)],
+        2,
     )
     return (
         power.reshape(scen, 1, units),

time: 82.5 us -> 81.1 us (0.983)
  waiting for transfers between devices: 24.9 us -> 14.3 us
  local copies, waits for them, and re-layouts: 0.01 us -> 7.79 us
  starting transfers between devices: 31.5 us -> 32.9 us
    ppermute x12, waiting for transfers between devices: 17.9 us -> 0.29 us  [gather_up(): lax.ppermute(value, 'hour', [(j, j ^ other) for j in range(ndev)])]
    all_to_all x4, waiting for transfers between devices: 6.93 us -> 14 us  [exchange(): lax.all_to_all(blocks, 'hour', split_axis=0, concat_axis=0, tiled=True)]
    unnamed x2 -> x3, local copies, waits for them, and re-layouts: 0.01 us -> 6.38 us
    all_to_all x4, starting transfers between devices: 18.3 us -> 20 us  [exchange(): lax.all_to_all(blocks, 'hour', split_axis=0, concat_axis=0, tiled=True)]
    slice x0 -> x1, local copies, waits for them, and re-layouts: none -> 1.4 us  [by_scenarios(): turned_near = turned[:, :near_lines]]
    pallas_call x8 -> x10, Pallas kernels: 24.7 us -> 24.5 us  [call(): pl.pallas_call(body, out_shape=[pltpu.VMEM(*s) if isinstance(s[0], tuple)...]
  transfers between devices with their start and end apart: 16 -> 16, of which waited for: 9 -> 5; matrix products, arithmetic and copies ran while one was open for 0% -> 10% of each run, Pallas kernels for 16% -> 23%
where the time goes in v5:
time: 81.1 us; the launch traced here: 80.3 us
  starting transfers between devices  32.9 us (41%)
  Pallas kernels  24.5 us (30%)
  waiting for transfers between devices  14.3 us (18%)
  local copies, waits for them, and re-layouts  7.79 us (10%)
  between operations  0.83 us (1%)
    pallas_call x10, Pallas kernels, call(): pl.pallas_call(body, out_shape=[pltpu.VMEM(*s) if isinstance(s[0], tuple)...  24.5 us
    all_to_all x4, starting transfers between devices, exchange(): lax.all_to_all(blocks, 'hour', split_axis=0, concat_axis=0, tiled=True)  20 us
    all_to_all x4, waiting for transfers between devices, exchange(): lax.all_to_all(blocks, 'hour', split_axis=0, concat_axis=0, tiled=True)  14 us
    ppermute x12, starting transfers between devices, gather_up(): lax.ppermute(value, 'hour', [(j, j ^ other) for j in range(ndev)])  12.9 us
    unnamed x3, local copies, waits for them, and re-layouts  6.38 us
  transfers between devices with their start and end apart: 16, of which 5 were waited for; matrix products, arithmetic and copies ran while one was open for 10% of the time, Pallas kernels for 23%

profile of v5, /device:TPU:0, one launch (start us, length us, event | category | flops | bytes accessed | tf_op | source)
XLA Modules:
  0.0 80.3 jit_solution(11089003464624042315)
XLA Ops:
  0.6 2.1 %shard_map.173 = (f32[16,128]{1,0:T(8,128)S(1)}, f32[80,128]{1,0:T(8,128)S(1)}, bf16[1280,512]{1,0:T(8,128)(2,1)S(1)}, f32[16,88,128]{2,1,0:T(8,128)}) custom-call(f32[16,16,128]{2,1,0:T(8,128)} %bitcast.42, f32[16,16,128]{2,1,0:T(8,128)} %bitcast.43, f32[16,16,128]{2,1,0:T(8,128)} %bitcast.44, f32[16,32,128]{2,1,0:T(8,128)} %bitcast.39, ...), custom_call_target="tpu_custom_call" | custom-call | bytes 4907584 | tf_op jit(solution)/shard_map/pallas_call | solution.py:162
  2.8 7.4 %all-to-all-start = ((f32[16,88,128]{2,1,0:T(8,128)}), f32[16,88,128]{2,1,0:T(8,128)S(1)}, u32[]{:S(2)}, u32[]{:S(2)}) async-start(f32[16,88,128]{2,1,0:T(8,128)} %get-tuple-element.41), calls=%async_computation | async-start | bytes 1441792 | tf_op jit(solution)/shard_map/all_to_all | solution.py:205
  10.2 1.7 %collective-permute-start.2 = (f32[16,128]{1,0:T(8,128)S(1)}, f32[16,128]{1,0:T(8,128)S(1)}, u32[]{:S(2)}, u32[]{:S(2)}) collective-permute-start(f32[16,128]{1,0:T(8,128)S(1)} %get-tuple-element.46), channel_id=1, source_target_pairs={{0,3},{1,2},{2,1},{3,0},{4,7},{5,6},{6,5},{7,4},{8,11},{9,10},{10,... | collective-permute-start | bytes 24584 | tf_op jit(solution)/shard_map/ppermute | solution.py:195
  12.2 6.4 %copy.19 = bf16[4096,512]{0,1:T(8,128)(2,1)} copy(bf16[4096,512]{1,0:T(8,128)(2,1)} %shift_far.5) | data formatting | bytes 8388608 | tf_op args[7]
  18.6 1.8 %collective-permute-start.3 = (f32[16,128]{1,0:T(8,128)S(1)}, f32[16,128]{1,0:T(8,128)S(1)}, u32[]{:S(2)}, u32[]{:S(2)}) collective-permute-start(f32[16,128]{1,0:T(8,128)S(1)} %add_add_fusion.1.rest_0_), channel_id=1, source_target_pairs={{0,4},{1,5},{2,6},{3,7},{4,0},{5,1},{6,2},{7,3},{8,12},{9,13},{10,... | collective-permute-start | bytes 24584 | tf_op jit(solution)/shard_map/ppermute | solution.py:195
  20.4 2.4 %collective-permute-start.4 = (f32[16,128]{1,0:T(8,128)S(1)}, f32[16,128]{1,0:T(8,128)S(1)}, u32[]{:S(2)}, u32[]{:S(2)}) collective-permute-start(f32[16,128]{1,0:T(8,128)S(1)} %add_add_fusion.1.rest_0_), channel_id=1, source_target_pairs={{0,8},{1,9},{2,10},{3,11},{4,12},{5,13},{6,14},{7,15},{8,0},{9,1},... | collective-permute-start | bytes 24584 | tf_op jit(solution)/shard_map/ppermute | solution.py:195
  23.1 4.8 %all-to-all-done = f32[16,88,128]{2,1,0:T(8,128)S(1)} async-done(((f32[16,88,128]{2,1,0:T(8,128)}), f32[16,88,128]{2,1,0:T(8,128)S(1)}, u32[]{:S(2)}, u32[]{:S(2)}) %all-to-all-start) | async-done | bytes 720928 | tf_op jit(solution)/shard_map/all_to_all | solution.py:205
  27.9 2.6 %shard_map.174 = (f32[256,128]{1,0:T(8,128)S(1)}, f32[256,128]{1,0:T(8,128)S(1)}, f32[256,128]{1,0:T(8,128)S(1)}, f32[256,128]{1,0:T(8,128)S(1)}, f32[16,4096]{1...) custom-call(f32[1408,128]{1,0:T(8,128)S(1)} %bitcast.28, bf16[1280,512]{1,0:T(8,128)(2,1)S(1)} %get-tuple-element.42.shift, ...), custom_call_target="tpu_custom_call" | custom-call | flops 201326592 | bytes 10461184 | tf_op jit(solution)/shard_map/pallas_call | solution.py:162
  31.2 5.5 %all-to-all-start.1 = ((f32[16,16,128]{2,1,0:T(8,128)}), f32[16,16,128]{2,1,0:T(8,128)S(1)}, u32[]{:S(2)}, u32[]{:S(2)}) async-start(f32[16,16,128]{2,1,0:T(8,128)} %bitcast.45), calls=%async_computation.1 | async-start | bytes 262144 | tf_op jit(solution)/shard_map/all_to_all | solution.py:205
  36.7 3.9 %shard_map.176 = (f32[16,4096]{1,0:T(8,128)S(1)}, f32[256,128]{1,0:T(8,128)S(1)}, f32[256,128]{1,0:T(8,128)S(1)}, f32[256,128]{1,0:T(8,128)S(1)}, f32[32,512]{1,0:T(8,128)S(1)}) custom-call(bf16[1280,512]{1,0:T(8,128)(2,1)S(1)} %get-tuple-element.42.shift, f32[256,128]{1,0:T(8,128)S(1)} %get-tuple-element.48.bar, f32[16,512]{1,0:T(8,128)S(1)} %get-tuple-element.49.load, ...), custom_call_target="tpu_custom_call" | custom-call | flops 201326592 | bytes 6397952 | tf_op jit(solution)/shard_map/pallas_call | solution.py:162
  40.6 4.0 %all-to-all-done.1 = f32[16,16,128]{2,1,0:T(8,128)S(1)} async-done(((f32[16,16,128]{2,1,0:T(8,128)}), f32[16,16,128]{2,1,0:T(8,128)S(1)}, u32[]{:S(2)}, u32[]{:S(2)}) %all-to-all-start.1) | async-done | bytes 131104 | tf_op jit(solution)/shard_map/all_to_all | solution.py:205
  44.6 0.8 shard_map.177
  45.4 3.5 %all-to-all-start.2 = ((f32[16,24,128]{2,1,0:T(8,128)}), f32[16,24,128]{2,1,0:T(8,128)S(1)}, u32[]{:S(2)}, u32[]{:S(2)}) async-start(f32[16,24,128]{2,1,0:T(8,128)} %bitcast.41), calls=%async_computation.2 | async-start | bytes 393216 | tf_op jit(solution)/shard_map/all_to_all | solution.py:205
  49.0 6.1 %shard_map.178 = (f32[16,4096]{1,0:T(8,128)}, f32[256,128]{1,0:T(8,128)S(1)}, f32[256,128]{1,0:T(8,128)S(1)}, f32[256,128]{1,0:T(8,128)S(1)}, f32[256,128]{1,0:T(8,128)S(1)}, /*index=5*/f32[16,512]{1,0:T(8,128)S(1)}) custom-call(bf16[1280,512]{1,0:T(8,128)(2,1)S(1)} %get-tuple-element.42.shift, f32[32,512]{1,0:T(8,128)S(1)} %get-tuple-element.56.sent, ...), custom_call_target="tpu_custom_call" | custom-call | flops 402653184 | bytes 6332416 | tf_op jit(solution)/shard_map/pallas_call | solution.py:162
  55.0 2.9 %all-to-all-done.2 = f32[16,24,128]{2,1,0:T(8,128)S(1)} async-done(((f32[16,24,128]{2,1,0:T(8,128)}), f32[16,24,128]{2,1,0:T(8,128)S(1)}, u32[]{:S(2)}, u32[]{:S(2)}) %all-to-all-start.2) | async-done | bytes 196640 | tf_op jit(solution)/shard_map/all_to_all | solution.py:205
  57.9 1.6 %shard_map.179 = (f32[32,128]{1,0:T(8,128)S(1)}, f32[16,128]{1,0:T(8,128)S(1)}, f32[16,56,128]{2,1,0:T(8,128)}, f32[32,512]{1,0:T(8,128)}) custom-call(f32[384,128]{1,0:T(8,128)S(1)} %bitcast.29, f32[256,128]{1,0:T(8,128)S(1)} %get-tuple-element.63.lifted, f32[256,128]{1,0:T(8,128)S(1)} %get-tuple-element.64.lower, f32[256,128]{1,0:T(8,128)S(1)} %get-tuple-element.65.power, ...), custom_call_target="tpu_custom_call" | custom-call | flops 201326592 | bytes 843776 | tf_op jit(solution)/shard_map/pallas_call | solution.py:162
  59.5 3.6 %all-to-all-start.3 = ((f32[16,56,128]{2,1,0:T(8,128)}), f32[16,56,128]{2,1,0:T(8,128)S(1)}, u32[]{:S(2)}, u32[]{:S(2)}) async-start(f32[16,56,128]{2,1,0:T(8,128)} %get-tuple-element.68), calls=%async_computation.3 | async-start | bytes 917504 | tf_op jit(solution)/shard_map/all_to_all | solution.py:205
  63.1 1.4 %slice.4.turned = bf16[512,1280]{1,0:T(8,128)(2,1)S(1)} slice(bf16[512,4096]{1,0:T(8,128)(2,1)} %bitcast.36), slice={[0:512], [0:1280]} | slice | bytes 2621440 | tf_op jit(solution)/shard_map/slice | solution.py:547
  64.5 1.6 %collective-permute-start.8 = (f32[16,128]{1,0:T(8,128)S(1)}, f32[16,128]{1,0:T(8,128)S(1)}, u32[]{:S(2)}, u32[]{:S(2)}) collective-permute-start(f32[16,128]{1,0:T(8,128)S(1)} %get-tuple-element.72), channel_id=1, source_target_pairs={{0,3},{1,2},{2,1},{3,0},{4,7},{5,6},{6,5},{7,4},{8,11},{9,10},{10,... | collective-permute-start | bytes 24584 | tf_op jit(solution)/shard_map/ppermute | solution.py:195
  66.5 3.0 %shard_map.180.flow = f32[16,4096]{1,0:T(8,128)} custom-call(bf16[512,1280]{1,0:T(8,128)(2,1)S(1)} %slice.4.turned, f32[1,4096]{1,0:T(1,128)S(1)} %bitcast.33, f32[32,512]{1,0:T(8,128)} %get-tuple-element.69.early, f32[512,128]{1,0:T(8,128)} %bitcast.40, bf16[512,4096]{1,0:T(8,128)(2,1)} %bitcast.37), custom_call_target="tpu_custom_call" | custom-call | flops 201326592 | bytes 5849088 | tf_op jit(solution)/shard_map/pallas_call | solution.py:162
  69.8 1.9 %collective-permute-start.9 = (f32[16,128]{1,0:T(8,128)S(1)}, f32[16,128]{1,0:T(8,128)S(1)}, u32[]{:S(2)}, u32[]{:S(2)}) collective-permute-start(f32[16,128]{1,0:T(8,128)S(1)} %add_add_fusion.rest_0_), channel_id=1, source_target_pairs={{0,4},{1,5},{2,6},{3,7},{4,0},{5,1},{6,2},{7,3},{8,12},{9,13},{10,... | collective-permute-start | bytes 24584 | tf_op jit(solution)/shard_map/ppermute | solution.py:195
  71.7 2.2 %collective-permute-start.10 = (f32[16,128]{1,0:T(8,128)S(1)}, f32[16,128]{1,0:T(8,128)S(1)}, u32[]{:S(2)}, u32[]{:S(2)}) collective-permute-start(f32[16,128]{1,0:T(8,128)S(1)} %add_add_fusion.rest_0_), channel_id=1, source_target_pairs={{0,8},{1,9},{2,10},{3,11},{4,12},{5,13},{6,14},{7,15},{8,0},{9,1},... | collective-permute-start | bytes 24584 | tf_op jit(solution)/shard_map/ppermute | solution.py:195
  74.2 2.2 %all-to-all-done.3 = f32[16,56,128]{2,1,0:T(8,128)S(1)} async-done(((f32[16,56,128]{2,1,0:T(8,128)}), f32[16,56,128]{2,1,0:T(8,128)S(1)}, u32[]{:S(2)}, u32[]{:S(2)}) %all-to-all-start.3) | async-done | bytes 458784 | tf_op jit(solution)/shard_map/all_to_all | solution.py:205
  76.4 3.1 %shard_map.181 = (f32[16,16,128]{2,1,0:T(8,128)}, f32[16,16,128]{2,1,0:T(8,128)}, f32[16,32,128]{2,1,0:T(8,128)}) custom-call(f32[896,128]{1,0:T(8,128)S(1)} %bitcast.26, f32[1,4096]{1,0:T(1,128)S(1)} %bitcast.34, bf16[512,1280]{1,0:T(8,128)(2,1)S(1)} %slice.4.turned, f32[16,4096]{1,0:T(8,128)} %shard_map.180.flow, bf16[512,4096]{1,0:T(8,128)(2,1)} %bitcast.38), custom_call_target="tpu_custom_call" | custom-call | flops 201326592 | bytes 6242304 | tf_op jit(solution)/shard_map/pallas_call | solution.py:162
  (24 shorter events, 3.1 us)
Async XLA Ops:
  2.8 25.1 %all-to-all-start = ((f32[16,88,128]{2,1,0:T(8,128)}), f32[16,88,128]{2,1,0:T(8,128)S(1)}, u32[]{:S(2)}, u32[]{:S(2)}) async-start(f32[16,88,128]{2,1,0:T(8,128)} %get-tuple-element.41), calls=%async_computation | async-start | bytes 1441792 | tf_op jit(solution)/shard_map/all_to_all | solution.py:205
  10.2 8.4 %collective-permute-start.2 = (f32[16,128]{1,0:T(8,128)S(1)}, f32[16,128]{1,0:T(8,128)S(1)}, u32[]{:S(2)}, u32[]{:S(2)}) collective-permute-start(f32[16,128]{1,0:T(8,128)S(1)} %get-tuple-element.46), channel_id=1, source_target_pairs={{0,3},{1,2},{2,1},{3,0},{4,7},{5,6},{6,5},{7,4},{8,11},{9,10},{10,... | collective-permute-start | bytes 24584 | tf_op jit(solution)/shard_map/ppermute | solution.py:195
  11.8 6.8 %collective-permute-start.1 = (f32[16,128]{1,0:T(8,128)S(1)}, f32[16,128]{1,0:T(8,128)S(1)}, u32[]{:S(2)}, u32[]{:S(2)}) collective-permute-start(f32[16,128]{1,0:T(8,128)S(1)} %get-tuple-element.46), channel_id=1, source_target_pairs={{0,2},{1,3},{2,0},{3,1},{4,6},{5,7},{6,4},{7,5},{8,10},{9,11},{10,... | collective-permute-start | bytes 24584 | tf_op jit(solution)/shard_map/ppermute | solution.py:195
  12.2 6.4 %collective-permute-start = (f32[16,128]{1,0:T(8,128)S(1)}, f32[16,128]{1,0:T(8,128)S(1)}, u32[]{:S(2)}, u32[]{:S(2)}) collective-permute-start(f32[16,128]{1,0:T(8,128)S(1)} %get-tuple-element.46), channel_id=1, source_target_pairs={{0,1},{1,0},{2,3},{3,2},{4,5},{5,4},{6,7},{7,6},{8,9},{9,8},{10,11... | collective-permute-start | bytes 24584 | tf_op jit(solution)/shard_map/ppermute | solution.py:195
  18.6 11.9 %collective-permute-start.3 = (f32[16,128]{1,0:T(8,128)S(1)}, f32[16,128]{1,0:T(8,128)S(1)}, u32[]{:S(2)}, u32[]{:S(2)}) collective-permute-start(f32[16,128]{1,0:T(8,128)S(1)} %add_add_fusion.1.rest_0_), channel_id=1, source_target_pairs={{0,4},{1,5},{2,6},{3,7},{4,0},{5,1},{6,2},{7,3},{8,12},{9,13},{10,... | collective-permute-start | bytes 24584 | tf_op jit(solution)/shard_map/ppermute | solution.py:195
  20.4 10.1 %collective-permute-start.4 = (f32[16,128]{1,0:T(8,128)S(1)}, f32[16,128]{1,0:T(8,128)S(1)}, u32[]{:S(2)}, u32[]{:S(2)}) collective-permute-start(f32[16,128]{1,0:T(8,128)S(1)} %add_add_fusion.1.rest_0_), channel_id=1, source_target_pairs={{0,8},{1,9},{2,10},{3,11},{4,12},{5,13},{6,14},{7,15},{8,0},{9,1},... | collective-permute-start | bytes 24584 | tf_op jit(solution)/shard_map/ppermute | solution.py:195
  22.8 7.7 %collective-permute-start.5 = (f32[16,128]{1,0:T(8,128)S(1)}, f32[16,128]{1,0:T(8,128)S(1)}, u32[]{:S(2)}, u32[]{:S(2)}) collective-permute-start(f32[16,128]{1,0:T(8,128)S(1)} %add_add_fusion.1.rest_0_), channel_id=1, source_target_pairs={{0,12},{1,13},{2,14},{3,15},{4,8},{5,9},{6,10},{7,11},{8,4},{9,5},... | collective-permute-start | bytes 24584 | tf_op jit(solution)/shard_map/ppermute | solution.py:195
  27.9 8.8 %copy-start = (f32[4096]{0:T(1024)S(1)}, f32[4096]{0:T(1024)}, u32[]{:S(2)}) copy-start(f32[4096]{0:T(1024)} %param.22) | copy-start | bytes 49156
  31.2 13.4 %all-to-all-start.1 = ((f32[16,16,128]{2,1,0:T(8,128)}), f32[16,16,128]{2,1,0:T(8,128)S(1)}, u32[]{:S(2)}, u32[]{:S(2)}) async-start(f32[16,16,128]{2,1,0:T(8,128)} %bitcast.45), calls=%async_computation.1 | async-start | bytes 262144 | tf_op jit(solution)/shard_map/all_to_all | solution.py:205
  45.4 12.5 %all-to-all-start.2 = ((f32[16,24,128]{2,1,0:T(8,128)}), f32[16,24,128]{2,1,0:T(8,128)S(1)}, u32[]{:S(2)}, u32[]{:S(2)}) async-start(f32[16,24,128]{2,1,0:T(8,128)} %bitcast.41), calls=%async_computation.2 | async-start | bytes 393216 | tf_op jit(solution)/shard_map/all_to_all | solution.py:205
  59.5 17.0 %all-to-all-start.3 = ((f32[16,56,128]{2,1,0:T(8,128)}), f32[16,56,128]{2,1,0:T(8,128)S(1)}, u32[]{:S(2)}, u32[]{:S(2)}) async-start(f32[16,56,128]{2,1,0:T(8,128)} %get-tuple-element.68), calls=%async_computation.3 | async-start | bytes 917504 | tf_op jit(solution)/shard_map/all_to_all | solution.py:205
  64.5 5.0 %collective-permute-start.8 = (f32[16,128]{1,0:T(8,128)S(1)}, f32[16,128]{1,0:T(8,128)S(1)}, u32[]{:S(2)}, u32[]{:S(2)}) collective-permute-start(f32[16,128]{1,0:T(8,128)S(1)} %get-tuple-element.72), channel_id=1, source_target_pairs={{0,3},{1,2},{2,1},{3,0},{4,7},{5,6},{6,5},{7,4},{8,11},{9,10},{10,... | collective-permute-start | bytes 24584 | tf_op jit(solution)/shard_map/ppermute | solution.py:195
  66.1 3.7 %collective-permute-start.7 = (f32[16,128]{1,0:T(8,128)S(1)}, f32[16,128]{1,0:T(8,128)S(1)}, u32[]{:S(2)}, u32[]{:S(2)}) collective-permute-start(f32[16,128]{1,0:T(8,128)S(1)} %get-tuple-element.72), channel_id=1, source_target_pairs={{0,2},{1,3},{2,0},{3,1},{4,6},{5,7},{6,4},{7,5},{8,10},{9,11},{10,... | collective-permute-start | bytes 24584 | tf_op jit(solution)/shard_map/ppermute | solution.py:195
  66.5 3.3 %collective-permute-start.6 = (f32[16,128]{1,0:T(8,128)S(1)}, f32[16,128]{1,0:T(8,128)S(1)}, u32[]{:S(2)}, u32[]{:S(2)}) collective-permute-start(f32[16,128]{1,0:T(8,128)S(1)} %get-tuple-element.72), channel_id=1, source_target_pairs={{0,1},{1,0},{2,3},{3,2},{4,5},{5,4},{6,7},{7,6},{8,9},{9,8},{10,11... | collective-permute-start | bytes 24584 | tf_op jit(solution)/shard_map/ppermute | solution.py:195
  69.8 9.8 %collective-permute-start.9 = (f32[16,128]{1,0:T(8,128)S(1)}, f32[16,128]{1,0:T(8,128)S(1)}, u32[]{:S(2)}, u32[]{:S(2)}) collective-permute-start(f32[16,128]{1,0:T(8,128)S(1)} %add_add_fusion.rest_0_), channel_id=1, source_target_pairs={{0,4},{1,5},{2,6},{3,7},{4,0},{5,1},{6,2},{7,3},{8,12},{9,13},{10,... | collective-permute-start | bytes 24584 | tf_op jit(solution)/shard_map/ppermute | solution.py:195
  71.7 7.9 %collective-permute-start.10 = (f32[16,128]{1,0:T(8,128)S(1)}, f32[16,128]{1,0:T(8,128)S(1)}, u32[]{:S(2)}, u32[]{:S(2)}) collective-permute-start(f32[16,128]{1,0:T(8,128)S(1)} %add_add_fusion.rest_0_), channel_id=1, source_target_pairs={{0,8},{1,9},{2,10},{3,11},{4,12},{5,13},{6,14},{7,15},{8,0},{9,1},... | collective-permute-start | bytes 24584 | tf_op jit(solution)/shard_map/ppermute | solution.py:195
  73.9 5.7 %collective-permute-start.11 = (f32[16,128]{1,0:T(8,128)S(1)}, f32[16,128]{1,0:T(8,128)S(1)}, u32[]{:S(2)}, u32[]{:S(2)}) collective-permute-start(f32[16,128]{1,0:T(8,128)S(1)} %add_add_fusion.rest_0_), channel_id=1, source_target_pairs={{0,12},{1,13},{2,14},{3,15},{4,8},{5,9},{6,10},{7,11},{8,4},{9,5},... | collective-permute-start | bytes 24584 | tf_op jit(solution)/shard_map/ppermute | solution.py:195

commit v6 on v5

--- a/solution.py
+++ b/solution.py
@@ -12,8 +12,8 @@
 dual_step = 0.01
 LANES = 128
 SUBLANES = 8
-NEAR = 5
-FAR_PARTS = 2
+NEAR = 4
+FAR_PARTS = 3
 
 
 def compose(earlier, later):
@@ -200,6 +200,7 @@
     bits = [1 << b for b in range(ndev.bit_length() - 1)]
     half = 1 << (len(bits) // 2)
     two_stages = [range(1, half), range(half, ndev, half)]
+    three_stages = [range(1, half)] + [[bit] for bit in bits if bit >= half]
 
     def exchange(blocks):
         return lax.all_to_all(blocks, "hour", split_axis=0, concat_axis=0, tiled=True)
@@ -520,8 +521,9 @@
             wait()
             value = two_steps(flow_v[:, at], injections, part_v, line, at)
             spread(out, row, lt, value)
+            some = pl.ds(row, value.shape[1] // LANES)
+            copies.send(out.reshape(scen, lt, LANES).at[:, some], flow_o.at[:, some])
             row += value.shape[1] // LANES
-        copies.send(out.reshape(scen, lt, LANES), flow_o)
         copies.close()
 
     def finish_upper(came, notes, settings, *rest):
@@ -578,7 +580,7 @@
         14,
     )
     came = exchange(sent).reshape(-1, LANES)
-    totals = gather_up(total, two_stages)
+    totals = gather_up(total, three_stages)
     power, lifted, lower, bar, flow, load, note = call(
         first,
         [came, shift, settings],
@@ -657,7 +659,7 @@
         [],
         [hourly, hourly, (scen, lt, LANES)],
         [turned_v, ((scen, lines), f32), own_flow],
-        FAR_PARTS + 4,
+        2 * FAR_PARTS + 4,
         flops=flops,
     )
     upper, capacity = call(
@@ -686,7 +688,7 @@
         and power.shape[0] == ndev
         and power.shape[1] == 1
         and capacity.shape[0] == LANES
-        and flow_dual.shape[2] % (16 * FAR_PARTS * LANES) == 0
+        and flow_dual.shape[2] % (16 * SUBLANES * LANES // 4) == 0
         and ndev % (2 * SUBLANES) == 0
         and ndev & (ndev - 1) == 0
         and all(size % (SUBLANES * LANES) == 0 for size in (power.shape[2], flow_dual.shape[2]))

time: 81.1 us -> 80.6 us (level)
    all_to_all x4, waiting for transfers between devices: 14 us -> 8.69 us  [exchange(): lax.all_to_all(blocks, 'hour', split_axis=0, concat_axis=0, tiled=True)]
    ppermute x12 -> x11, waiting for transfers between devices: 0.29 us -> 5.26 us  [gather_up(): lax.ppermute(value, 'hour', [(j, j ^ other) for j in range(ndev)])]
    all_to_all x4, starting transfers between devices: 20 us -> 19.1 us  [exchange(): lax.all_to_all(blocks, 'hour', split_axis=0, concat_axis=0, tiled=True)]
    ppermute x12 -> x11, starting transfers between devices: 12.9 us -> 13.3 us  [gather_up(): lax.ppermute(value, 'hour', [(j, j ^ other) for j in range(ndev)])]
  transfers between devices with their start and end apart: 16 -> 15, of which waited for: 5 -> 6; matrix products, arithmetic and copies ran while one was open for 10% -> 10% of each run, Pallas kernels for 23% -> 24%
where the time goes in v6:
time: 80.6 us; the launch traced here: 79.8 us
  starting transfers between devices  32.4 us (40%)
  Pallas kernels  24.9 us (31%)
  waiting for transfers between devices  14 us (17%)
  local copies, waits for them, and re-layouts  7.72 us (10%)
  between operations  0.81 us (1%)
    pallas_call x10, Pallas kernels, call(): pl.pallas_call(body, out_shape=[pltpu.VMEM(*s) if isinstance(s[0], tuple)...  24.9 us
    all_to_all x4, starting transfers between devices, exchange(): lax.all_to_all(blocks, 'hour', split_axis=0, concat_axis=0, tiled=True)  19.1 us
    ppermute x11, starting transfers between devices, gather_up(): lax.ppermute(value, 'hour', [(j, j ^ other) for j in range(ndev)])  13.3 us
    all_to_all x4, waiting for transfers between devices, exchange(): lax.all_to_all(blocks, 'hour', split_axis=0, concat_axis=0, tiled=True)  8.69 us
    unnamed x3, local copies, waits for them, and re-layouts  6.43 us
    ppermute x11, waiting for transfers between devices, gather_up(): lax.ppermute(value, 'hour', [(j, j ^ other) for j in range(ndev)])  5.26 us
  transfers between devices with their start and end apart: 15, of which 6 were waited for; matrix products, arithmetic and copies ran while one was open for 10% of the time, Pallas kernels for 24%

profile of v6, /device:TPU:0, one launch (start us, length us, event | category | flops | bytes accessed | tf_op | source)
XLA Modules:
  0.0 79.8 jit_solution(13422609257952998374)
XLA Ops:
  0.6 2.1 %shard_map.173 = (f32[16,128]{1,0:T(8,128)S(1)}, f32[80,128]{1,0:T(8,128)S(1)}, bf16[1024,512]{1,0:T(8,128)(2,1)S(1)}, f32[16,88,128]{2,1,0:T(8,128)}) custom-call(f32[16,16,128]{2,1,0:T(8,128)} %bitcast.42, f32[16,16,128]{2,1,0:T(8,128)} %bitcast.43, f32[16,16,128]{2,1,0:T(8,128)} %bitcast.44, f32[16,32,128]{2,1,0:T(8,128)} %bitcast.39, ...), custom_call_target="tpu_custom_call" | custom-call | bytes 4907584 | tf_op jit(solution)/shard_map/pallas_call | solution.py:162
  2.7 7.4 %all-to-all-start = ((f32[16,88,128]{2,1,0:T(8,128)}), f32[16,88,128]{2,1,0:T(8,128)S(1)}, u32[]{:S(2)}, u32[]{:S(2)}) async-start(f32[16,88,128]{2,1,0:T(8,128)} %get-tuple-element.41), calls=%async_computation | async-start | bytes 1441792 | tf_op jit(solution)/shard_map/all_to_all | solution.py:206
  10.2 1.7 %collective-permute-start.2 = (f32[16,128]{1,0:T(8,128)S(1)}, f32[16,128]{1,0:T(8,128)S(1)}, u32[]{:S(2)}, u32[]{:S(2)}) collective-permute-start(f32[16,128]{1,0:T(8,128)S(1)} %get-tuple-element.46), channel_id=1, source_target_pairs={{0,3},{1,2},{2,1},{3,0},{4,7},{5,6},{6,5},{7,4},{8,11},{9,10},{10,... | collective-permute-start | bytes 24584 | tf_op jit(solution)/shard_map/ppermute | solution.py:195
  12.2 4.2 %collective-permute-done.2 = f32[16,128]{1,0:T(8,128)S(1)} collective-permute-done((f32[16,128]{1,0:T(8,128)S(1)}, f32[16,128]{1,0:T(8,128)S(1)}, u32[]{:S(2)}, u32[]{:S(2)}) %collective-permute-start.2) | collective-permute-done | bytes 8224 | tf_op jit(solution)/shard_map/ppermute | solution.py:195
  16.4 0.8 collective-permute-done.1
  17.2 6.4 %copy.19 = bf16[4096,512]{0,1:T(8,128)(2,1)} copy(bf16[4096,512]{1,0:T(8,128)(2,1)} %shift_far.5) | data formatting | bytes 8388608 | tf_op args[7]
  23.7 4.6 %collective-permute-start.4 = (f32[16,128]{1,0:T(8,128)S(1)}, f32[16,128]{1,0:T(8,128)S(1)}, u32[]{:S(2)}, u32[]{:S(2)}) collective-permute-start(f32[16,128]{1,0:T(8,128)S(1)} %add.24.rest_0_), channel_id=1, source_target_pairs={{0,8},{1,9},{2,10},{3,11},{4,12},{5,13},{6,14},{7,15},{8,0},{9,1},... | collective-permute-start | bytes 24584 | tf_op jit(solution)/shard_map/ppermute | solution.py:195
  28.3 2.6 %shard_map.174 = (f32[256,128]{1,0:T(8,128)S(1)}, f32[256,128]{1,0:T(8,128)S(1)}, f32[256,128]{1,0:T(8,128)S(1)}, f32[256,128]{1,0:T(8,128)S(1)}, f32[16,4096]{1...) custom-call(f32[1408,128]{1,0:T(8,128)S(1)} %bitcast.28, bf16[1024,512]{1,0:T(8,128)(2,1)S(1)} %get-tuple-element.42.shift, ...), custom_call_target="tpu_custom_call" | custom-call | flops 201326592 | bytes 10199040 | tf_op jit(solution)/shard_map/pallas_call | solution.py:162
  31.6 4.6 %all-to-all-start.1 = ((f32[16,16,128]{2,1,0:T(8,128)}), f32[16,16,128]{2,1,0:T(8,128)S(1)}, u32[]{:S(2)}, u32[]{:S(2)}) async-start(f32[16,16,128]{2,1,0:T(8,128)} %bitcast.45), calls=%async_computation.1 | async-start | bytes 262144 | tf_op jit(solution)/shard_map/all_to_all | solution.py:206
  36.3 3.9 %shard_map.176 = (f32[16,4096]{1,0:T(8,128)S(1)}, f32[256,128]{1,0:T(8,128)S(1)}, f32[256,128]{1,0:T(8,128)S(1)}, f32[256,128]{1,0:T(8,128)S(1)}, f32[32,512]{1,0:T(8,128)S(1)}) custom-call(bf16[1024,512]{1,0:T(8,128)(2,1)S(1)} %get-tuple-element.42.shift, f32[256,128]{1,0:T(8,128)S(1)} %get-tuple-element.48.bar, f32[16,512]{1,0:T(8,128)S(1)} %get-tuple-element.49.load, ...), custom_call_target="tpu_custom_call" | custom-call | flops 201326592 | bytes 6135808 | tf_op jit(solution)/shard_map/pallas_call | solution.py:162
  40.2 4.0 %all-to-all-done.1 = f32[16,16,128]{2,1,0:T(8,128)S(1)} async-done(((f32[16,16,128]{2,1,0:T(8,128)}), f32[16,16,128]{2,1,0:T(8,128)S(1)}, u32[]{:S(2)}, u32[]{:S(2)}) %all-to-all-start.1) | async-done | bytes 131104 | tf_op jit(solution)/shard_map/all_to_all | solution.py:206
  44.2 0.8 shard_map.177
  45.0 3.5 %all-to-all-start.2 = ((f32[16,24,128]{2,1,0:T(8,128)}), f32[16,24,128]{2,1,0:T(8,128)S(1)}, u32[]{:S(2)}, u32[]{:S(2)}) async-start(f32[16,24,128]{2,1,0:T(8,128)} %bitcast.41), calls=%async_computation.2 | async-start | bytes 393216 | tf_op jit(solution)/shard_map/all_to_all | solution.py:206
  48.5 6.5 %shard_map.178 = (f32[16,4096]{1,0:T(8,128)}, f32[256,128]{1,0:T(8,128)S(1)}, f32[256,128]{1,0:T(8,128)S(1)}, f32[256,128]{1,0:T(8,128)S(1)}, f32[256,128]{1,0:T(8,128)S(1)}, /*index=5*/f32[16,512]{1,0:T(8,128)S(1)}) custom-call(bf16[1024,512]{1,0:T(8,128)(2,1)S(1)} %get-tuple-element.42.shift, f32[32,512]{1,0:T(8,128)S(1)} %get-tuple-element.56.sent, ...), custom_call_target="tpu_custom_call" | custom-call | flops 402653184 | bytes 6070272 | tf_op jit(solution)/shard_map/pallas_call | solution.py:162
  55.0 2.5 %all-to-all-done.2 = f32[16,24,128]{2,1,0:T(8,128)S(1)} async-done(((f32[16,24,128]{2,1,0:T(8,128)}), f32[16,24,128]{2,1,0:T(8,128)S(1)}, u32[]{:S(2)}, u32[]{:S(2)}) %all-to-all-start.2) | async-done | bytes 196640 | tf_op jit(solution)/shard_map/all_to_all | solution.py:206
  57.5 1.6 %shard_map.179 = (f32[32,128]{1,0:T(8,128)S(1)}, f32[16,128]{1,0:T(8,128)S(1)}, f32[16,56,128]{2,1,0:T(8,128)}, f32[32,512]{1,0:T(8,128)}) custom-call(f32[384,128]{1,0:T(8,128)S(1)} %bitcast.29, f32[256,128]{1,0:T(8,128)S(1)} %get-tuple-element.63.lifted, f32[256,128]{1,0:T(8,128)S(1)} %get-tuple-element.64.lower, f32[256,128]{1,0:T(8,128)S(1)} %get-tuple-element.65.power, ...), custom_call_target="tpu_custom_call" | custom-call | flops 201326592 | bytes 843776 | tf_op jit(solution)/shard_map/pallas_call | solution.py:162
  59.1 3.6 %all-to-all-start.3 = ((f32[16,56,128]{2,1,0:T(8,128)}), f32[16,56,128]{2,1,0:T(8,128)S(1)}, u32[]{:S(2)}, u32[]{:S(2)}) async-start(f32[16,56,128]{2,1,0:T(8,128)} %get-tuple-element.68), calls=%async_computation.3 | async-start | bytes 917504 | tf_op jit(solution)/shard_map/all_to_all | solution.py:206
  62.6 1.3 %slice.4.turned = bf16[512,1024]{1,0:T(8,128)(2,1)S(1)} slice(bf16[512,4096]{1,0:T(8,128)(2,1)} %bitcast.36), slice={[0:512], [0:1024]} | slice | bytes 2097152 | tf_op jit(solution)/shard_map/slice | solution.py:549
  63.9 1.7 %collective-permute-start.7 = (f32[16,128]{1,0:T(8,128)S(1)}, f32[16,128]{1,0:T(8,128)S(1)}, u32[]{:S(2)}, u32[]{:S(2)}) collective-permute-start(f32[16,128]{1,0:T(8,128)S(1)} %get-tuple-element.72), channel_id=1, source_target_pairs={{0,3},{1,2},{2,1},{3,0},{4,7},{5,6},{6,5},{7,4},{8,11},{9,10},{10,... | collective-permute-start | bytes 24584 | tf_op jit(solution)/shard_map/ppermute | solution.py:195
  66.0 3.0 %shard_map.180.flow = f32[16,4096]{1,0:T(8,128)} custom-call(bf16[512,1024]{1,0:T(8,128)(2,1)S(1)} %slice.4.turned, f32[1,4096]{1,0:T(1,128)S(1)} %bitcast.33, f32[32,512]{1,0:T(8,128)} %get-tuple-element.69.early, f32[512,128]{1,0:T(8,128)} %bitcast.40, bf16[512,4096]{1,0:T(8,128)(2,1)} %bitcast.37), custom_call_target="tpu_custom_call" | custom-call | flops 201326592 | bytes 5586944 | tf_op jit(solution)/shard_map/pallas_call | solution.py:162
  69.3 1.8 %collective-permute-start.8 = (f32[16,128]{1,0:T(8,128)S(1)}, f32[16,128]{1,0:T(8,128)S(1)}, u32[]{:S(2)}, u32[]{:S(2)}) collective-permute-start(f32[16,128]{1,0:T(8,128)S(1)} %add_add_fusion.rest_0_), channel_id=1, source_target_pairs={{0,4},{1,5},{2,6},{3,7},{4,0},{5,1},{6,2},{7,3},{8,12},{9,13},{10,... | collective-permute-start | bytes 24584 | tf_op jit(solution)/shard_map/ppermute | solution.py:195
  71.1 2.2 %collective-permute-start.9 = (f32[16,128]{1,0:T(8,128)S(1)}, f32[16,128]{1,0:T(8,128)S(1)}, u32[]{:S(2)}, u32[]{:S(2)}) collective-permute-start(f32[16,128]{1,0:T(8,128)S(1)} %add_add_fusion.rest_0_), channel_id=1, source_target_pairs={{0,8},{1,9},{2,10},{3,11},{4,12},{5,13},{6,14},{7,15},{8,0},{9,1},... | collective-permute-start | bytes 24584 | tf_op jit(solution)/shard_map/ppermute | solution.py:195
  73.8 2.2 %all-to-all-done.3 = f32[16,56,128]{2,1,0:T(8,128)S(1)} async-done(((f32[16,56,128]{2,1,0:T(8,128)}), f32[16,56,128]{2,1,0:T(8,128)S(1)}, u32[]{:S(2)}, u32[]{:S(2)}) %all-to-all-start.3) | async-done | bytes 458784 | tf_op jit(solution)/shard_map/all_to_all | solution.py:206
  76.0 3.1 %shard_map.181 = (f32[16,16,128]{2,1,0:T(8,128)}, f32[16,16,128]{2,1,0:T(8,128)}, f32[16,32,128]{2,1,0:T(8,128)}) custom-call(f32[896,128]{1,0:T(8,128)S(1)} %bitcast.26, f32[1,4096]{1,0:T(1,128)S(1)} %bitcast.34, bf16[512,1024]{1,0:T(8,128)(2,1)S(1)} %slice.4.turned, f32[16,4096]{1,0:T(8,128)} %shard_map.180.flow, bf16[512,4096]{1,0:T(8,128)(2,1)} %bitcast.38), custom_call_target="tpu_custom_call" | custom-call | flops 201326592 | bytes 5980160 | tf_op jit(solution)/shard_map/pallas_call | solution.py:162
  (23 shorter events, 3.0 us)
Async XLA Ops:
  2.7 25.6 %all-to-all-start = ((f32[16,88,128]{2,1,0:T(8,128)}), f32[16,88,128]{2,1,0:T(8,128)S(1)}, u32[]{:S(2)}, u32[]{:S(2)}) async-start(f32[16,88,128]{2,1,0:T(8,128)} %get-tuple-element.41), calls=%async_computation | async-start | bytes 1441792 | tf_op jit(solution)/shard_map/all_to_all | solution.py:206
  10.2 6.2 %collective-permute-start.2 = (f32[16,128]{1,0:T(8,128)S(1)}, f32[16,128]{1,0:T(8,128)S(1)}, u32[]{:S(2)}, u32[]{:S(2)}) collective-permute-start(f32[16,128]{1,0:T(8,128)S(1)} %get-tuple-element.46), channel_id=1, source_target_pairs={{0,3},{1,2},{2,1},{3,0},{4,7},{5,6},{6,5},{7,4},{8,11},{9,10},{10,... | collective-permute-start | bytes 24584 | tf_op jit(solution)/shard_map/ppermute | solution.py:195
  11.8 5.3 %collective-permute-start.1 = (f32[16,128]{1,0:T(8,128)S(1)}, f32[16,128]{1,0:T(8,128)S(1)}, u32[]{:S(2)}, u32[]{:S(2)}) collective-permute-start(f32[16,128]{1,0:T(8,128)S(1)} %get-tuple-element.46), channel_id=1, source_target_pairs={{0,2},{1,3},{2,0},{3,1},{4,6},{5,7},{6,4},{7,5},{8,10},{9,11},{10,... | collective-permute-start | bytes 24584 | tf_op jit(solution)/shard_map/ppermute | solution.py:195
  12.2 5.0 %collective-permute-start = (f32[16,128]{1,0:T(8,128)S(1)}, f32[16,128]{1,0:T(8,128)S(1)}, u32[]{:S(2)}, u32[]{:S(2)}) collective-permute-start(f32[16,128]{1,0:T(8,128)S(1)} %get-tuple-element.46), channel_id=1, source_target_pairs={{0,1},{1,0},{2,3},{3,2},{4,5},{5,4},{6,7},{7,6},{8,9},{9,8},{10,11... | collective-permute-start | bytes 24584 | tf_op jit(solution)/shard_map/ppermute | solution.py:195
  17.2 6.5 %collective-permute-start.3 = (f32[16,128]{1,0:T(8,128)S(1)}, f32[16,128]{1,0:T(8,128)S(1)}, u32[]{:S(2)}, u32[]{:S(2)}) collective-permute-start(f32[16,128]{1,0:T(8,128)S(1)} %add_add_fusion.1), channel_id=1, source_target_pairs={{0,4},{1,5},{2,6},{3,7},{4,0},{5,1},{6,2},{7,3},{8,12},{9,13},{10,... | collective-permute-start | bytes 24584 | tf_op jit(solution)/shard_map/ppermute | solution.py:195
  23.7 7.3 %collective-permute-start.4 = (f32[16,128]{1,0:T(8,128)S(1)}, f32[16,128]{1,0:T(8,128)S(1)}, u32[]{:S(2)}, u32[]{:S(2)}) collective-permute-start(f32[16,128]{1,0:T(8,128)S(1)} %add.24.rest_0_), channel_id=1, source_target_pairs={{0,8},{1,9},{2,10},{3,11},{4,12},{5,13},{6,14},{7,15},{8,0},{9,1},... | collective-permute-start | bytes 24584 | tf_op jit(solution)/shard_map/ppermute | solution.py:195
  28.3 7.9 %copy-start = (f32[4096]{0:T(1024)S(1)}, f32[4096]{0:T(1024)}, u32[]{:S(2)}) copy-start(f32[4096]{0:T(1024)} %param.22) | copy-start | bytes 49156
  31.6 12.6 %all-to-all-start.1 = ((f32[16,16,128]{2,1,0:T(8,128)}), f32[16,16,128]{2,1,0:T(8,128)S(1)}, u32[]{:S(2)}, u32[]{:S(2)}) async-start(f32[16,16,128]{2,1,0:T(8,128)} %bitcast.45), calls=%async_computation.1 | async-start | bytes 262144 | tf_op jit(solution)/shard_map/all_to_all | solution.py:206
  45.0 12.5 %all-to-all-start.2 = ((f32[16,24,128]{2,1,0:T(8,128)}), f32[16,24,128]{2,1,0:T(8,128)S(1)}, u32[]{:S(2)}, u32[]{:S(2)}) async-start(f32[16,24,128]{2,1,0:T(8,128)} %bitcast.41), calls=%async_computation.2 | async-start | bytes 393216 | tf_op jit(solution)/shard_map/all_to_all | solution.py:206
  59.1 17.0 %all-to-all-start.3 = ((f32[16,56,128]{2,1,0:T(8,128)}), f32[16,56,128]{2,1,0:T(8,128)S(1)}, u32[]{:S(2)}, u32[]{:S(2)}) async-start(f32[16,56,128]{2,1,0:T(8,128)} %get-tuple-element.68), calls=%async_computation.3 | async-start | bytes 917504 | tf_op jit(solution)/shard_map/all_to_all | solution.py:206
  63.9 5.1 %collective-permute-start.7 = (f32[16,128]{1,0:T(8,128)S(1)}, f32[16,128]{1,0:T(8,128)S(1)}, u32[]{:S(2)}, u32[]{:S(2)}) collective-permute-start(f32[16,128]{1,0:T(8,128)S(1)} %get-tuple-element.72), channel_id=1, source_target_pairs={{0,3},{1,2},{2,1},{3,0},{4,7},{5,6},{6,5},{7,4},{8,11},{9,10},{10,... | collective-permute-start | bytes 24584 | tf_op jit(solution)/shard_map/ppermute | solution.py:195
  65.6 3.7 %collective-permute-start.6 = (f32[16,128]{1,0:T(8,128)S(1)}, f32[16,128]{1,0:T(8,128)S(1)}, u32[]{:S(2)}, u32[]{:S(2)}) collective-permute-start(f32[16,128]{1,0:T(8,128)S(1)} %get-tuple-element.72), channel_id=1, source_target_pairs={{0,2},{1,3},{2,0},{3,1},{4,6},{5,7},{6,4},{7,5},{8,10},{9,11},{10,... | collective-permute-start | bytes 24584 | tf_op jit(solution)/shard_map/ppermute | solution.py:195
  66.0 3.3 %collective-permute-start.5 = (f32[16,128]{1,0:T(8,128)S(1)}, f32[16,128]{1,0:T(8,128)S(1)}, u32[]{:S(2)}, u32[]{:S(2)}) collective-permute-start(f32[16,128]{1,0:T(8,128)S(1)} %get-tuple-element.72), channel_id=1, source_target_pairs={{0,1},{1,0},{2,3},{3,2},{4,5},{5,4},{6,7},{7,6},{8,9},{9,8},{10,11... | collective-permute-start | bytes 24584 | tf_op jit(solution)/shard_map/ppermute | solution.py:195
  69.3 9.8 %collective-permute-start.8 = (f32[16,128]{1,0:T(8,128)S(1)}, f32[16,128]{1,0:T(8,128)S(1)}, u32[]{:S(2)}, u32[]{:S(2)}) collective-permute-start(f32[16,128]{1,0:T(8,128)S(1)} %add_add_fusion.rest_0_), channel_id=1, source_target_pairs={{0,4},{1,5},{2,6},{3,7},{4,0},{5,1},{6,2},{7,3},{8,12},{9,13},{10,... | collective-permute-start | bytes 24584 | tf_op jit(solution)/shard_map/ppermute | solution.py:195
  71.1 8.0 %collective-permute-start.9 = (f32[16,128]{1,0:T(8,128)S(1)}, f32[16,128]{1,0:T(8,128)S(1)}, u32[]{:S(2)}, u32[]{:S(2)}) collective-permute-start(f32[16,128]{1,0:T(8,128)S(1)} %add_add_fusion.rest_0_), channel_id=1, source_target_pairs={{0,8},{1,9},{2,10},{3,11},{4,12},{5,13},{6,14},{7,15},{8,0},{9,1},... | collective-permute-start | bytes 24584 | tf_op jit(solution)/shard_map/ppermute | solution.py:195
  73.3 5.9 %collective-permute-start.10 = (f32[16,128]{1,0:T(8,128)S(1)}, f32[16,128]{1,0:T(8,128)S(1)}, u32[]{:S(2)}, u32[]{:S(2)}) collective-permute-start(f32[16,128]{1,0:T(8,128)S(1)} %add_add_fusion.rest_0_), channel_id=1, source_target_pairs={{0,12},{1,13},{2,14},{3,15},{4,8},{5,9},{6,10},{7,11},{8,4},{9,5},... | collective-permute-start | bytes 24584 | tf_op jit(solution)/shard_map/ppermute | solution.py:195
